TPU v7x, 512 devices: a whole 4x4x16 slice. The times are simulated.
512 devices in a mesh: occ: 16 (over z), aux: 8 (over x, core), pair: 4 (over y).
Axes of the slice: x: 4, y: 4, z: 16, core: 2. Of those that a mesh axis runs over, the one named last changes fastest.
Arguments:
- amp_fit: bfloat16 [256, 288, 288], P('aux', None, 'occ'), may hold values from -6 to 6
- amp_cabs: bfloat16 [96, 288, 288], P('aux', None, 'occ'), may hold values from -6 to 6
- coef: bfloat16 [288, 3072], P('occ'), may hold values from -0.375 to 0.375
- f12_weight: float32 [288], P('occ'), may hold values from 0.3 to 3
- ints_fit: bfloat16 [256, 288, 3072], P('aux', 'occ'), may hold values from -0.01953125 to 0.01953125
- ints_cabs: bfloat16 [96, 288, 3072], P('aux', 'occ'), may hold values from -0.01953125 to 0.01953125
- shell_len: int32 [24], replicated, may hold values from 1 to 128, 2400 in all
- pair_blocks: int32 [160, 2], P('pair'), may hold values from 0 to 23
- pair_count: int32 [4], P('pair'), may hold values from 1 to 40, as said below
Outputs:
- pair_density: float32 [160, 128, 128], P('pair', 'occ')
Inputs may be any that keep to these rules, and one draw needn't show every extreme that they name: `pair_count`: some owner has exactly 40 live slots in every draw.
All inputs are finite; a program needn't handle non-finite values.
Results may differ from a plain program's by a relative error of at most 0.0029.
Values may be sent and summed in bfloat16 or wider, within the bound.
No kernel may reach another device: no remote copies, remote signals or barrier semaphores. Data moves between devices by JAX's collectives and lax.ppermute only.
A program may use at most 64 MiB of HBM per device.

v0:
```python
import jax
import jax.numpy as jnp
from jax import lax
from jax.sharding import PartitionSpec as P


def on_device(
    amp_fit, amp_cabs, coef, f12_weight, ints_fit, ints_cabs, shell_len, pair_blocks, pair_count
):
    nblocks = shell_len.shape[0]
    padded = coef.shape[1]
    blocksz = padded // nblocks
    valid_blk = (jnp.arange(blocksz, dtype=jnp.int32)[None, :] < shell_len[:, None]).astype(
        jnp.float32
    )
    valid = valid_blk.reshape(padded)
    coef_m = jnp.where(valid[None, :] > 0, coef, jnp.zeros_like(coef))
    fit_amps, cabs_amps = (
        lax.all_to_all(amp_fit, "occ", split_axis=1, concat_axis=2, tiled=True),
        lax.all_to_all(amp_cabs, "occ", split_axis=1, concat_axis=2, tiled=True),
    )
    fit_count, occ_local, occ_total = fit_amps.shape
    cabs_count = cabs_amps.shape[0]
    fit_rows = fit_amps.reshape(fit_count * occ_local, occ_total)
    cabs_rows = cabs_amps.reshape(cabs_count * occ_local, occ_total)
    panel_rows = lax.all_gather(coef_m, "occ", axis=0, tiled=True)
    fit_half = jnp.dot(fit_rows, panel_rows, preferred_element_type=jnp.float32)
    cabs_half = jnp.dot(cabs_rows, panel_rows, preferred_element_type=jnp.float32)
    half_fit = fit_half.astype(jnp.bfloat16).reshape(fit_count * occ_local, nblocks, blocksz)
    cabs_scaled = cabs_half.reshape(cabs_count, occ_local, padded) * f12_weight[None, :, None]
    half_cabs = cabs_scaled.astype(jnp.bfloat16).reshape(cabs_count * occ_local, nblocks, blocksz)
    right_fit = ints_fit.reshape(fit_count * occ_local, nblocks, blocksz)
    right_cabs = ints_cabs.reshape(cabs_count * occ_local, nblocks, blocksz)
    row_blk = pair_blocks[:, 0]
    col_blk = pair_blocks[:, 1]
    blocks = jnp.einsum(
        "ksr,ksc->src",
        jnp.take(half_fit, row_blk, axis=1),
        jnp.take(right_fit, col_blk, axis=1),
        preferred_element_type=jnp.float32,
    )
    blocks = blocks + jnp.einsum(
        "ksr,ksc->src",
        jnp.take(half_cabs, row_blk, axis=1),
        jnp.take(right_cabs, col_blk, axis=1),
        preferred_element_type=jnp.float32,
    )
    slot_total = pair_blocks.shape[0]
    live = (jnp.arange(slot_total, dtype=jnp.int32) < pair_count[0]).astype(jnp.float32)
    row_mask = jnp.take(valid_blk, row_blk, axis=0)
    col_mask = jnp.take(valid_blk, col_blk, axis=0)
    partial_value = blocks * row_mask[:, :, None] * col_mask[:, None, :] * live[:, None, None]
    summed = lax.psum(partial_value, "aux")
    result = lax.psum_scatter(summed, "occ", scatter_dimension=1, tiled=True)
    return result


def solution(mesh):
    placed = (
        P("aux", None, "occ"),
        P("aux", None, "occ"),
        P("occ", None),
        P("occ"),
        P("aux", "occ", None),
        P("aux", "occ", None),
        P(),
        P("pair", None),
        P("pair"),
    )
    return jax.shard_map(
        on_device, mesh=mesh, in_specs=placed, out_specs=P("pair", "occ", None), check_vma=False
    )
```

profile of v0, /device:TPU:1, one launch (start us, length us, event | category | flops | bytes accessed | tf_op | source)
XLA Modules:
  0.0 279.5 jit_solution(7401577793302705467)
XLA Ops:
  6.5 0.7 fusion.22
  7.3 1.6 select_bitcast_fusion
  8.9 0.0 all-gather.3.cloned.1.call-update
  8.9 2.1 copy.29
  11.0 1.7 reshape.140
  12.7 15.9 %all-to-all-start.1 = ((bf16[16,2,1944]{2,1,0:T(2,128)(2,1)}), bf16[16,2,1944]{2,1,0:T(2,128)(2,1)}, u32[]{:S(2)}, u32[]{:S(2)}) async-start(bf16[16,2,1944]{2,1,0:T(2,128)(2,1)} %reshape.140), calls=%async_computation.1 | async-start | bytes 262144 | tf_op jit(solution)/shard_map/all_to_all | solution.py:20
  28.6 3.4 %copy.23 = bf16[32,288,18]{0,2,1:T(8,128)(2,1)S(1)} copy(bf16[32,288,18]{1,0,2:T(8,128)(2,1)} %param.15) | data formatting | bytes 663552 | tf_op args[0]
  32.0 1.9 reshape.142
  34.0 6.7 %all-to-all-done.1 = bf16[16,2,1944]{2,1,0:T(2,128)(2,1)} async-done(((bf16[16,2,1944]{2,1,0:T(2,128)(2,1)}), bf16[16,2,1944]{2,1,0:T(2,128)(2,1)}, u32[]{:S(2)}, u32[]{:S(2)}) %all-to-all-start.1) | async-done | bytes 124448 | tf_op jit(solution)/shard_map/all_to_all | solution.py:20
  40.7 6.3 %all-to-all-start = ((bf16[16,2,5184]{2,1,0:T(2,128)(2,1)}), bf16[16,2,5184]{2,1,0:T(2,128)(2,1)}, u32[]{:S(2)}, u32[]{:S(2)}) async-start(bf16[16,2,5184]{2,1,0:T(2,128)(2,1)} %reshape.142), calls=%async_computation | async-start | bytes 671744 | tf_op jit(solution)/shard_map/all_to_all | solution.py:19
  47.0 0.0 copy-start.8
  47.0 0.0 reduce-scatter.2.cloned.1.call-start
  47.1 1.0 reshape.71
  48.1 1.2 copy.32
  49.3 0.7 mul.38
  50.0 6.2 %copy.27 = bf16[32,18,3072]{2,1,0:T(8,128)(2,1)} copy(bf16[32,18,3072]{2,0,1:T(8,128)(2,1)} %param.19) | data formatting | bytes 7077888 | tf_op args[4]
  56.2 7.0 %reshape.68 = bf16[576,24,128]{2,1,0:T(8,128)(2,1)} reshape(bf16[32,18,3072]{2,1,0:T(8,128)(2,1)} %copy.27) | data formatting | bytes 7077888 | tf_op jit(solution)/shard_map/reshape | solution.py:32
  63.2 2.8 copy.28
  66.0 0.6 compare_and_fusion.1
  66.6 3.7 %gather_fusion.3 = bf16[40,216,128]{2,1,0:T(8,128)(2,1)} fusion(bf16[216,24,128]{2,0,1:T(8,128)(2,1)} %copy.32, s32[1024]{0:T(1024)S(1)} %pad_clamp_fusion), kind=kCustom, calls=%fused_computation.4.clone | custom fusion | bytes 4423840 | tf_op jit(solution)/shard_map/jit(_take)/gather | solution.py:45
  70.3 5.0 %gather_fusion.1 = bf16[40,576,128]{2,1,0:T(8,128)(2,1)} fusion(bf16[576,24,128]{2,0,1:T(8,128)(2,1)S(1)} %copy.28, s32[1024]{0:T(1024)S(1)} %pad_clamp_fusion), kind=kCustom, calls=%fused_computation.3.clone | custom fusion | bytes 11796640 | tf_op jit(solution)/shard_map/jit(_take)/gather | solution.py:39
  76.0 0.6 gather_fusion.5
  76.6 0.7 pad_clamp_fusion.1
  77.2 0.6 gather_fusion.4
  77.8 1.4 broadcast_select_fusion
  79.2 2.3 reshape.141
  81.5 0.3 copy.41
  81.9 0.9 reshape.69
  82.8 3.3 %reshape.143 = bf16[288,18,32]{2,1,0:T(8,128)(2,1)} reshape(bf16[16,2,5184]{2,1,0:T(2,128)(2,1)} %all-to-all-done) | data formatting | bytes 663552
  86.1 4.4 %copy.25 = bf16[32,18,16,18]{1,0,3,2:T(8,128)(2,1)S(1)} copy(bf16[32,18,16,18]{0,3,1,2:T(8,128)(2,1)} %bitcast.64) | data formatting | bytes 663552 | tf_op jit(solution)/shard_map/all_to_all | solution.py:19
  90.5 4.3 %reshape.66 = bf16[576,288]{0,1:T(8,128)(2,1)S(1)} reshape(bf16[32,18,16,18]{1,0,3,2:T(8,128)(2,1)S(1)} %copy.25) | data formatting | bytes 663552 | tf_op jit(solution)/shard_map/reshape | solution.py:24
  94.8 0.0 all-gather.3.cloned.1.call-done
  94.8 2.1 reshape.127
  97.0 0.9 convolution_bitcast_fusion
  97.8 0.3 fusion.8
  98.1 2.3 gather_fusion.2
  100.5 2.0 fusion.16
  102.5 1.0 copy.40
  103.5 5.0 %gather_fusion = bf16[40,576,128]{2,1,0:T(8,128)(2,1)} fusion(bf16[576,24,128]{2,0,1:T(8,128)(2,1)S(1)} %bitcast.63, s32[1024]{0:T(1024)S(1)} %pad_clamp_fusion.1), kind=kCustom, calls=%fused_computation.clone | custom fusion | bytes 11796640 | tf_op jit(solution)/shard_map/jit(_take)/gather | solution.py:38
  108.6 3.6 %fusion.9 = f32[40,128,128]{2,1,0:T(8,128)S(1)} fusion(bf16[40,216,128]{2,1,0:T(8,128)(2,1)} %gather_fusion.3, bf16[40,216,128]{2,1,0:T(8,128)(2,1)} %gather_fusion.2, pred[40]{0:T(512)(128)(4,1)S(1)} %copy-done.6, pred[40]{0:T(512)(128)(4,1)S(1)} %copy-done.5), kind=kOutput, calls=%fused_computation.19 | convolution fusion | flops 285327360 | bytes 7045200 | tf_op jit(solution)/shard_map/ksr,ksc->src/dot_general | solution.py:42
  112.2 0.4 copy-done
  112.5 6.2 %multiply_multiply_fusion = f32[40,128,128]{2,1,0:T(8,128)} fusion(f32[40,128,128]{2,1,0:T(8,128)S(1)} %fusion.9, bf16[40,576,128]{2,1,0:T(8,128)(2,1)} %gather_fusion.1, pred[40]{0:T(512)(128)(4,1)S(1)} %copy-done.6, bf16[40,576,128]{2,1,0:T(8,128)(2,1)S(1)} %copy-done, pred[40]{0:T(512)(128)(4,1)S(1)} %copy-done.5, f32[40]{0:T(128)S(1)} %compare_convert_fusion, ...), kind=kOutput, calls=%fused_computation.18 | convolution fusion | flops 763494400 | bytes 17080560 | tf_op jit(solution)/shard_map/ksr,ksc->src/dot_general | solution.py:36
  118.8 0.0 reduce-scatter.2.cloned.1.call-update
  118.8 0.0 all-reduce.2.cloned.1.call-start
  118.9 69.1 %reduce-scatter.2.cloned.1.call-done = f32[40,8,128]{2,1,0:T(8,128)} async-done(((f32[40,128,128]{2,1,0:T(8,128)}), f32[40,8,128]{2,1,0:T(8,128)}) %reduce-scatter.2.cloned.1.call-update) | async-done | bytes 163856 | tf_op jit(solution)/shard_map/reduce_scatter | solution.py:54
  187.9 0.0 all-reduce.2.cloned.1.call-update
  187.9 83.5 %all-reduce.2.cloned.1.call-done = f32[40,8,128]{2,1,0:T(8,128)} async-done(((f32[40,8,128]{2,1,0:T(8,128)}), f32[40,8,128]{2,1,0:T(8,128)}) %all-reduce.2.cloned.1.call-update) | async-done | bytes 163856 | tf_op jit(solution)/shard_map/psum | solution.py:53
  271.4 1.6 copy.44
  (21 shorter events, 0.0 us)
Async XLA Ops:
  6.5 88.3 %all-gather.3.cloned.1.call-start = ((), (), s32[]{:S(2)}) async-start(), calls=%async_computation.5 | async-start | bytes 2506752 | tf_op jit(solution)/shard_map/all_gather | solution.py:26
  12.7 34.4 %copy-start.1 = (bf16[12,18,3072]{2,1,0:T(8,128)(2,1)S(1)}, bf16[12,18,3072]{2,1,0:T(8,128)(2,1)}, u32[]{:S(2)}) copy-start(bf16[12,18,3072]{2,1,0:T(8,128)(2,1)} %param.20) | copy-start | bytes 3981316
  12.7 28.0 %all-to-all-start.1 = ((bf16[16,2,1944]{2,1,0:T(2,128)(2,1)}), bf16[16,2,1944]{2,1,0:T(2,128)(2,1)}, u32[]{:S(2)}, u32[]{:S(2)}) async-start(bf16[16,2,1944]{2,1,0:T(2,128)(2,1)} %reshape.140), calls=%async_computation.1 | async-start | bytes 262144 | tf_op jit(solution)/shard_map/all_to_all | solution.py:20
  40.7 42.1 %all-to-all-start = ((bf16[16,2,5184]{2,1,0:T(2,128)(2,1)}), bf16[16,2,5184]{2,1,0:T(2,128)(2,1)}, u32[]{:S(2)}, u32[]{:S(2)}) async-start(bf16[16,2,5184]{2,1,0:T(2,128)(2,1)} %reshape.142), calls=%async_computation | async-start | bytes 671744 | tf_op jit(solution)/shard_map/all_to_all | solution.py:19
  47.0 2.3 copy-start.8
  47.0 140.9 %reduce-scatter.2.cloned.1.call-start = ((), (), s32[]{:S(2)}) async-start(), calls=%async_computation.3 | async-start | bytes 2785280 | tf_op jit(solution)/shard_map/reduce_scatter | solution.py:54
  63.2 2.8 %copy-start.7 = (s32[40,2]{0,1:T(2,128)S(1)}, s32[40,2]{0,1:T(2,128)}, u32[]{:S(2)}) copy-start(s32[40,2]{0,1:T(2,128)} %param.22) | copy-start | bytes 964
  97.0 0.9 copy-start.4
  103.5 5.0 %copy-start.5 = (pred[40]{0:T(512)(128)(4,1)S(1)}, pred[40]{0:T(512)(128)(4,1)}, u32[]{:S(2)}) copy-start(pred[40]{0:T(512)(128)(4,1)} %get-tuple-element.6) | copy-start | bytes 124
  103.5 5.0 %copy-start.6 = (pred[40]{0:T(512)(128)(4,1)S(1)}, pred[40]{0:T(512)(128)(4,1)}, u32[]{:S(2)}) copy-start(pred[40]{0:T(512)(128)(4,1)} %get-tuple-element.12) | copy-start | bytes 124
  108.5 4.0 %copy-start = (bf16[40,576,128]{2,1,0:T(8,128)(2,1)S(1)}, bf16[40,576,128]{2,1,0:T(8,128)(2,1)}, u32[]{:S(2)}) copy-start(bf16[40,576,128]{2,1,0:T(8,128)(2,1)} %gather_fusion) | copy-start | bytes 17694724
  108.5 4.0 %copy-start.2 = (f32[40,128]{1,0:T(8,128)S(1)}, f32[40,128]{1,0:T(8,128)}, u32[]{:S(2)}) copy-start(f32[40,128]{1,0:T(8,128)} %get-tuple-element.16) | copy-start | bytes 61444
  108.6 4.0 %copy-start.3 = (f32[40,128]{1,0:T(8,128)S(1)}, f32[40,128]{1,0:T(8,128)}, u32[]{:S(2)}) copy-start(f32[40,128]{1,0:T(8,128)} %get-tuple-element.17) | copy-start | bytes 61444
  118.8 152.6 %all-reduce.2.cloned.1.call-start = ((), (), s32[]{:S(2)}) async-start(), calls=%async_computation.4 | async-start | bytes 327680 | tf_op jit(solution)/shard_map/psum | solution.py:53
Sparse Core Ops, SparseCore 0:
  9.4 85.2 all-gather.2
  118.9 68.9 reduce-scatter.1
  190.2 81.0 all-reduce.1
where the time goes:
time: 280 us
  waiting for transfers between devices  159 us (57%)
  local copies, waits for them, and re-layouts  65.9 us (24%)
  starting transfers between devices  22.3 us (8%)
  between operations  14 us (5%)
  matrix products  12.7 us (5%)
  other arithmetic  5.24 us (2%)
    psum x1, waiting for transfers between devices, on_device(): summed = lax.psum(partial_value, 'aux')  83.5 us
    reduce_scatter x1, waiting for transfers between devices, on_device(): result = lax.psum_scatter(summed, 'occ', scatter_dimension=1, tiled=True)  69.1 us
    unnamed x27, local copies, waits for them, and re-layouts  25.1 us
    all_to_all x1, starting transfers between devices, on_device(): lax.all_to_all(amp_cabs, 'occ', split_axis=1, concat_axis=2, tiled=True)  15.9 us
    reshape x2, local copies, waits for them, and re-layouts, on_device(): right_fit = ints_fit.reshape(fit_count * occ_local, nblocks, blocksz)  9.81 us
    all_to_all x1, waiting for transfers between devices, on_device(): lax.all_to_all(amp_cabs, 'occ', split_axis=1, concat_axis=2, tiled=True)  6.71 us
    all_to_all x1, starting transfers between devices, on_device(): lax.all_to_all(amp_fit, 'occ', split_axis=1, concat_axis=2, tiled=True)  6.32 us
    dot_general x1, matrix products, on_device(): jnp.einsum('ksr,ksc->src', jnp.take(half_fit, row_blk, axis=1), jnp.take(...  6.23 us
  transfers between devices with their start and end apart: 5, of which 3 were waited for; matrix products, arithmetic and copies ran while one was open for 20% of the time, Pallas kernels for 0%

commit v1 on v0

v1 whole, which is shorter than its diff:
```python
import functools
import math

import jax
import jax.numpy as jnp
from jax import lax
from jax.experimental import pallas as pl
from jax.experimental.pallas import tpu as pltpu
from jax.sharding import PartitionSpec as P

F32, BF16, F16 = jnp.float32, jnp.bfloat16, jnp.float16
LANES = 128
LN2 = math.log(2.0)
NT = (((1,), (1,)), ((), ()))
TN = (((0,), (0,)), ((), ()))


def iota(shape, dim):
    return lax.broadcasted_iota(jnp.int32, shape, dim)


def dot(a, b, dims=(((1,), (0,)), ((), ()))):
    return lax.dot_general(a, b, dims, preferred_element_type=F32)


def one_hot(cond):
    return jnp.where(cond, 1.0, 0.0).astype(BF16)


def swap_pieces(xs, piece):
    lane = iota(xs[0].shape, 1)
    bit = 1
    while bit < len(xs):
        keep = ((lane // piece) & bit) == 0
        ys = list(xs)
        for k in range(len(xs)):
            if k & bit == 0:
                lo, hi = xs[k], xs[k + bit]
                ys[k] = jnp.where(keep, lo, pltpu.roll(hi, piece * bit, 1))
                ys[k + bit] = jnp.where(keep, pltpu.roll(lo, LANES - piece * bit, 1), hi)
        xs = ys
        bit *= 2
    return xs


def vmem(n):
    return [pl.BlockSpec(memory_space=pltpu.VMEM)] * n


SMEM = pl.BlockSpec(memory_space=pltpu.SMEM)
PARAMS = pltpu.CompilerParams(vmem_limit_bytes=40 * 1024 * 1024)


NO, NI, NA, NP, NF, NC, NJ = 16, 18, 8, 4, 32, 12, 5
ROWS = 40
CQ = 16
TJ = NO * NJ


def pack_amps(info, fit, cabs, coef, out, cab32, x, msg):
    first_j = info[3]
    x[0 : NJ * NF, :] = fit[pl.ds(first_j, NJ)].reshape(NJ * NF, NO * NI)
    for q in range(NC):
        cab32[24 * q : 24 * q + NI, :] = cabs[q].astype(F32)
    zero = jnp.zeros((CQ - NC, NO * NI), F32)
    for jj in range(NJ):
        picked = [cab32[pl.ds(24 * q + first_j + jj, 1), :] for q in range(NC)]
        rows = jnp.concatenate(picked + [zero], axis=0)
        x[NJ * NF + CQ * jj : NJ * NF + CQ * (jj + 1), :] = rows.astype(BF16)
    x[NJ * (NF + CQ) :, :] = jnp.zeros((256 - NJ * (NF + CQ), NO * NI), BF16)
    shape = (NO, ROWS, NO * NI)
    t = iota(shape, 1)
    place = jnp.where((iota(shape, 2) == NI * iota(shape, 0) + t) & (t < NI), 1.0, 0.0)
    place = place.reshape(NO * ROWS, NO * NI).astype(BF16)
    msg[...] = dot(place, x[...], NT).reshape(NO, ROWS, 256)
    tiles = [coef[:, LANES * a : LANES * (a + 1)].astype(F32) for a in range(24)]
    none = jnp.zeros_like(tiles[0])
    left = swap_pieces(tiles[:16], 8)
    right = swap_pieces(tiles[16:] + [none] * 8, 8)
    for o in range(NO):
        msg[o, NI : 2 * NI, 0:LANES] = left[o]
        msg[o, NI : 2 * NI, LANES : 2 * LANES] = right[o]
    out[...] = msg[...].astype(BF16)


def partial_t(got, weight, fit, cabs, out, a_fit, a_cab, padded):
    @pl.when(pl.program_id(0) == 0)
    def _():
        shape = (NI, NO, NO * ROWS)
        pick = jnp.where(iota(shape, 2) == ROWS * iota(shape, 1) + iota(shape, 0), 1.0, 0.0)
        pick = pick.reshape(NI * NO, NO * ROWS).astype(BF16)
        amps = dot(pick, got[...].reshape(NO * ROWS, 256))
        amps = [[amps[NO * t : NO * (t + 1), LANES * h : LANES * (h + 1)] for h in (0, 1)] for t in range(NI)]
        lane = iota((NO, LANES), 1)

        def lay(ref_rows, width, start, store):
            per = LANES // width
            for jj in range(NJ):
                half, off = divmod(start + width * jj, LANES)
                for m in range(-(-NI // per)):
                    tile = jnp.zeros((NO, LANES), F32)
                    for k in range(min(per, NI - m * per)):
                        moved = amps[m * per + k][half]
                        if (width * k - off) % LANES:
                            moved = pltpu.roll(moved, (width * k - off) % LANES, 1)
                        tile = jnp.where((lane >= width * k) & (lane < width * (k + 1)), moved, tile)
                    store[NO * jj : NO * (jj + 1), LANES * m : LANES * (m + 1)] = tile.astype(BF16)

        lay(NO, NF, 0, a_fit)
        lay(NO, CQ, NJ * NF, a_cab)
        shape = (3 * LANES, 32 * NC)
        source = iota(shape, 0)
        target = iota(shape, 1)
        order = one_hot(((target >> 5) == (source & 15)) & ((target & 31) == (source >> 4)))
        weighted = dot(a_cab[...], order) * weight[...]
        a_cab[...] = weighted.astype(BF16)
        padded[...] = jnp.zeros(padded.shape, BF16)

    for q in range(NC):
        padded[32 * q : 32 * q + NI, :] = cabs[q]
    total = dot(a_fit[:, : NI * NF], fit[...].reshape(NI * NF, 1024)) + dot(a_cab[...], padded[...])
    pieces = swap_pieces([total[:, LANES * k : LANES * (k + 1)] for k in range(8)], 16)
    for k in range(8):
        out[k] = pieces[k].astype(BF16)


def sum_aux(got, out, total):
    total[...] = jnp.sum(got[...].astype(F32), axis=0)
    for o in range(NO):
        out[o, 0:15, :] = total[15 * o : 15 * o + 15, :]
        out[o, 15:16, :] = jnp.zeros((1, LANES), F32)


def sum_occ(got, out):
    total = jnp.sum(got[...], axis=0)
    top = jnp.max(jnp.max(jnp.abs(total), axis=1, keepdims=True), axis=0, keepdims=True)
    power = jnp.ceil(jnp.log(jnp.maximum(top, 1e-30)) * (1.0 / LN2))
    scaled = total * (jnp.exp(power * -LN2) * 16384.0)
    out[...] = jnp.where(iota(total.shape, 0) == 15, power, scaled)


def pair_blocks_kernel(info, got, amps, out, tsum, tmat, dmat):
    occ, aux, count = info[0], info[1], info[4]
    values = got[...]
    values = values * (jnp.exp(values[:, 15:16, :] * LN2) * (1.0 / 16384.0))
    for y in range(NP):
        for o in range(NO):
            tsum[y, 15 * o : 15 * o + 15, :] = values[NO * y + o, 0:15, :]
    for y in range(NP):
        for g in range(3):
            tmat[TJ * y : TJ * (y + 1), LANES * g : LANES * (g + 1)] = tsum[y, TJ * g : TJ * (g + 1), :]
    shape = (NP, NJ, NO, NO * ROWS)
    y, jj = iota(shape, 0), iota(shape, 1)
    first_j = jnp.minimum(NJ * y, NI - NJ)
    row = ROWS * iota(shape, 2) + NI + first_j + jj
    pick = (iota(shape, 3) == row) & (first_j + jj >= NJ * y)
    pick = jnp.where(pick, 1.0, 0.0).reshape(NP * TJ, NO * ROWS).astype(BF16)
    coef = dot(pick, amps[...].reshape(NO * ROWS, 256)).astype(BF16)
    high = tmat[...].astype(BF16)
    low = (tmat[...] - high.astype(F32)).astype(BF16)
    blocks = dot(coef, high, TN) + dot(coef, low, TN)
    for g in range(3):
        dmat[g] = blocks[:, LANES * g : LANES * (g + 1)]
    lane, row = iota((8, LANES), 1), iota((8, LANES), 0)
    for q in range(5):
        tile = jnp.zeros((8, LANES), F32)
        for k in range(8):
            slot = 8 * q + k
            a, b = info[32 + 2 * slot], info[33 + 2 * slot]
            block = dmat[b >> 3, pl.ds(pl.multiple_of(8 * a, 8), 8), :]
            block = pltpu.roll(block, (16 * (k + 8 - (b & 7))) & 127, 1)
            rows_kept = jnp.where(slot < count, info[8 + a] - 8 * occ, 0)
            lanes_kept = jnp.clip(info[8 + b] - 16 * aux, 0, 16) + 16 * k
            tile = jnp.where((lane >= 16 * k) & (lane < lanes_kept) & (row < rows_kept), block, tile)
        for p in range(NA):
            out[p, 8 * q : 8 * (q + 1), :] = tile


def unpack(got, out):
    for q in range(5):
        blocks = swap_pieces([got[p, 8 * q : 8 * (q + 1), :] for p in range(NA)], 16)
        for k in range(8):
            out[8 * q + k] = blocks[k]


def exchange(x, axes):
    return lax.all_to_all(x, axes, split_axis=0, concat_axis=0, tiled=True)


def shape_of(shape, dtype):
    return jax.ShapeDtypeStruct(shape, dtype)


def on_device(amp_fit, amp_cabs, coef, f12_weight, ints_fit, ints_cabs, shell_len, pair_blocks, pair_count):
    occ, aux, pair = (lax.axis_index(a).astype(jnp.int32) for a in ("occ", "aux", "pair"))
    first_j = jnp.minimum(NJ * pair, NI - NJ)
    info = jnp.concatenate(
        [
            jnp.stack([occ, aux, pair, first_j, pair_count[0], occ, occ, occ]),
            shell_len,
            pair_blocks.reshape(-1),
        ]
    )
    weight = jnp.tile(jnp.pad(f12_weight, (0, 32 - NI)), NC)[None, :]

    sent = pl.pallas_call(
        pack_amps,
        out_shape=shape_of((NO, ROWS, 256), BF16),
        in_specs=[SMEM] + vmem(3),
        out_specs=vmem(1)[0],
        scratch_shapes=[
            pltpu.VMEM((24 * NC, NO * NI), F32),
            pltpu.VMEM((256, NO * NI), BF16),
            pltpu.VMEM((NO, ROWS, 256), F32),
        ],
        compiler_params=PARAMS,
    )(info, jnp.transpose(amp_fit, (2, 0, 1)), jnp.transpose(amp_cabs, (0, 2, 1)), coef)
    amps = exchange(sent, "occ")

    sent = pl.pallas_call(
        partial_t,
        grid=(3,),
        out_shape=shape_of((NA, 3 * TJ, LANES), BF16),
        in_specs=[
            pl.BlockSpec((NO, ROWS, 256), lambda g: (0, 0, 0)),
            pl.BlockSpec((1, 32 * NC), lambda g: (0, 0)),
            pl.BlockSpec((NI, NF, 1024), lambda g: (0, 0, g)),
            pl.BlockSpec((NC, NI, 1024), lambda g: (0, 0, g)),
        ],
        out_specs=pl.BlockSpec((NA, TJ, LANES), lambda g: (0, g, 0)),
        scratch_shapes=[
            pltpu.VMEM((TJ, 5 * LANES), BF16),
            pltpu.VMEM((TJ, 3 * LANES), BF16),
            pltpu.VMEM((32 * NC, 1024), BF16),
        ],
        compiler_params=PARAMS,
    )(amps, weight, jnp.transpose(ints_fit, (1, 0, 2)), ints_cabs)
    got = exchange(sent, "aux")

    sent = pl.pallas_call(
        sum_aux,
        out_shape=shape_of((NO, 16, LANES), F32),
        in_specs=vmem(1),
        out_specs=vmem(1)[0],
        scratch_shapes=[pltpu.VMEM((3 * TJ, LANES), F32)],
        compiler_params=PARAMS,
    )(got)
    got = exchange(sent, "occ")

    sent = pl.pallas_call(
        sum_occ,
        out_shape=shape_of((16, LANES), F32),
        in_specs=vmem(1),
        out_specs=vmem(1)[0],
        compiler_params=PARAMS,
    )(got)
    sent = jnp.broadcast_to(sent.astype(F16)[None], (NP * NO, 16, LANES))
    got = exchange(sent, ("pair", "occ")).astype(F32)

    sent = pl.pallas_call(
        pair_blocks_kernel,
        out_shape=shape_of((NA, 40, LANES), F32),
        in_specs=[SMEM] + vmem(2),
        out_specs=vmem(1)[0],
        scratch_shapes=[
            pltpu.VMEM((NP, 3 * TJ, LANES), F32),
            pltpu.VMEM((NP * TJ, 3 * LANES), F32),
            pltpu.VMEM((3, 256, LANES), F32),
        ],
        compiler_params=PARAMS,
    )(info, got, amps)
    got = exchange(sent, "aux")

    return pl.pallas_call(
        unpack,
        out_shape=shape_of((40, 8, LANES), F32),
        in_specs=vmem(1),
        out_specs=vmem(1)[0],
        compiler_params=PARAMS,
    )(got)


def solution(mesh):
    placed = (
        P("aux", None, "occ"),
        P("aux", None, "occ"),
        P("occ", None),
        P("occ"),
        P("aux", "occ", None),
        P("aux", "occ", None),
        P(),
        P("pair", None),
        P("pair"),
    )
    return jax.shard_map(
        on_device, mesh=mesh, in_specs=placed, out_specs=P("pair", "occ", None), check_vma=False
    )
```

time: 280 us -> 124 us (0.44)
  waiting for transfers between devices: 159 us -> 14.5 us
  blocking collectives: 0 us -> 76.3 us
  local copies, waits for them, and re-layouts: 65.9 us -> 8.75 us
  between operations: 14 us -> 0.71 us
  matrix products: 12.7 us -> 0 us
  Pallas kernels: 0 us -> 7.89 us
  starting transfers between devices: 22.3 us -> 15.7 us
  other arithmetic: 5.24 us -> 0.04 us
    psum x1 -> x0, waiting for transfers between devices: 83.5 us -> none  [on_device(): summed = lax.psum(partial_value, 'aux')]
    all_to_all x0 -> x4, blocking collectives: none -> 76.3 us  [exchange(): return lax.all_to_all(x, axes, split_axis=0, concat_axis=0, tiled=True)]
    reduce_scatter x1 -> x0, waiting for transfers between devices: 69.1 us -> none  [on_device(): result = lax.psum_scatter(summed, 'occ', scatter_dimension=1, tiled=True)]
    reshape x7 -> x1, local copies, waits for them, and re-layouts: 18.2 us -> 0.11 us  [on_device(): pair_blocks.reshape(-1)]
    unnamed x27 -> x11, local copies, waits for them, and re-layouts: 25.1 us -> 7.1 us
    gather x6 -> x0, local copies, waits for them, and re-layouts: 17.3 us -> none  [the longest x1 5.02 us: on_device(): jnp.take(right_fit, col_blk, axis=1)]
    dot_general x4 -> x0, matrix products: 12.7 us -> none  [the longest x1 6.23 us: on_device(): jnp.einsum('ksr,ksc->src', jnp.take(half_fit, row_blk, axis=1), jnp.take(...]
    pallas_call x0 -> x6, Pallas kernels: none -> 7.89 us  [the longest x1 3.27 us: on_device(): pl.pallas_call(partial_t, grid=(3,), out_shape=shape_of((NA, 3 * TJ, LANE...]
  transfers between devices with their start and end apart: 5 -> 1, of which waited for: 3 -> 1; matrix products, arithmetic and copies ran while one was open for 20% -> 1% of each run, Pallas kernels for 0% -> 0%
where the time goes in v1:
time: 124 us
  blocking collectives  76.3 us (62%)
  starting transfers between devices  15.7 us (13%)
  waiting for transfers between devices  14.5 us (12%)
  local copies, waits for them, and re-layouts  8.75 us (7%)
  Pallas kernels  7.89 us (6%)
    all_to_all x4, blocking collectives, exchange(): return lax.all_to_all(x, axes, split_axis=0, concat_axis=0, tiled=True)  76.3 us
    all_to_all x1, starting transfers between devices, exchange(): return lax.all_to_all(x, axes, split_axis=0, concat_axis=0, tiled=True)  15.7 us
    all_to_all x1, waiting for transfers between devices, exchange(): return lax.all_to_all(x, axes, split_axis=0, concat_axis=0, tiled=True)  14.5 us
    unnamed x11, local copies, waits for them, and re-layouts  7.1 us
    pallas_call x1, Pallas kernels, on_device(): pl.pallas_call(partial_t, grid=(3,), out_shape=shape_of((NA, 3 * TJ, LANE...  3.27 us
  transfers between devices with their start and end apart: 1, of which 1 were waited for; matrix products, arithmetic and copies ran while one was open for 1% of the time, Pallas kernels for 0%

profile of v1, /device:TPU:1, one launch (start us, length us, event | category | flops | bytes accessed | tf_op | source)
XLA Modules:
  0.0 123.9 jit_solution(794130437178862497)
XLA Ops:
  0.7 0.8 copy.11
  1.4 0.1 reshape.5
  1.5 0.7 concatenate.3.info
  2.3 0.0 copy-start.2
  2.3 1.0 copy-done.2
  3.3 0.0 copy-start.3
  3.3 0.9 copy-done.3
  4.2 0.0 copy-start.4
  4.2 0.9 copy-done.4
  5.1 1.8 %shard_map.91 = bf16[16,40,256]{2,1,0:T(8,128)(2,1)} custom-call(s32[112]{0:T(128)S(1)} %concatenate.3.info, bf16[18,32,288]{2,1,0:T(8,128)(2,1)S(1)} %bitcast.8, bf16[12,18,288]{2,1,0:T(8,128)(2,1)S(1)} %bitcast.9, bf16[18,3072]{1,0:T(8,128)(2,1)S(1)} %copy-done.4), custom_call_target="tpu_custom_call" | custom-call | tf_op jit(solution)/shard_map/pallas_call | solution.py:206
  6.9 15.7 %all-to-all-start = ((bf16[16,40,256]{2,1,0:T(8,128)(2,1)}), bf16[16,40,256]{2,1,0:T(8,128)(2,1)S(1)}, u32[]{:S(2)}, u32[]{:S(2)}) async-start(bf16[16,40,256]{2,1,0:T(8,128)(2,1)} %shard_map.91), calls=%async_computation | async-start | bytes 655360 | tf_op jit(solution)/shard_map/all_to_all | solution.py:187
  22.7 0.7 pad.4
  23.3 0.1 broadcast_in_dim_tile.3.weight
  23.4 14.5 %all-to-all-done.got.amps = bf16[16,40,256]{2,1,0:T(8,128)(2,1)S(1)} async-done(((bf16[16,40,256]{2,1,0:T(8,128)(2,1)}), bf16[16,40,256]{2,1,0:T(8,128)(2,1)S(1)}, u32[]{:S(2)}, u32[]{:S(2)}) %all-to-all-start) | async-done | bytes 327712 | tf_op jit(solution)/shard_map/all_to_all | solution.py:187
  37.9 0.0 copy-start
  37.9 2.0 %copy-done = bf16[32,18,3072]{2,0,1:T(8,128)(2,1)S(1)} copy-done((bf16[32,18,3072]{2,0,1:T(8,128)(2,1)S(1)}, bf16[32,18,3072]{2,0,1:T(8,128)(2,1)}, u32[]{:S(2)}) %copy-start) | copy-done | bytes 3538968
  39.9 0.0 copy-start.1
  39.9 1.5 %copy-done.1 = bf16[12,18,3072]{2,1,0:T(8,128)(2,1)S(1)} copy-done((bf16[12,18,3072]{2,1,0:T(8,128)(2,1)S(1)}, bf16[12,18,3072]{2,1,0:T(8,128)(2,1)}, u32[]{:S(2)}) %copy-start.1) | copy-done | bytes 1327128
  41.4 3.3 %shard_map.92 = bf16[8,240,128]{2,1,0:T(8,128)(2,1)S(1)} custom-call(bf16[16,40,256]{2,1,0:T(8,128)(2,1)S(1)} %all-to-all-done.got.amps, f32[1,384]{1,0:T(1,128)S(1)} %broadcast_in_dim_tile.3.weight, bf16[18,32,3072]{2,1,0:T(8,128)(2,1)S(1)} %bitcast.7, bf16[12,18,3072]{2,1,0:T(8,128)(2,1)S(1)} %copy-done.1), custom_call_target="tpu_custom_call" | custom-call | tf_op jit(solution)/shard_map/pallas_call | solution.py:220
  44.6 19.6 %all_to_all.25.got = bf16[8,240,128]{2,1,0:T(8,128)(2,1)S(1)} all-to-all(bf16[8,240,128]{2,1,0:T(8,128)(2,1)S(1)} %shard_map.92), channel_id=1, replica_groups=mesh['occ'=16,'aux'=8,'pair'=4] {'aux'}, dimensions={0} | all-to-all | bytes 983040 | tf_op jit(solution)/shard_map/all_to_all | solution.py:187
  64.3 0.1 shard_map.93
  64.4 17.7 %all_to_all.26.got = f32[16,16,128]{2,1,0:T(8,128)S(1)} all-to-all(f32[16,16,128]{2,1,0:T(8,128)S(1)} %shard_map.93), channel_id=1, replica_groups=mesh['occ'=16,'aux'=8,'pair'=4] {'occ'}, dimensions={0} | all-to-all | bytes 262144 | tf_op jit(solution)/shard_map/all_to_all | solution.py:187
  82.1 0.1 shard_map.94
  82.3 27.1 %all_to_all.27 = f16[64,16,128]{2,1,0:T(8,128)(2,1)S(1)} all-to-all(f16[64,16,128]{2,1,0:T(8,128)(2,1)S(1)} %broadcast_in_dim.2), channel_id=1, replica_groups=mesh['occ'=16,'aux'=8,'pair'=4] {'pair','occ'}, dimensions={0} | all-to-all | bytes 524288 | tf_op jit(solution)/shard_map/all_to_all | solution.py:187
  109.4 1.7 %shard_map.95 = f32[8,40,128]{2,1,0:T(8,128)S(1)} custom-call(s32[112]{0:T(128)S(1)} %concatenate.3.info, f32[64,16,128]{2,1,0:T(8,128)S(1)} %convert_element_type.9.got, bf16[16,40,256]{2,1,0:T(8,128)(2,1)S(1)} %all-to-all-done.got.amps), custom_call_target="tpu_custom_call" | custom-call | tf_op jit(solution)/shard_map/pallas_call | solution.py:260
  111.1 11.8 %all_to_all.28.got = f32[8,40,128]{2,1,0:T(8,128)S(1)} all-to-all(f32[8,40,128]{2,1,0:T(8,128)S(1)} %shard_map.95), channel_id=1, replica_groups=mesh['occ'=16,'aux'=8,'pair'=4] {'aux'}, dimensions={0} | all-to-all | bytes 327680 | tf_op jit(solution)/shard_map/all_to_all | solution.py:187
  123.0 0.9 shard_map.96
  (4 shorter events, 0.1 us)
Async XLA Ops:
  2.3 1.0 copy-start.2
  3.3 0.9 copy-start.3
  4.2 0.9 copy-start.4
  6.9 31.0 %all-to-all-start = ((bf16[16,40,256]{2,1,0:T(8,128)(2,1)}), bf16[16,40,256]{2,1,0:T(8,128)(2,1)S(1)}, u32[]{:S(2)}, u32[]{:S(2)}) async-start(bf16[16,40,256]{2,1,0:T(8,128)(2,1)} %shard_map.91), calls=%async_computation | async-start | bytes 655360 | tf_op jit(solution)/shard_map/all_to_all | solution.py:187
  37.9 2.0 %copy-start = (bf16[32,18,3072]{2,0,1:T(8,128)(2,1)S(1)}, bf16[32,18,3072]{2,0,1:T(8,128)(2,1)}, u32[]{:S(2)}) copy-start(bf16[32,18,3072]{2,0,1:T(8,128)(2,1)} %param.13) | copy-start | bytes 10616836
  39.9 1.5 %copy-start.1 = (bf16[12,18,3072]{2,1,0:T(8,128)(2,1)S(1)}, bf16[12,18,3072]{2,1,0:T(8,128)(2,1)}, u32[]{:S(2)}) copy-start(bf16[12,18,3072]{2,1,0:T(8,128)(2,1)} %cabs.1) | copy-start | bytes 3981316

commit v2 on v1

--- a/solution.py
+++ b/solution.py
@@ -48,7 +48,13 @@
 
 
 SMEM = pl.BlockSpec(memory_space=pltpu.SMEM)
-PARAMS = pltpu.CompilerParams(vmem_limit_bytes=40 * 1024 * 1024)
+ANY = pl.BlockSpec(memory_space=pl.ANY)
+
+def room(mib):
+    return pltpu.CompilerParams(vmem_limit_bytes=mib * 1024 * 1024)
+
+
+PARAMS = room(40)
 
 
 NO, NI, NA, NP, NF, NC, NJ = 16, 18, 8, 4, 32, 12, 5
@@ -57,9 +63,22 @@
 TJ = NO * NJ
 
 
-def pack_amps(info, fit, cabs, coef, out, cab32, x, msg):
-    first_j = info[3]
-    x[0 : NJ * NF, :] = fit[pl.ds(first_j, NJ)].reshape(NJ * NF, NO * NI)
+def pack_amps(fit_hbm, cabs_hbm, coef_hbm, out, fit, cabs, coef, cab32, x, msg, sems):
+    first_j = jnp.minimum(NJ * lax.axis_index("pair"), NI - NJ)
+    copies = [
+        pltpu.make_async_copy(cabs_hbm, cabs, sems.at[0]),
+        pltpu.make_async_copy(fit_hbm.at[pl.ds(first_j, NJ)], fit, sems.at[1]),
+        pltpu.make_async_copy(coef_hbm, coef, sems.at[2]),
+    ]
+    for c in copies:
+        c.start()
+    shape = (NO, ROWS, NO * NI)
+    t = iota(shape, 1)
+    place = jnp.where((iota(shape, 2) == NI * iota(shape, 0) + t) & (t < NI), 1.0, 0.0)
+    place = place.reshape(NO * ROWS, NO * NI).astype(BF16)
+    for c in copies:
+        c.wait()
+    x[0 : NJ * NF, :] = fit[...].reshape(NJ * NF, NO * NI)
     for q in range(NC):
         cab32[24 * q : 24 * q + NI, :] = cabs[q].astype(F32)
     zero = jnp.zeros((CQ - NC, NO * NI), F32)
@@ -68,10 +87,6 @@
         rows = jnp.concatenate(picked + [zero], axis=0)
         x[NJ * NF + CQ * jj : NJ * NF + CQ * (jj + 1), :] = rows.astype(BF16)
     x[NJ * (NF + CQ) :, :] = jnp.zeros((256 - NJ * (NF + CQ), NO * NI), BF16)
-    shape = (NO, ROWS, NO * NI)
-    t = iota(shape, 1)
-    place = jnp.where((iota(shape, 2) == NI * iota(shape, 0) + t) & (t < NI), 1.0, 0.0)
-    place = place.reshape(NO * ROWS, NO * NI).astype(BF16)
     msg[...] = dot(place, x[...], NT).reshape(NO, ROWS, 256)
     tiles = [coef[:, LANES * a : LANES * (a + 1)].astype(F32) for a in range(24)]
     none = jnp.zeros_like(tiles[0])
@@ -83,45 +98,55 @@
     out[...] = msg[...].astype(BF16)
 
 
-def partial_t(got, weight, fit, cabs, out, a_fit, a_cab, padded):
-    @pl.when(pl.program_id(0) == 0)
-    def _():
-        shape = (NI, NO, NO * ROWS)
-        pick = jnp.where(iota(shape, 2) == ROWS * iota(shape, 1) + iota(shape, 0), 1.0, 0.0)
-        pick = pick.reshape(NI * NO, NO * ROWS).astype(BF16)
-        amps = dot(pick, got[...].reshape(NO * ROWS, 256))
-        amps = [[amps[NO * t : NO * (t + 1), LANES * h : LANES * (h + 1)] for h in (0, 1)] for t in range(NI)]
-        lane = iota((NO, LANES), 1)
-
-        def lay(ref_rows, width, start, store):
-            per = LANES // width
-            for jj in range(NJ):
-                half, off = divmod(start + width * jj, LANES)
-                for m in range(-(-NI // per)):
-                    tile = jnp.zeros((NO, LANES), F32)
-                    for k in range(min(per, NI - m * per)):
-                        moved = amps[m * per + k][half]
-                        if (width * k - off) % LANES:
-                            moved = pltpu.roll(moved, (width * k - off) % LANES, 1)
-                        tile = jnp.where((lane >= width * k) & (lane < width * (k + 1)), moved, tile)
-                    store[NO * jj : NO * (jj + 1), LANES * m : LANES * (m + 1)] = tile.astype(BF16)
-
-        lay(NO, NF, 0, a_fit)
-        lay(NO, CQ, NJ * NF, a_cab)
-        shape = (3 * LANES, 32 * NC)
-        source = iota(shape, 0)
-        target = iota(shape, 1)
-        order = one_hot(((target >> 5) == (source & 15)) & ((target & 31) == (source >> 4)))
-        weighted = dot(a_cab[...], order) * weight[...]
-        a_cab[...] = weighted.astype(BF16)
-        padded[...] = jnp.zeros(padded.shape, BF16)
-
-    for q in range(NC):
-        padded[32 * q : 32 * q + NI, :] = cabs[q]
-    total = dot(a_fit[:, : NI * NF], fit[...].reshape(NI * NF, 1024)) + dot(a_cab[...], padded[...])
-    pieces = swap_pieces([total[:, LANES * k : LANES * (k + 1)] for k in range(8)], 16)
-    for k in range(8):
-        out[k] = pieces[k].astype(BF16)
+def partial_t(got, weight, fit_hbm, cabs_hbm, out, a_fit, a_cab, fit, cabs, padded, sems):
+    spans = [pl.ds(1024 * g, 1024) for g in range(3)]
+    copies = [
+        (
+            pltpu.make_async_copy(cabs_hbm.at[:, :, s], cabs.at[:, :, s], sems.at[0, g]),
+            pltpu.make_async_copy(fit_hbm.at[:, s], fit.at[:, s], sems.at[1, g]),
+        )
+        for g, s in enumerate(spans)
+    ]
+    for pair in copies:
+        for c in pair:
+            c.start()
+    padded[...] = jnp.zeros(padded.shape, BF16)
+    shape = (NI, NO, NO * ROWS)
+    pick = jnp.where(iota(shape, 2) == ROWS * iota(shape, 1) + iota(shape, 0), 1.0, 0.0)
+    pick = pick.reshape(NI * NO, NO * ROWS).astype(BF16)
+    amps = dot(pick, got[...].reshape(NO * ROWS, 256))
+    amps = [[amps[NO * t : NO * (t + 1), LANES * h : LANES * (h + 1)] for h in (0, 1)] for t in range(NI)]
+    lane = iota((NO, LANES), 1)
+
+    def lay(width, start, store):
+        per = LANES // width
+        for jj in range(NJ):
+            half, off = divmod(start + width * jj, LANES)
+            for m in range(-(-NI // per)):
+                tile = jnp.zeros((NO, LANES), F32)
+                for k in range(min(per, NI - m * per)):
+                    moved = amps[m * per + k][half]
+                    if (width * k - off) % LANES:
+                        moved = pltpu.roll(moved, (width * k - off) % LANES, 1)
+                    tile = jnp.where((lane >= width * k) & (lane < width * (k + 1)), moved, tile)
+                store[NO * jj : NO * (jj + 1), LANES * m : LANES * (m + 1)] = tile.astype(BF16)
+
+    lay(NF, 0, a_fit)
+    lay(CQ, NJ * NF, a_cab)
+    shape = (3 * LANES, 32 * NC)
+    source = iota(shape, 0)
+    target = iota(shape, 1)
+    order = one_hot(((target >> 5) == (source & 15)) & ((target & 31) == (source >> 4)))
+    a_cab[...] = (dot(a_cab[...], order) * weight[...]).astype(BF16)
+    for g in range(3):
+        for c in copies[g]:
+            c.wait()
+        for q in range(NC):
+            padded[32 * q : 32 * q + NI, :] = cabs[q, :, spans[g]]
+        total = dot(a_fit[:, : NI * NF], fit[:, spans[g]]) + dot(a_cab[...], padded[...])
+        pieces = swap_pieces([total[:, LANES * k : LANES * (k + 1)] for k in range(8)], 16)
+        for k in range(8):
+            out[k, TJ * g : TJ * (g + 1), :] = pieces[k].astype(BF16)
 
 
 def sum_aux(got, out, total):
@@ -139,8 +164,8 @@
     out[...] = jnp.where(iota(total.shape, 0) == 15, power, scaled)
 
 
-def pair_blocks_kernel(info, got, amps, out, tsum, tmat, dmat):
-    occ, aux, count = info[0], info[1], info[4]
+def pair_blocks_kernel(lens, pairs, counts, got, amps, out, tsum, tmat, dmat):
+    occ, aux, count = lax.axis_index("occ"), lax.axis_index("aux"), counts[0]
     values = got[...]
     values = values * (jnp.exp(values[:, 15:16, :] * LN2) * (1.0 / 16384.0))
     for y in range(NP):
@@ -166,11 +191,11 @@
         tile = jnp.zeros((8, LANES), F32)
         for k in range(8):
             slot = 8 * q + k
-            a, b = info[32 + 2 * slot], info[33 + 2 * slot]
+            a, b = pairs[0, slot], pairs[1, slot]
             block = dmat[b >> 3, pl.ds(pl.multiple_of(8 * a, 8), 8), :]
             block = pltpu.roll(block, (16 * (k + 8 - (b & 7))) & 127, 1)
-            rows_kept = jnp.where(slot < count, info[8 + a] - 8 * occ, 0)
-            lanes_kept = jnp.clip(info[8 + b] - 16 * aux, 0, 16) + 16 * k
+            rows_kept = jnp.where(slot < count, lens[a] - 8 * occ, 0)
+            lanes_kept = jnp.clip(lens[b] - 16 * aux, 0, 16) + 16 * k
             tile = jnp.where((lane >= 16 * k) & (lane < lanes_kept) & (row < rows_kept), block, tile)
         for p in range(NA):
             out[p, 8 * q : 8 * (q + 1), :] = tile
@@ -192,49 +217,41 @@
 
 
 def on_device(amp_fit, amp_cabs, coef, f12_weight, ints_fit, ints_cabs, shell_len, pair_blocks, pair_count):
-    occ, aux, pair = (lax.axis_index(a).astype(jnp.int32) for a in ("occ", "aux", "pair"))
-    first_j = jnp.minimum(NJ * pair, NI - NJ)
-    info = jnp.concatenate(
-        [
-            jnp.stack([occ, aux, pair, first_j, pair_count[0], occ, occ, occ]),
-            shell_len,
-            pair_blocks.reshape(-1),
-        ]
-    )
     weight = jnp.tile(jnp.pad(f12_weight, (0, 32 - NI)), NC)[None, :]
 
     sent = pl.pallas_call(
         pack_amps,
         out_shape=shape_of((NO, ROWS, 256), BF16),
-        in_specs=[SMEM] + vmem(3),
+        in_specs=[ANY] * 3,
         out_specs=vmem(1)[0],
         scratch_shapes=[
+            pltpu.VMEM((NJ, NF, NO * NI), BF16),
+            pltpu.VMEM((NC, NI, NO * NI), BF16),
+            pltpu.VMEM((NI, 24 * LANES), BF16),
             pltpu.VMEM((24 * NC, NO * NI), F32),
             pltpu.VMEM((256, NO * NI), BF16),
             pltpu.VMEM((NO, ROWS, 256), F32),
+            pltpu.SemaphoreType.DMA((3,)),
         ],
-        compiler_params=PARAMS,
-    )(info, jnp.transpose(amp_fit, (2, 0, 1)), jnp.transpose(amp_cabs, (0, 2, 1)), coef)
+        compiler_params=room(60),
+    )(jnp.transpose(amp_fit, (2, 0, 1)), jnp.transpose(amp_cabs, (0, 2, 1)), coef)
     amps = exchange(sent, "occ")
 
     sent = pl.pallas_call(
         partial_t,
-        grid=(3,),
         out_shape=shape_of((NA, 3 * TJ, LANES), BF16),
-        in_specs=[
-            pl.BlockSpec((NO, ROWS, 256), lambda g: (0, 0, 0)),
-            pl.BlockSpec((1, 32 * NC), lambda g: (0, 0)),
-            pl.BlockSpec((NI, NF, 1024), lambda g: (0, 0, g)),
-            pl.BlockSpec((NC, NI, 1024), lambda g: (0, 0, g)),
-        ],
-        out_specs=pl.BlockSpec((NA, TJ, LANES), lambda g: (0, g, 0)),
+        in_specs=vmem(2) + [ANY] * 2,
+        out_specs=vmem(1)[0],
         scratch_shapes=[
             pltpu.VMEM((TJ, 5 * LANES), BF16),
             pltpu.VMEM((TJ, 3 * LANES), BF16),
+            pltpu.VMEM((NI * NF, 24 * LANES), BF16),
+            pltpu.VMEM((NC, NI, 24 * LANES), BF16),
             pltpu.VMEM((32 * NC, 1024), BF16),
+            pltpu.SemaphoreType.DMA((2, 3)),
         ],
-        compiler_params=PARAMS,
-    )(amps, weight, jnp.transpose(ints_fit, (1, 0, 2)), ints_cabs)
+        compiler_params=room(52),
+    )(amps, weight, jnp.transpose(ints_fit, (1, 0, 2)).reshape(NI * NF, 24 * LANES), ints_cabs)
     got = exchange(sent, "aux")
 
     sent = pl.pallas_call(
@@ -260,7 +277,7 @@
     sent = pl.pallas_call(
         pair_blocks_kernel,
         out_shape=shape_of((NA, 40, LANES), F32),
-        in_specs=[SMEM] + vmem(2),
+        in_specs=[SMEM] * 3 + vmem(2),
         out_specs=vmem(1)[0],
         scratch_shapes=[
             pltpu.VMEM((NP, 3 * TJ, LANES), F32),
@@ -268,7 +285,7 @@
             pltpu.VMEM((3, 256, LANES), F32),
         ],
         compiler_params=PARAMS,
-    )(info, got, amps)
+    )(shell_len, pair_blocks.T, pair_count, got, amps)
     got = exchange(sent, "aux")
 
     return pl.pallas_call(

time: 124 us -> 118 us (0.952)
  blocking collectives: 76.3 us -> 49.2 us
  waiting for transfers between devices: 14.5 us -> 31.9 us
  starting transfers between devices: 15.7 us -> 24.9 us
  local copies, waits for them, and re-layouts: 8.75 us -> 1.5 us
  Pallas kernels: 7.89 us -> 9.16 us
    all_to_all x4 -> x3, blocking collectives: 76.3 us -> 49.2 us  [exchange(): return lax.all_to_all(x, axes, split_axis=0, concat_axis=0, tiled=True)]
    all_to_all x1 -> x2, waiting for transfers between devices: 14.5 us -> 31.9 us  [exchange(): return lax.all_to_all(x, axes, split_axis=0, concat_axis=0, tiled=True)]
    all_to_all x1 -> x2, starting transfers between devices: 15.7 us -> 24.9 us  [exchange(): return lax.all_to_all(x, axes, split_axis=0, concat_axis=0, tiled=True)]
    unnamed x11 -> x4, local copies, waits for them, and re-layouts: 7.1 us -> 0.01 us
  transfers between devices with their start and end apart: 1 -> 2, of which waited for: 1 -> 2; matrix products, arithmetic and copies ran while one was open for 1% -> 1% of each run, Pallas kernels for 0% -> 0%
where the time goes in v2:
time: 118 us; the launch traced here: 117 us
  blocking collectives  49.2 us (42%)
  waiting for transfers between devices  31.9 us (27%)
  starting transfers between devices  24.9 us (21%)
  Pallas kernels  9.16 us (8%)
  local copies, waits for them, and re-layouts  1.5 us (1%)
    all_to_all x3, blocking collectives, exchange(): return lax.all_to_all(x, axes, split_axis=0, concat_axis=0, tiled=True)  49.2 us
    all_to_all x2, waiting for transfers between devices, exchange(): return lax.all_to_all(x, axes, split_axis=0, concat_axis=0, tiled=True)  31.9 us
    all_to_all x2, starting transfers between devices, exchange(): return lax.all_to_all(x, axes, split_axis=0, concat_axis=0, tiled=True)  24.9 us
    pallas_call x1, Pallas kernels, on_device(): pl.pallas_call(partial_t, out_shape=shape_of((NA, 3 * TJ, LANES), BF16),...  4 us
  transfers between devices with their start and end apart: 2, of which 2 were waited for; matrix products, arithmetic and copies ran while one was open for 1% of the time, Pallas kernels for 0%

profile of v2, /device:TPU:1, one launch (start us, length us, event | category | flops | bytes accessed | tf_op | source)
XLA Modules:
  0.0 117.5 jit_solution(7820742880814136656)
XLA Ops:
  0.0 2.3 %shard_map.91 = bf16[16,40,256]{2,1,0:T(8,128)(2,1)} custom-call(bf16[18,32,288]{2,1,0:T(8,128)(2,1)} %bitcast.8, bf16[12,18,288]{2,1,0:T(8,128)(2,1)} %bitcast.9, bf16[18,3072]{1,0:T(8,128)(2,1)} %coef_hbm.1), custom_call_target="tpu_custom_call" | custom-call | tf_op jit(solution)/shard_map/pallas_call | solution.py:222
  2.3 15.8 %all-to-all-start = ((bf16[16,40,256]{2,1,0:T(8,128)(2,1)}), bf16[16,40,256]{2,1,0:T(8,128)(2,1)S(1)}, u32[]{:S(2)}, u32[]{:S(2)}) async-start(bf16[16,40,256]{2,1,0:T(8,128)(2,1)} %shard_map.91), calls=%async_computation | async-start | bytes 655360 | tf_op jit(solution)/shard_map/all_to_all | solution.py:212
  18.1 0.7 pad.4
  18.8 0.1 broadcast_in_dim_tile.3.weight
  18.8 14.5 %all-to-all-done.got.amps = bf16[16,40,256]{2,1,0:T(8,128)(2,1)S(1)} async-done(((bf16[16,40,256]{2,1,0:T(8,128)(2,1)}), bf16[16,40,256]{2,1,0:T(8,128)(2,1)S(1)}, u32[]{:S(2)}, u32[]{:S(2)}) %all-to-all-start) | async-done | bytes 327712 | tf_op jit(solution)/shard_map/all_to_all | solution.py:212
  33.3 0.0 copy-start
  33.3 0.0 copy-start.1
  33.3 4.0 %shard_map.92 = bf16[8,240,128]{2,1,0:T(8,128)(2,1)S(1)} custom-call(bf16[16,40,256]{2,1,0:T(8,128)(2,1)S(1)} %all-to-all-done.got.amps, f32[1,384]{1,0:T(1,128)S(1)} %broadcast_in_dim_tile.3.weight, bf16[576,3072]{1,0:T(8,128)(2,1)} %bitcast.7, bf16[12,18,3072]{2,1,0:T(8,128)(2,1)} %cabs_hbm.1), custom_call_target="tpu_custom_call" | custom-call | tf_op jit(solution)/shard_map/pallas_call | solution.py:240
  37.3 19.6 %all_to_all.25.got = bf16[8,240,128]{2,1,0:T(8,128)(2,1)S(1)} all-to-all(bf16[8,240,128]{2,1,0:T(8,128)(2,1)S(1)} %shard_map.92), channel_id=1, replica_groups=mesh['occ'=16,'aux'=8,'pair'=4] {'aux'}, dimensions={0} | all-to-all | bytes 983040 | tf_op jit(solution)/shard_map/all_to_all | solution.py:212
  57.0 0.1 shard_map.93
  57.1 17.7 %all_to_all.26.got = f32[16,16,128]{2,1,0:T(8,128)S(1)} all-to-all(f32[16,16,128]{2,1,0:T(8,128)S(1)} %shard_map.93), channel_id=1, replica_groups=mesh['occ'=16,'aux'=8,'pair'=4] {'occ'}, dimensions={0} | all-to-all | bytes 262144 | tf_op jit(solution)/shard_map/all_to_all | solution.py:212
  74.8 0.1 shard_map.94
  74.9 0.7 broadcast_in_dim.2
  75.6 9.2 %all-to-all-start.3 = ((f16[64,16,128]{2,1,0:T(8,128)(2,1)}), f16[64,16,128]{2,1,0:T(8,128)(2,1)S(1)}, u32[]{:S(2)}, u32[]{:S(2)}) async-start(f16[64,16,128]{2,1,0:T(8,128)(2,1)} %broadcast_in_dim.2), calls=%async_computation.3 | async-start | bytes 524288 | tf_op jit(solution)/shard_map/all_to_all | solution.py:212
  85.5 17.4 %all-to-all-done.3 = f16[64,16,128]{2,1,0:T(8,128)(2,1)S(1)} async-done(((f16[64,16,128]{2,1,0:T(8,128)(2,1)}), f16[64,16,128]{2,1,0:T(8,128)(2,1)S(1)}, u32[]{:S(2)}, u32[]{:S(2)}) %all-to-all-start.3) | async-done | bytes 262176 | tf_op jit(solution)/shard_map/all_to_all | solution.py:212
  102.9 0.0 copy-done
  103.0 0.0 copy-done.1
  103.0 1.7 %shard_map.95 = f32[8,40,128]{2,1,0:T(8,128)S(1)} custom-call(s32[24]{0:T(128)S(1)} %copy-done.1, s32[2,40]{1,0:T(2,128)S(1)} %bitcast.6, s32[1]{0:T(128)S(6)} %copy.10.counts, f32[64,16,128]{2,1,0:T(8,128)S(1)} %convert_element_type.9.got, bf16[16,40,256]{2,1,0:T(8,128)(2,1)S(1)} %all-to-all-done.got.amps), custom_call_target="tpu_custom_call" | custom-call | tf_op jit(solution)/shard_map/pallas_call | solution.py:277
  104.7 11.9 %all_to_all.27.got = f32[8,40,128]{2,1,0:T(8,128)S(1)} all-to-all(f32[8,40,128]{2,1,0:T(8,128)S(1)} %shard_map.95), channel_id=1, replica_groups=mesh['occ'=16,'aux'=8,'pair'=4] {'aux'}, dimensions={0} | all-to-all | bytes 327680 | tf_op jit(solution)/shard_map/all_to_all | solution.py:212
  116.5 0.9 shard_map.96
  (3 shorter events, 0.0 us)
Async XLA Ops:
  2.3 31.0 %all-to-all-start = ((bf16[16,40,256]{2,1,0:T(8,128)(2,1)}), bf16[16,40,256]{2,1,0:T(8,128)(2,1)S(1)}, u32[]{:S(2)}, u32[]{:S(2)}) async-start(bf16[16,40,256]{2,1,0:T(8,128)(2,1)} %shard_map.91), calls=%async_computation | async-start | bytes 655360 | tf_op jit(solution)/shard_map/all_to_all | solution.py:212
  33.3 69.6 %copy-start = (s32[40,2]{0,1:T(2,128)S(1)}, s32[40,2]{0,1:T(2,128)}, u32[]{:S(2)}) copy-start(s32[40,2]{0,1:T(2,128)} %param.16) | copy-start | bytes 964
  33.3 69.6 %copy-start.1 = (s32[24]{0:T(128)S(1)}, s32[24]{0:T(128)}, u32[]{:S(2)}) copy-start(s32[24]{0:T(128)} %lens.1) | copy-start | bytes 292
  75.6 27.3 %all-to-all-start.3 = ((f16[64,16,128]{2,1,0:T(8,128)(2,1)}), f16[64,16,128]{2,1,0:T(8,128)(2,1)S(1)}, u32[]{:S(2)}, u32[]{:S(2)}) async-start(f16[64,16,128]{2,1,0:T(8,128)(2,1)} %broadcast_in_dim.2), calls=%async_computation.3 | async-start | bytes 524288 | tf_op jit(solution)/shard_map/all_to_all | solution.py:212

commit v3 on v2

v3 whole, which is shorter than its diff:
```python
import functools
import math

import jax
import jax.numpy as jnp
from jax import lax
from jax.experimental import pallas as pl
from jax.experimental.pallas import tpu as pltpu
from jax.sharding import PartitionSpec as P

F32, BF16, F16 = jnp.float32, jnp.bfloat16, jnp.float16
LANES = 128
LN2 = math.log(2.0)
NT = (((1,), (1,)), ((), ()))
TN = (((0,), (0,)), ((), ()))


def iota(shape, dim):
    return lax.broadcasted_iota(jnp.int32, shape, dim)


def dot(a, b, dims=(((1,), (0,)), ((), ()))):
    return lax.dot_general(a, b, dims, preferred_element_type=F32)


def one_hot(cond):
    return jnp.where(cond, 1.0, 0.0).astype(BF16)


def swap_pieces(xs, piece):
    lane = iota(xs[0].shape, 1)
    bit = 1
    while bit < len(xs):
        keep = ((lane // piece) & bit) == 0
        ys = list(xs)
        for k in range(len(xs)):
            if k & bit == 0:
                lo, hi = xs[k], xs[k + bit]
                ys[k] = jnp.where(keep, lo, pltpu.roll(hi, piece * bit, 1))
                ys[k + bit] = jnp.where(keep, pltpu.roll(lo, LANES - piece * bit, 1), hi)
        xs = ys
        bit *= 2
    return xs


def vmem(n):
    return [pl.BlockSpec(memory_space=pltpu.VMEM)] * n


SMEM = pl.BlockSpec(memory_space=pltpu.SMEM)
ANY = pl.BlockSpec(memory_space=pl.ANY)

def room(mib):
    return pltpu.CompilerParams(vmem_limit_bytes=mib * 1024 * 1024)


PARAMS = room(40)


NO, NI, NA, NP, NF, NC, NJ = 16, 18, 8, 4, 32, 12, 5
CQ = 16
TJ = NO * NJ
TROWS = 3 * TJ
ROWS = 24
CROWS = 240


def pack_amps(fit_hbm, cabs_hbm, coef_hbm, out, fit, cabs, coef, cab32, x, extra, piece, sems):
    aux, pair = lax.axis_index("aux"), lax.axis_index("pair")
    first_j = jnp.minimum(NJ * pair, NI - NJ)
    columns = pl.ds(pl.multiple_of(3 * LANES * aux, LANES), 3 * LANES)
    copies = [
        pltpu.make_async_copy(cabs_hbm, cabs, sems.at[0]),
        pltpu.make_async_copy(fit_hbm.at[pl.ds(first_j, NJ)], fit, sems.at[1]),
        pltpu.make_async_copy(coef_hbm.at[:, columns], coef, sems.at[2]),
    ]
    for c in copies:
        c.start()
    shape = (NO, ROWS, NO * NI)
    t = iota(shape, 1)
    place = jnp.where((iota(shape, 2) == NI * iota(shape, 0) + t) & (t < NI), 1.0, 0.0)
    place = place.reshape(NO * ROWS, NO * NI).astype(BF16)
    source, target = iota((LANES, LANES), 0), iota((LANES, LANES), 1)
    mine = source == 8 * (target & 15) + 2 * pair + ((target >> 4) & 1)
    for c in copies:
        c.wait()
    x[0 : NJ * NF, :] = fit[...].reshape(NJ * NF, NO * NI)
    for q in range(NC):
        cab32[24 * q : 24 * q + NI, :] = cabs[q].astype(F32)
    zero = jnp.zeros((CQ - NC, NO * NI), F32)
    for jj in range(NJ):
        picked = [cab32[pl.ds(24 * q + first_j + jj, 1), :] for q in range(NC)]
        rows = jnp.concatenate(picked + [zero], axis=0)
        x[NJ * NF + CQ * jj : NJ * NF + CQ * (jj + 1), :] = rows.astype(BF16)
    x[NJ * (NF + CQ) :, :] = jnp.zeros((256 - NJ * (NF + CQ), NO * NI), BF16)
    piece[...] = sum(
        dot(coef[:, LANES * k : LANES * (k + 1)], one_hot(mine & ((target >> 5) == k))) for k in range(3)
    )
    lane = iota((6, LANES), 1)
    third = piece[12:18, :]
    extra[...] = jnp.zeros(extra.shape, F32)
    extra[18:24, 0:LANES] = jnp.where(lane < 96, piece[0:6, :], pltpu.roll(third, 96, 1))
    extra[18:24, LANES:] = jnp.where(lane < 96, piece[6:12, :], pltpu.roll(third, 64, 1))
    extra[0:6, LANES:] = jnp.where(lane >= 112, pltpu.roll(third, 48, 1), 0.0)
    extra[6:12, LANES:] = jnp.where(lane >= 112, pltpu.roll(third, 32, 1), 0.0)
    out[...] = (dot(place, x[...], NT).reshape(NO, ROWS, 256) + extra[...][None]).astype(BF16)


def partial_t(got, weight, fit_hbm, cabs_hbm, out, a_fit, a_cab, fit, cabs, padded, own, sems):
    spans = [pl.ds(1024 * g, 1024) for g in range(3)]
    copies = [
        (
            pltpu.make_async_copy(cabs_hbm.at[:, :, s], cabs.at[:, :, s], sems.at[0, g]),
            pltpu.make_async_copy(fit_hbm.at[:, s], fit.at[:, s], sems.at[1, g]),
        )
        for g, s in enumerate(spans)
    ]
    for pair in copies:
        for c in pair:
            c.start()
    padded[...] = jnp.zeros(padded.shape, BF16)
    messages = got[...].reshape(NO * ROWS, 256)
    shape = (NI, NO, NO * ROWS)
    pick = jnp.where(iota(shape, 2) == ROWS * iota(shape, 1) + iota(shape, 0), 1.0, 0.0)
    pick = pick.reshape(NI * NO, NO * ROWS).astype(BF16)
    amps = dot(pick, messages)
    amps = [[amps[NO * t : NO * (t + 1), LANES * h : LANES * (h + 1)] for h in (0, 1)] for t in range(NI)]
    lane = iota((NO, LANES), 1)

    def lay(width, start, store):
        per = LANES // width
        for jj in range(NJ):
            half, off = divmod(start + width * jj, LANES)
            for m in range(-(-NI // per)):
                tile = jnp.zeros((NO, LANES), F32)
                for k in range(min(per, NI - m * per)):
                    moved = amps[m * per + k][half]
                    if (width * k - off) % LANES:
                        moved = pltpu.roll(moved, (width * k - off) % LANES, 1)
                    tile = jnp.where((lane >= width * k) & (lane < width * (k + 1)), moved, tile)
                store[NO * jj : NO * (jj + 1), LANES * m : LANES * (m + 1)] = tile.astype(BF16)

    lay(NF, 0, a_fit)
    lay(CQ, NJ * NF, a_cab)
    shape = (3 * LANES, 32 * NC)
    source = iota(shape, 0)
    target = iota(shape, 1)
    order = one_hot(((target >> 5) == (source & 15)) & ((target & 31) == (source >> 4)))
    a_cab[...] = (dot(a_cab[...], order) * weight[...]).astype(BF16)

    shape = (NO * NI, NO * ROWS)
    row, source = iota(shape, 0), iota(shape, 1)
    occ = (row * 3641) >> 16
    rest = row - NI * occ
    sixth = rest - jnp.where(rest >= 12, 12, jnp.where(rest >= 6, 6, 0))
    base = source - ROWS * occ - sixth
    main = dot(one_hot(base == 18), messages)
    spare0 = dot(one_hot(base == 0), messages[:, LANES:])
    spare1 = dot(one_hot(base == 6), messages[:, LANES:])
    shape = (NO * NI, LANES)
    lane, row = iota(shape, 1), iota(shape, 0)
    rest = row - NI * ((row * 3641) >> 16)
    third = jnp.where(lane < 32, pltpu.roll(main[:, :LANES], 32, 1), pltpu.roll(main[:, LANES:], 64, 1))
    third = jnp.where(lane < 64, third, pltpu.roll(spare0, 80, 1))
    third = jnp.where(lane < 80, third, pltpu.roll(spare1, 96, 1))
    coef = jnp.where(rest < 6, main[:, :LANES], jnp.where(rest < 12, main[:, LANES:], third))
    last = coef[TROWS:]
    lane = iota((48, LANES), 1)
    for b in range(3):
        own[TJ * b : TJ * (b + 1), :] = coef[TJ * b : TJ * (b + 1)]
        moved = pltpu.roll(last, 96 - 32 * b, 1)
        own[TJ * b : TJ * b + 48, :] = jnp.where(lane < 96, coef[TJ * b : TJ * b + 48], moved)
    packed = own[...].astype(BF16)
    for p in range(NA):
        out[p, TROWS:, :] = packed

    for g in range(3):
        for c in copies[g]:
            c.wait()
        for q in range(NC):
            padded[32 * q : 32 * q + NI, :] = cabs[q, :, spans[g]]
        total = dot(a_fit[:, : NI * NF], fit[:, spans[g]]) + dot(a_cab[...], padded[...])
        pieces = swap_pieces([total[:, LANES * k : LANES * (k + 1)] for k in range(8)], 16)
        for k in range(8):
            out[k, TJ * g : TJ * (g + 1), :] = pieces[k].astype(BF16)


def scale_of(top):
    top = jnp.max(jnp.max(top, axis=1, keepdims=True), axis=0, keepdims=True)
    power = jnp.ceil(jnp.log(jnp.maximum(top, 1e-30)) * (1.0 / LN2))
    return power, jnp.exp(power * -LN2) * 16384.0


def unscale(power):
    return jnp.exp(power * LN2) * (1.0 / 16384.0)


def sum_aux(counts, pairs, got, out):
    total = jnp.sum(got[:, 0:TROWS, :].astype(F32), axis=0)
    power, factor = scale_of(jnp.abs(total))
    out[0:TROWS, :] = total * factor
    out[TROWS:, :] = jnp.zeros((16, LANES), F32)
    out[TROWS : TROWS + 1, :] = jnp.broadcast_to(power, (1, LANES))
    out[TROWS + 1 : TROWS + 3, 0:40] = pairs[...].astype(F32)
    out[TROWS + 3 : TROWS + 4, :] = jnp.broadcast_to(counts[0].astype(F32), (1, LANES))


def all_blocks(lens, got, coefs, out, ints, words, tmat, dmat, msg, sem):
    aux, pair = lax.axis_index("aux"), lax.axis_index("pair")
    for y in range(NP):
        ints[8 * y : 8 * (y + 1), :] = got[y, TROWS : TROWS + 8, :].astype(jnp.int32)
    copy = pltpu.make_async_copy(ints, words, sem)
    copy.start()

    lane = iota((1, LANES), 1)
    for g in range(3):
        limit = jnp.zeros((1, LANES), jnp.int32)
        for k in range(8):
            limit = jnp.where((lane >> 4) == k, lens[8 * g + k], limit)
        kept = (lane & 15) + 16 * aux < limit
        for y in range(NP):
            part = got[y, TJ * g : TJ * (g + 1), :] * unscale(got[y, TROWS : TROWS + 1, :])
            part = jnp.where(kept, part, 0.0)
            high = part.astype(BF16)
            tmat[TJ * y : TJ * (y + 1), LANES * g : LANES * (g + 1)] = high
            low = (part - high.astype(F32)).astype(BF16)
            tmat[TJ * y : TJ * (y + 1), LANES * (g + 3) : LANES * (g + 4)] = low
    shape = (NP, NJ, NO, NO * NI)
    y, jj = iota(shape, 0), iota(shape, 1)
    j = jnp.minimum(NJ * y, NI - NJ) + jj
    pick = (iota(shape, 3) == NI * iota(shape, 2) + j) & (j >= NJ * y)
    pick = jnp.where(pick, 1.0, 0.0).reshape(NP * TJ, NO * NI).astype(BF16)
    ordered = dot(pick, tmat[...], TN).astype(BF16)

    for p in range(NA):
        limit = jnp.zeros((1, LANES), jnp.int32)
        for k in range(3):
            limit = jnp.where((lane >> 5) == k, lens[3 * p + k], limit)
        kept = 8 * (lane & 15) + 2 * pair + ((lane >> 4) & 1) < limit
        rows = [coefs[p, TROWS + TJ * b : TROWS + TJ * (b + 1), :].astype(F32) for b in range(3)]
        last = pltpu.roll(rows[0][:48], 32, 1)
        last = jnp.where(lane >= 32, pltpu.roll(rows[1][:48], 64, 1), last)
        last = jnp.where(lane >= 64, pltpu.roll(rows[2][:48], 96, 1), last)
        coef = jnp.concatenate(rows + [last], axis=0)
        coef = jnp.where(kept, coef, 0.0).astype(BF16)
        blocks = dot(coef, ordered[:, : 3 * LANES], TN) + dot(coef, ordered[:, 3 * LANES :], TN)
        for g in range(3):
            dmat[g, LANES * p : LANES * (p + 1), :] = blocks[:, LANES * g : LANES * (g + 1)]

    copy.wait()
    lane = iota((32, LANES), 1)
    top = jnp.zeros((32, LANES), F32)
    for q in range(20):
        y = q // 5
        count = words[8 * y + 3, 0]
        tile = jnp.zeros((32, LANES), F32)
        for k in range(8):
            slot = 8 * (q % 5) + k
            a, b = words[8 * y + 1, slot], words[8 * y + 2, slot]
            third = (a * 171) >> 9
            start = pl.multiple_of(LANES * third + 32 * (a - 3 * third), 32)
            block = dmat[b >> 3, pl.ds(start, 32), :]
            block = pltpu.roll(block, (16 * (k + 8 - (b & 7))) & 127, 1)
            end = jnp.where(slot < count, 16 * (k + 1), 0)
            tile = jnp.where((lane >= 16 * k) & (lane < end), block, tile)
        top = jnp.maximum(top, jnp.abs(tile))
        for e in range(2):
            msg[pl.ds(2 * q + e, NO, stride=48), :] = tile[NO * e : NO * (e + 1)]
    power, factor = scale_of(top)
    row = iota((48, LANES), 0)
    for o in range(NO):
        scaled = jnp.where(row < 40, msg[48 * o : 48 * (o + 1), :] * factor, 0.0)
        out[o] = jnp.where(row == 40, power, scaled)


def sum_occ(got, out, total):
    total[...] = sum(got[o, 0:40, :] * unscale(got[o, 40:41, :]) for o in range(NO))
    for y in range(NP):
        rows = total[10 * y : 10 * (y + 1), :]
        for p in range(NA):
            out[NA * y + p, 0:10, :] = rows
            out[NA * y + p, 10:16, :] = jnp.zeros((6, LANES), F32)


def unpack(got, out, rows):
    for q in range(5):
        for p in range(NA):
            for y in range(NP):
                rows[p, 2 * y : 2 * y + 2, :] = got[NA * y + p, 2 * q : 2 * q + 2, :]
        blocks = swap_pieces([rows[p] for p in range(NA)], 16)
        for k in range(8):
            out[8 * q + k] = blocks[k]


def exchange(x, axes):
    return lax.all_to_all(x, axes, split_axis=0, concat_axis=0, tiled=True)


def shape_of(shape, dtype):
    return jax.ShapeDtypeStruct(shape, dtype)


def on_device(amp_fit, amp_cabs, coef, f12_weight, ints_fit, ints_cabs, shell_len, pair_blocks, pair_count):
    weight = jnp.tile(jnp.pad(f12_weight, (0, 32 - NI)), NC)[None, :]

    sent = pl.pallas_call(
        pack_amps,
        out_shape=shape_of((NO, ROWS, 256), BF16),
        in_specs=[ANY] * 3,
        out_specs=vmem(1)[0],
        scratch_shapes=[
            pltpu.VMEM((NJ, NF, NO * NI), BF16),
            pltpu.VMEM((NC, NI, NO * NI), BF16),
            pltpu.VMEM((NI, 3 * LANES), BF16),
            pltpu.VMEM((24 * NC, NO * NI), F32),
            pltpu.VMEM((256, NO * NI), BF16),
            pltpu.VMEM((ROWS, 256), F32),
            pltpu.VMEM((NI, LANES), F32),
            pltpu.SemaphoreType.DMA((3,)),
        ],
        compiler_params=room(60),
    )(jnp.transpose(amp_fit, (2, 0, 1)), jnp.transpose(amp_cabs, (0, 2, 1)), coef)
    amps = exchange(sent, "occ")

    sent = pl.pallas_call(
        partial_t,
        out_shape=shape_of((NA, TROWS + CROWS, LANES), BF16),
        in_specs=vmem(2) + [ANY] * 2,
        out_specs=vmem(1)[0],
        scratch_shapes=[
            pltpu.VMEM((TJ, 5 * LANES), BF16),
            pltpu.VMEM((TJ, 3 * LANES), BF16),
            pltpu.VMEM((NI * NF, 24 * LANES), BF16),
            pltpu.VMEM((NC, NI, 24 * LANES), BF16),
            pltpu.VMEM((32 * NC, 1024), BF16),
            pltpu.VMEM((CROWS, LANES), F32),
            pltpu.SemaphoreType.DMA((2, 3)),
        ],
        compiler_params=room(52),
    )(amps, weight, jnp.transpose(ints_fit, (1, 0, 2)).reshape(NI * NF, 24 * LANES), ints_cabs)
    shares = exchange(sent, "aux")

    sent = pl.pallas_call(
        sum_aux,
        out_shape=shape_of((TROWS + 16, LANES), F32),
        in_specs=[SMEM] + vmem(2),
        out_specs=vmem(1)[0],
        compiler_params=PARAMS,
    )(pair_count, pair_blocks.T, shares)
    sent = jnp.broadcast_to(sent.astype(F16)[None], (NP, TROWS + 16, LANES))
    got = exchange(sent, "pair").astype(F32)

    sent = pl.pallas_call(
        all_blocks,
        out_shape=shape_of((NO, 48, LANES), F32),
        in_specs=[SMEM] + vmem(2),
        out_specs=vmem(1)[0],
        scratch_shapes=[
            pltpu.VMEM((8 * NP, LANES), jnp.int32),
            pltpu.SMEM((8 * NP, LANES), jnp.int32),
            pltpu.VMEM((NP * TJ, 6 * LANES), BF16),
            pltpu.VMEM((3, 8 * LANES, LANES), F32),
            pltpu.VMEM((NO * 48, LANES), F32),
            pltpu.SemaphoreType.DMA,
        ],
        compiler_params=PARAMS,
    )(shell_len, got, shares)
    got = exchange(sent.astype(F16), "occ").astype(F32)

    sent = pl.pallas_call(
        sum_occ,
        out_shape=shape_of((NP * NA, 16, LANES), F32),
        in_specs=vmem(1),
        out_specs=vmem(1)[0],
        scratch_shapes=[pltpu.VMEM((40, LANES), F32)],
        compiler_params=PARAMS,
    )(got)
    got = exchange(sent, ("pair", "aux"))

    return pl.pallas_call(
        unpack,
        out_shape=shape_of((40, 8, LANES), F32),
        in_specs=vmem(1),
        out_specs=vmem(1)[0],
        scratch_shapes=[pltpu.VMEM((NA, 8, LANES), F32)],
        compiler_params=PARAMS,
    )(got)


def solution(mesh):
    placed = (
        P("aux", None, "occ"),
        P("aux", None, "occ"),
        P("occ", None),
        P("occ"),
        P("aux", "occ", None),
        P("aux", "occ", None),
        P(),
        P("pair", None),
        P("pair"),
    )
    return jax.shard_map(
        on_device, mesh=mesh, in_specs=placed, out_specs=P("pair", "occ", None), check_vma=False
    )
```

time: 118 us -> 109 us (0.924)
  waiting for transfers between devices: 31.9 us -> 25.6 us
  blocking collectives: 49.2 us -> 43.8 us
  Pallas kernels: 9.16 us -> 12.9 us
    all_to_all x2, waiting for transfers between devices: 31.9 us -> 25.6 us  [exchange(): return lax.all_to_all(x, axes, split_axis=0, concat_axis=0, tiled=True)]
    all_to_all x3, blocking collectives: 49.2 us -> 43.8 us  [exchange(): return lax.all_to_all(x, axes, split_axis=0, concat_axis=0, tiled=True)]
    pallas_call x4, Pallas kernels: 5.93 us -> 9.86 us  [the longest x1 5.57 us: on_device(): pl.pallas_call(partial_t, out_shape=shape_of((NA, TROWS + CROWS, LANES),...]
where the time goes in v3:
time: 109 us
  blocking collectives  43.8 us (40%)
  waiting for transfers between devices  25.6 us (23%)
  starting transfers between devices  24.9 us (23%)
  Pallas kernels  12.9 us (12%)
    all_to_all x3, blocking collectives, exchange(): return lax.all_to_all(x, axes, split_axis=0, concat_axis=0, tiled=True)  43.8 us
    all_to_all x2, waiting for transfers between devices, exchange(): return lax.all_to_all(x, axes, split_axis=0, concat_axis=0, tiled=True)  25.6 us
    all_to_all x2, starting transfers between devices, exchange(): return lax.all_to_all(x, axes, split_axis=0, concat_axis=0, tiled=True)  24.9 us
    pallas_call x1, Pallas kernels, on_device(): pl.pallas_call(partial_t, out_shape=shape_of((NA, TROWS + CROWS, LANES),...  5.57 us
    pallas_call x1, Pallas kernels, on_device(): pl.pallas_call(all_blocks, out_shape=shape_of((NO, 48, LANES), F32), in_s...  4.05 us
  transfers between devices with their start and end apart: 2, of which 2 were waited for; matrix products, arithmetic and copies ran while one was open for 1% of the time, Pallas kernels for 0%

profile of v3, /device:TPU:1, one launch (start us, length us, event | category | flops | bytes accessed | tf_op | source)
XLA Modules:
  0.0 108.8 jit_solution(15672083933630448472)
XLA Ops:
  0.0 2.1 %shard_map.91 = bf16[16,24,256]{2,1,0:T(8,128)(2,1)} custom-call(bf16[18,32,288]{2,1,0:T(8,128)(2,1)} %bitcast.8, bf16[12,18,288]{2,1,0:T(8,128)(2,1)} %bitcast.9, bf16[18,3072]{1,0:T(8,128)(2,1)} %coef_hbm.1), custom_call_target="tpu_custom_call" | custom-call | tf_op jit(solution)/shard_map/pallas_call | solution.py:306
  2.1 15.8 %all-to-all-start = ((bf16[16,24,256]{2,1,0:T(8,128)(2,1)}), bf16[16,24,256]{2,1,0:T(8,128)(2,1)S(1)}, u32[]{:S(2)}, u32[]{:S(2)}) async-start(bf16[16,24,256]{2,1,0:T(8,128)(2,1)} %shard_map.91), calls=%async_computation | async-start | bytes 393216 | tf_op jit(solution)/shard_map/all_to_all | solution.py:296
  17.9 0.7 pad.4
  18.5 0.1 broadcast_in_dim_tile.3.weight
  18.6 11.8 %all-to-all-done.got = bf16[16,24,256]{2,1,0:T(8,128)(2,1)S(1)} async-done(((bf16[16,24,256]{2,1,0:T(8,128)(2,1)}), bf16[16,24,256]{2,1,0:T(8,128)(2,1)S(1)}, u32[]{:S(2)}, u32[]{:S(2)}) %all-to-all-start) | async-done | bytes 196640 | tf_op jit(solution)/shard_map/all_to_all | solution.py:296
  30.4 0.0 copy-start
  30.4 5.6 %shard_map.92 = bf16[8,480,128]{2,1,0:T(8,128)(2,1)} custom-call(bf16[16,24,256]{2,1,0:T(8,128)(2,1)S(1)} %all-to-all-done.got, f32[1,384]{1,0:T(1,128)S(1)} %broadcast_in_dim_tile.3.weight, bf16[576,3072]{1,0:T(8,128)(2,1)} %bitcast.7, bf16[12,18,3072]{2,1,0:T(8,128)(2,1)} %cabs_hbm.1), custom_call_target="tpu_custom_call" | custom-call | tf_op jit(solution)/shard_map/pallas_call | solution.py:325
  36.0 0.0 copy-start.1
  36.0 9.1 %all-to-all-start.1 = ((bf16[8,480,128]{2,1,0:T(8,128)(2,1)}), bf16[8,480,128]{2,1,0:T(8,128)(2,1)S(1)}, u32[]{:S(2)}, u32[]{:S(2)}) async-start(bf16[8,480,128]{2,1,0:T(8,128)(2,1)} %shard_map.92), calls=%async_computation.1 | async-start | bytes 1966080 | tf_op jit(solution)/shard_map/all_to_all | solution.py:296
  45.8 13.7 %all-to-all-done.1.got.coefs = bf16[8,480,128]{2,1,0:T(8,128)(2,1)S(1)} async-done(((bf16[8,480,128]{2,1,0:T(8,128)(2,1)}), bf16[8,480,128]{2,1,0:T(8,128)(2,1)S(1)}, u32[]{:S(2)}, u32[]{:S(2)}) %all-to-all-start.1) | async-done | bytes 983072 | tf_op jit(solution)/shard_map/all_to_all | solution.py:296
  59.6 0.0 copy-done
  59.6 0.2 shard_map.93
  59.8 9.5 %all_to_all.25 = f16[4,256,128]{2,1,0:T(8,128)(2,1)S(1)} all-to-all(f16[4,256,128]{2,1,0:T(8,128)(2,1)S(1)} %broadcast_in_dim.2), channel_id=1, replica_groups=mesh['occ'=16,'aux'=8,'pair'=4] {'pair'}, dimensions={0} | all-to-all | bytes 524288 | tf_op jit(solution)/shard_map/all_to_all | solution.py:296
  69.4 0.0 copy-done.1
  69.4 4.0 %shard_map.94 = f32[16,48,128]{2,1,0:T(8,128)S(1)} custom-call(s32[24]{0:T(128)S(1)} %copy-done.1, f32[4,256,128]{2,1,0:T(8,128)S(1)} %convert_element_type.15.got, bf16[8,480,128]{2,1,0:T(8,128)(2,1)S(1)} %all-to-all-done.1.got.coefs), custom_call_target="tpu_custom_call" | custom-call | tf_op jit(solution)/shard_map/pallas_call | solution.py:353
  73.5 16.8 %all_to_all.26 = f16[16,48,128]{2,1,0:T(8,128)(2,1)S(1)} all-to-all(f16[16,48,128]{2,1,0:T(8,128)(2,1)S(1)} %convert_element_type.16), channel_id=1, replica_groups=mesh['occ'=16,'aux'=8,'pair'=4] {'occ'}, dimensions={0} | all-to-all | bytes 393216 | tf_op jit(solution)/shard_map/all_to_all | solution.py:296
  90.3 0.1 shard_map.95
  90.4 17.5 %all_to_all.27.got = f32[32,16,128]{2,1,0:T(8,128)S(1)} all-to-all(f32[32,16,128]{2,1,0:T(8,128)S(1)} %shard_map.95), channel_id=1, replica_groups=mesh['occ'=16,'aux'=8,'pair'=4] {'pair','aux'}, dimensions={0} | all-to-all | bytes 524288 | tf_op jit(solution)/shard_map/all_to_all | solution.py:296
  107.8 1.0 shard_map.96
  (6 shorter events, 0.1 us)
Async XLA Ops:
  2.1 28.3 %all-to-all-start = ((bf16[16,24,256]{2,1,0:T(8,128)(2,1)}), bf16[16,24,256]{2,1,0:T(8,128)(2,1)S(1)}, u32[]{:S(2)}, u32[]{:S(2)}) async-start(bf16[16,24,256]{2,1,0:T(8,128)(2,1)} %shard_map.91), calls=%async_computation | async-start | bytes 393216 | tf_op jit(solution)/shard_map/all_to_all | solution.py:296
  30.4 29.1 %copy-start = (s32[40,2]{0,1:T(2,128)S(1)}, s32[40,2]{0,1:T(2,128)}, u32[]{:S(2)}) copy-start(s32[40,2]{0,1:T(2,128)} %param.16) | copy-start | bytes 964
  36.0 33.4 %copy-start.1 = (s32[24]{0:T(128)S(1)}, s32[24]{0:T(128)}, u32[]{:S(2)}) copy-start(s32[24]{0:T(128)} %lens.1) | copy-start | bytes 292
  36.0 23.5 %all-to-all-start.1 = ((bf16[8,480,128]{2,1,0:T(8,128)(2,1)}), bf16[8,480,128]{2,1,0:T(8,128)(2,1)S(1)}, u32[]{:S(2)}, u32[]{:S(2)}) async-start(bf16[8,480,128]{2,1,0:T(8,128)(2,1)} %shard_map.92), calls=%async_computation.1 | async-start | bytes 1966080 | tf_op jit(solution)/shard_map/all_to_all | solution.py:296

commit v4 on v3

--- a/solution.py
+++ b/solution.py
@@ -60,6 +60,7 @@
 NO, NI, NA, NP, NF, NC, NJ = 16, 18, 8, 4, 32, 12, 5
 CQ = 16
 TJ = NO * NJ
+GROUP = 8 * LANES
 TROWS = 3 * TJ
 ROWS = 24
 CROWS = 240
@@ -106,19 +107,19 @@
     out[...] = (dot(place, x[...], NT).reshape(NO, ROWS, 256) + extra[...][None]).astype(BF16)
 
 
-def partial_t(got, weight, fit_hbm, cabs_hbm, out, a_fit, a_cab, fit, cabs, padded, own, sems):
-    spans = [pl.ds(1024 * g, 1024) for g in range(3)]
-    copies = [
-        (
-            pltpu.make_async_copy(cabs_hbm.at[:, :, s], cabs.at[:, :, s], sems.at[0, g]),
-            pltpu.make_async_copy(fit_hbm.at[:, s], fit.at[:, s], sems.at[1, g]),
-        )
-        for g, s in enumerate(spans)
-    ]
-    for pair in copies:
-        for c in pair:
-            c.start()
-    padded[...] = jnp.zeros(padded.shape, BF16)
+def join_cabs(cabs_hbm, out, cabs, sem):
+    copy = pltpu.make_async_copy(cabs_hbm, cabs, sem)
+    copy.start()
+    copy.wait()
+    for q in range(NC):
+        out[NI * q : NI * (q + 1), :] = cabs[q]
+
+
+def partial_t(got, weight, cabs, fit_hbm, out, a_fit, a_cab, own, fit, sems):
+    spans = [pl.ds(GROUP * g, GROUP) for g in range(3)]
+    copies = [pltpu.make_async_copy(fit_hbm.at[:, s], fit.at[:, s], sems.at[g]) for g, s in enumerate(spans)]
+    for c in copies:
+        c.start()
     messages = got[...].reshape(NO * ROWS, 256)
     shape = (NI, NO, NO * ROWS)
     pick = jnp.where(iota(shape, 2) == ROWS * iota(shape, 1) + iota(shape, 0), 1.0, 0.0)
@@ -142,11 +143,11 @@
 
     lay(NF, 0, a_fit)
     lay(CQ, NJ * NF, a_cab)
-    shape = (3 * LANES, 32 * NC)
-    source = iota(shape, 0)
-    target = iota(shape, 1)
-    order = one_hot(((target >> 5) == (source & 15)) & ((target & 31) == (source >> 4)))
-    a_cab[...] = (dot(a_cab[...], order) * weight[...]).astype(BF16)
+    shape = (3 * LANES, 2 * LANES)
+    source, target = iota(shape, 0), iota(shape, 1)
+    q = (target * 3641) >> 16
+    order = one_hot((q == (source & 15)) & (target - NI * q == (source >> 4)))
+    a_cab[:, : 2 * LANES] = (dot(a_cab[...], order) * weight[...]).astype(BF16)
 
     shape = (NO * NI, NO * ROWS)
     row, source = iota(shape, 0), iota(shape, 1)
@@ -175,11 +176,8 @@
         out[p, TROWS:, :] = packed
 
     for g in range(3):
-        for c in copies[g]:
-            c.wait()
-        for q in range(NC):
-            padded[32 * q : 32 * q + NI, :] = cabs[q, :, spans[g]]
-        total = dot(a_fit[:, : NI * NF], fit[:, spans[g]]) + dot(a_cab[...], padded[...])
+        copies[g].wait()
+        total = dot(a_fit[:, : NI * NF], fit[:, spans[g]]) + dot(a_cab[:, : NI * NC], cabs[:, spans[g]])
         pieces = swap_pieces([total[:, LANES * k : LANES * (k + 1)] for k in range(8)], 16)
         for k in range(8):
             out[k, TJ * g : TJ * (g + 1), :] = pieces[k].astype(BF16)
@@ -274,20 +272,26 @@
 
 
 def sum_occ(got, out, total):
-    total[...] = sum(got[o, 0:40, :] * unscale(got[o, 40:41, :]) for o in range(NO))
+    blocks = sum(got[o, 0:40, :] * unscale(got[o, 40:41, :]) for o in range(NO))
+    power, factor = scale_of(jnp.abs(blocks))
+    total[...] = blocks * factor
+    rest = jnp.where(iota((6, LANES), 0) == 0, power, 0.0)
     for y in range(NP):
         rows = total[10 * y : 10 * (y + 1), :]
         for p in range(NA):
             out[NA * y + p, 0:10, :] = rows
-            out[NA * y + p, 10:16, :] = jnp.zeros((6, LANES), F32)
+            out[NA * y + p, 10:16, :] = rest
 
 
 def unpack(got, out, rows):
+    for y in range(NP):
+        for p in range(NA):
+            part = got[NA * y + p]
+            part = part * unscale(part[10:11, :])
+            for q in range(5):
+                rows[q, p, 2 * y : 2 * y + 2, :] = part[2 * q : 2 * q + 2, :]
     for q in range(5):
-        for p in range(NA):
-            for y in range(NP):
-                rows[p, 2 * y : 2 * y + 2, :] = got[NA * y + p, 2 * q : 2 * q + 2, :]
-        blocks = swap_pieces([rows[p] for p in range(NA)], 16)
+        blocks = swap_pieces([rows[q, p] for p in range(NA)], 16)
         for k in range(8):
             out[8 * q + k] = blocks[k]
 
@@ -301,7 +305,7 @@
 
 
 def on_device(amp_fit, amp_cabs, coef, f12_weight, ints_fit, ints_cabs, shell_len, pair_blocks, pair_count):
-    weight = jnp.tile(jnp.pad(f12_weight, (0, 32 - NI)), NC)[None, :]
+    weight = jnp.pad(jnp.tile(f12_weight, NC), (0, 2 * LANES - NI * NC))[None, :]
 
     sent = pl.pallas_call(
         pack_amps,
@@ -322,22 +326,29 @@
     )(jnp.transpose(amp_fit, (2, 0, 1)), jnp.transpose(amp_cabs, (0, 2, 1)), coef)
     amps = exchange(sent, "occ")
 
+    cabs = pl.pallas_call(
+        join_cabs,
+        out_shape=shape_of((NC * NI, 24 * LANES), BF16),
+        in_specs=[ANY],
+        out_specs=vmem(1)[0],
+        scratch_shapes=[pltpu.VMEM((NC, NI, 24 * LANES), BF16), pltpu.SemaphoreType.DMA],
+        compiler_params=room(51),
+        cost_estimate=pl.CostEstimate(flops=0, bytes_accessed=5_000_000, transcendentals=0),
+    )(ints_cabs)
     sent = pl.pallas_call(
         partial_t,
         out_shape=shape_of((NA, TROWS + CROWS, LANES), BF16),
-        in_specs=vmem(2) + [ANY] * 2,
+        in_specs=vmem(3) + [ANY],
         out_specs=vmem(1)[0],
         scratch_shapes=[
             pltpu.VMEM((TJ, 5 * LANES), BF16),
             pltpu.VMEM((TJ, 3 * LANES), BF16),
+            pltpu.VMEM((CROWS, LANES), F32),
             pltpu.VMEM((NI * NF, 24 * LANES), BF16),
-            pltpu.VMEM((NC, NI, 24 * LANES), BF16),
-            pltpu.VMEM((32 * NC, 1024), BF16),
-            pltpu.VMEM((CROWS, LANES), F32),
-            pltpu.SemaphoreType.DMA((2, 3)),
+            pltpu.SemaphoreType.DMA((3,)),
         ],
-        compiler_params=room(52),
-    )(amps, weight, jnp.transpose(ints_fit, (1, 0, 2)).reshape(NI * NF, 24 * LANES), ints_cabs)
+        compiler_params=room(51),
+    )(amps, weight, cabs, jnp.transpose(ints_fit, (1, 0, 2)).reshape(NI * NF, 24 * LANES))
     shares = exchange(sent, "aux")
 
     sent = pl.pallas_call(
@@ -375,14 +386,14 @@
         scratch_shapes=[pltpu.VMEM((40, LANES), F32)],
         compiler_params=PARAMS,
     )(got)
-    got = exchange(sent, ("pair", "aux"))
+    got = exchange(sent.astype(F16), ("pair", "aux")).astype(F32)
 
     return pl.pallas_call(
         unpack,
         out_shape=shape_of((40, 8, LANES), F32),
         in_specs=vmem(1),
         out_specs=vmem(1)[0],
-        scratch_shapes=[pltpu.VMEM((NA, 8, LANES), F32)],
+        scratch_shapes=[pltpu.VMEM((5, NA, 8, LANES), F32)],
         compiler_params=PARAMS,
     )(got)
 

time: 109 us -> 108 us (level)
  Pallas kernels: 12.9 us -> 14.2 us
  blocking collectives: 43.8 us -> 42.5 us
  waiting for transfers between devices: 25.6 us -> 24.5 us
    pallas_call x0 -> x1, Pallas kernels: none -> 1.65 us  [on_device(): pl.pallas_call(join_cabs, out_shape=shape_of((NC * NI, 24 * LANES), BF16)...]
    all_to_all x3, blocking collectives: 43.8 us -> 42.5 us  [exchange(): return lax.all_to_all(x, axes, split_axis=0, concat_axis=0, tiled=True)]
  transfers between devices with their start and end apart: 2 -> 2, of which waited for: 2 -> 2; matrix products, arithmetic and copies ran while one was open for 1% -> 0% of each run, Pallas kernels for 0% -> 2%
where the time goes in v4:
time: 108 us; the launch traced here: 107 us
  blocking collectives  42.5 us (39%)
  starting transfers between devices  24.9 us (23%)
  waiting for transfers between devices  24.5 us (23%)
  Pallas kernels  14.2 us (13%)
    all_to_all x3, blocking collectives, exchange(): return lax.all_to_all(x, axes, split_axis=0, concat_axis=0, tiled=True)  42.5 us
    all_to_all x2, starting transfers between devices, exchange(): return lax.all_to_all(x, axes, split_axis=0, concat_axis=0, tiled=True)  24.9 us
    all_to_all x2, waiting for transfers between devices, exchange(): return lax.all_to_all(x, axes, split_axis=0, concat_axis=0, tiled=True)  24.5 us
    pallas_call x1, Pallas kernels, on_device(): pl.pallas_call(partial_t, out_shape=shape_of((NA, TROWS + CROWS, LANES),...  5.07 us
    pallas_call x1, Pallas kernels, on_device(): pl.pallas_call(all_blocks, out_shape=shape_of((NO, 48, LANES), F32), in_s...  4.04 us
  transfers between devices with their start and end apart: 2, of which 2 were waited for; matrix products, arithmetic and copies ran while one was open for 0% of the time, Pallas kernels for 2%

profile of v4, /device:TPU:1, one launch (start us, length us, event | category | flops | bytes accessed | tf_op | source)
XLA Modules:
  0.0 107.2 jit_solution(4689810745972470995)
XLA Ops:
  0.0 2.1 %shard_map.91 = bf16[16,24,256]{2,1,0:T(8,128)(2,1)} custom-call(bf16[18,32,288]{2,1,0:T(8,128)(2,1)} %bitcast.10, bf16[12,18,288]{2,1,0:T(8,128)(2,1)} %bitcast.11, bf16[18,3072]{1,0:T(8,128)(2,1)} %coef_hbm.1), custom_call_target="tpu_custom_call" | custom-call | tf_op jit(solution)/shard_map/pallas_call | solution.py:310
  2.1 0.0 copy-start.2
  2.1 15.8 %all-to-all-start = ((bf16[16,24,256]{2,1,0:T(8,128)(2,1)}), bf16[16,24,256]{2,1,0:T(8,128)(2,1)S(1)}, u32[]{:S(2)}, u32[]{:S(2)}) async-start(bf16[16,24,256]{2,1,0:T(8,128)(2,1)} %shard_map.91), calls=%async_computation | async-start | bytes 393216 | tf_op jit(solution)/shard_map/all_to_all | solution.py:300
  17.9 1.7 %shard_map.92.cabs = bf16[216,3072]{1,0:T(8,128)(2,1)S(1)} custom-call(bf16[12,18,3072]{2,1,0:T(8,128)(2,1)} %cabs_hbm.1), custom_call_target="tpu_custom_call" | custom-call | bytes 5000000 | tf_op jit(solution)/shard_map/pallas_call | solution.py:329
  19.5 0.0 copy-done.2
  19.6 0.1 tile.10
  19.7 10.8 %all-to-all-done.got = bf16[16,24,256]{2,1,0:T(8,128)(2,1)S(1)} async-done(((bf16[16,24,256]{2,1,0:T(8,128)(2,1)}), bf16[16,24,256]{2,1,0:T(8,128)(2,1)S(1)}, u32[]{:S(2)}, u32[]{:S(2)}) %all-to-all-start) | async-done | bytes 196640 | tf_op jit(solution)/shard_map/all_to_all | solution.py:300
  30.4 5.1 %shard_map.93 = bf16[8,480,128]{2,1,0:T(8,128)(2,1)} custom-call(bf16[16,24,256]{2,1,0:T(8,128)(2,1)S(1)} %all-to-all-done.got, f32[1,256]{1,0:T(1,128)S(1)} %bitcast.7, bf16[216,3072]{1,0:T(8,128)(2,1)S(1)} %shard_map.92.cabs, bf16[576,3072]{1,0:T(8,128)(2,1)} %bitcast.9), custom_call_target="tpu_custom_call" | custom-call | tf_op jit(solution)/shard_map/pallas_call | solution.py:338
  35.5 0.0 copy-start
  35.5 9.1 %all-to-all-start.1 = ((bf16[8,480,128]{2,1,0:T(8,128)(2,1)}), bf16[8,480,128]{2,1,0:T(8,128)(2,1)S(1)}, u32[]{:S(2)}, u32[]{:S(2)}) async-start(bf16[8,480,128]{2,1,0:T(8,128)(2,1)} %shard_map.93), calls=%async_computation.1 | async-start | bytes 1966080 | tf_op jit(solution)/shard_map/all_to_all | solution.py:300
  44.7 0.0 copy-start.1
  45.3 13.7 %all-to-all-done.1.got.coefs = bf16[8,480,128]{2,1,0:T(8,128)(2,1)S(1)} async-done(((bf16[8,480,128]{2,1,0:T(8,128)(2,1)}), bf16[8,480,128]{2,1,0:T(8,128)(2,1)S(1)}, u32[]{:S(2)}, u32[]{:S(2)}) %all-to-all-start.1) | async-done | bytes 983072 | tf_op jit(solution)/shard_map/all_to_all | solution.py:300
  59.1 0.0 copy-done
  59.1 0.2 shard_map.94
  59.3 9.5 %all_to_all.25 = f16[4,256,128]{2,1,0:T(8,128)(2,1)S(1)} all-to-all(f16[4,256,128]{2,1,0:T(8,128)(2,1)S(1)} %broadcast_in_dim.10), channel_id=1, replica_groups=mesh['occ'=16,'aux'=8,'pair'=4] {'pair'}, dimensions={0} | all-to-all | bytes 524288 | tf_op jit(solution)/shard_map/all_to_all | solution.py:300
  68.9 0.0 copy-done.1
  68.9 4.0 %shard_map.95 = f32[16,48,128]{2,1,0:T(8,128)S(1)} custom-call(s32[24]{0:T(128)S(1)} %copy-done.1, f32[4,256,128]{2,1,0:T(8,128)S(1)} %convert_element_type.21.got, bf16[8,480,128]{2,1,0:T(8,128)(2,1)S(1)} %all-to-all-done.1.got.coefs), custom_call_target="tpu_custom_call" | custom-call | tf_op jit(solution)/shard_map/pallas_call | solution.py:364
  73.0 16.8 %all_to_all.26 = f16[16,48,128]{2,1,0:T(8,128)(2,1)S(1)} all-to-all(f16[16,48,128]{2,1,0:T(8,128)(2,1)S(1)} %convert_element_type.22), channel_id=1, replica_groups=mesh['occ'=16,'aux'=8,'pair'=4] {'occ'}, dimensions={0} | all-to-all | bytes 393216 | tf_op jit(solution)/shard_map/all_to_all | solution.py:300
  89.8 0.2 shard_map.96
  90.0 16.2 %all_to_all.27 = f16[32,16,128]{2,1,0:T(8,128)(2,1)S(1)} all-to-all(f16[32,16,128]{2,1,0:T(8,128)(2,1)S(1)} %convert_element_type.24), channel_id=1, replica_groups=mesh['occ'=16,'aux'=8,'pair'=4] {'pair','aux'}, dimensions={0} | all-to-all | bytes 262144 | tf_op jit(solution)/shard_map/all_to_all | solution.py:300
  106.2 1.0 shard_map.97
  (9 shorter events, 0.2 us)
Async XLA Ops:
  2.1 17.4 %copy-start.2 = (f32[18]{0:T(128)S(1)}, f32[18]{0:T(128)}, u32[]{:S(2)}) copy-start(f32[18]{0:T(128)} %param.12) | copy-start | bytes 220
  2.1 28.3 %all-to-all-start = ((bf16[16,24,256]{2,1,0:T(8,128)(2,1)}), bf16[16,24,256]{2,1,0:T(8,128)(2,1)S(1)}, u32[]{:S(2)}, u32[]{:S(2)}) async-start(bf16[16,24,256]{2,1,0:T(8,128)(2,1)} %shard_map.91), calls=%async_computation | async-start | bytes 393216 | tf_op jit(solution)/shard_map/all_to_all | solution.py:300
  35.5 23.6 %copy-start = (s32[40,2]{0,1:T(2,128)S(1)}, s32[40,2]{0,1:T(2,128)}, u32[]{:S(2)}) copy-start(s32[40,2]{0,1:T(2,128)} %param.16) | copy-start | bytes 964
  35.5 23.5 %all-to-all-start.1 = ((bf16[8,480,128]{2,1,0:T(8,128)(2,1)}), bf16[8,480,128]{2,1,0:T(8,128)(2,1)S(1)}, u32[]{:S(2)}, u32[]{:S(2)}) async-start(bf16[8,480,128]{2,1,0:T(8,128)(2,1)} %shard_map.93), calls=%async_computation.1 | async-start | bytes 1966080 | tf_op jit(solution)/shard_map/all_to_all | solution.py:300
  44.7 24.2 %copy-start.1 = (s32[24]{0:T(128)S(1)}, s32[24]{0:T(128)}, u32[]{:S(2)}) copy-start(s32[24]{0:T(128)} %lens.1) | copy-start | bytes 292

commit v5 on v4

--- a/solution.py
+++ b/solution.py
@@ -149,31 +149,32 @@
     order = one_hot((q == (source & 15)) & (target - NI * q == (source >> 4)))
     a_cab[:, : 2 * LANES] = (dot(a_cab[...], order) * weight[...]).astype(BF16)
 
-    shape = (NO * NI, NO * ROWS)
-    row, source = iota(shape, 0), iota(shape, 1)
-    occ = (row * 3641) >> 16
-    rest = row - NI * occ
-    sixth = rest - jnp.where(rest >= 12, 12, jnp.where(rest >= 6, 6, 0))
-    base = source - ROWS * occ - sixth
-    main = dot(one_hot(base == 18), messages)
-    spare0 = dot(one_hot(base == 0), messages[:, LANES:])
-    spare1 = dot(one_hot(base == 6), messages[:, LANES:])
-    shape = (NO * NI, LANES)
-    lane, row = iota(shape, 1), iota(shape, 0)
-    rest = row - NI * ((row * 3641) >> 16)
-    third = jnp.where(lane < 32, pltpu.roll(main[:, :LANES], 32, 1), pltpu.roll(main[:, LANES:], 64, 1))
-    third = jnp.where(lane < 64, third, pltpu.roll(spare0, 80, 1))
-    third = jnp.where(lane < 80, third, pltpu.roll(spare1, 96, 1))
-    coef = jnp.where(rest < 6, main[:, :LANES], jnp.where(rest < 12, main[:, LANES:], third))
-    last = coef[TROWS:]
-    lane = iota((48, LANES), 1)
-    for b in range(3):
-        own[TJ * b : TJ * (b + 1), :] = coef[TJ * b : TJ * (b + 1)]
-        moved = pltpu.roll(last, 96 - 32 * b, 1)
-        own[TJ * b : TJ * b + 48, :] = jnp.where(lane < 96, coef[TJ * b : TJ * b + 48], moved)
-    packed = own[...].astype(BF16)
-    for p in range(NA):
-        out[p, TROWS:, :] = packed
+    def pack_coefficients():
+        shape = (NO * NI, NO * ROWS)
+        row, source = iota(shape, 0), iota(shape, 1)
+        occ = (row * 3641) >> 16
+        rest = row - NI * occ
+        sixth = rest - jnp.where(rest >= 12, 12, jnp.where(rest >= 6, 6, 0))
+        base = source - ROWS * occ - sixth
+        main = dot(one_hot(base == 18), messages)
+        spare0 = dot(one_hot(base == 0), messages[:, LANES:])
+        spare1 = dot(one_hot(base == 6), messages[:, LANES:])
+        shape = (NO * NI, LANES)
+        lane, row = iota(shape, 1), iota(shape, 0)
+        rest = row - NI * ((row * 3641) >> 16)
+        third = jnp.where(lane < 32, pltpu.roll(main[:, :LANES], 32, 1), pltpu.roll(main[:, LANES:], 64, 1))
+        third = jnp.where(lane < 64, third, pltpu.roll(spare0, 80, 1))
+        third = jnp.where(lane < 80, third, pltpu.roll(spare1, 96, 1))
+        coef = jnp.where(rest < 6, main[:, :LANES], jnp.where(rest < 12, main[:, LANES:], third))
+        last = coef[TROWS:]
+        lane = iota((48, LANES), 1)
+        for b in range(3):
+            own[TJ * b : TJ * (b + 1), :] = coef[TJ * b : TJ * (b + 1)]
+            moved = pltpu.roll(last, 96 - 32 * b, 1)
+            own[TJ * b : TJ * b + 48, :] = jnp.where(lane < 96, coef[TJ * b : TJ * b + 48], moved)
+        packed = own[...].astype(BF16)
+        for p in range(NA):
+            out[p, TROWS:, :] = packed
 
     for g in range(3):
         copies[g].wait()
@@ -181,6 +182,8 @@
         pieces = swap_pieces([total[:, LANES * k : LANES * (k + 1)] for k in range(8)], 16)
         for k in range(8):
             out[k, TJ * g : TJ * (g + 1), :] = pieces[k].astype(BF16)
+        if g == 0:
+            pack_coefficients()
 
 
 def scale_of(top):
@@ -241,7 +244,8 @@
         last = jnp.where(lane >= 64, pltpu.roll(rows[2][:48], 96, 1), last)
         coef = jnp.concatenate(rows + [last], axis=0)
         coef = jnp.where(kept, coef, 0.0).astype(BF16)
-        blocks = dot(coef, ordered[:, : 3 * LANES], TN) + dot(coef, ordered[:, 3 * LANES :], TN)
+        blocks = dot(coef, ordered, TN)
+        blocks = blocks[:, : 3 * LANES] + blocks[:, 3 * LANES :]
         for g in range(3):
             dmat[g, LANES * p : LANES * (p + 1), :] = blocks[:, LANES * g : LANES * (g + 1)]
 
@@ -347,7 +351,7 @@
             pltpu.VMEM((NI * NF, 24 * LANES), BF16),
             pltpu.SemaphoreType.DMA((3,)),
         ],
-        compiler_params=room(51),
+        compiler_params=room(49),
     )(amps, weight, cabs, jnp.transpose(ints_fit, (1, 0, 2)).reshape(NI * NF, 24 * LANES))
     shares = exchange(sent, "aux")
 

time: 108 us -> 107 us (level)
  no operation moved by 1% of the time
where the time goes in v5:
time: 107 us; the launch traced here: 106 us
  blocking collectives  42.5 us (40%)
  starting transfers between devices  24.9 us (23%)
  waiting for transfers between devices  24.5 us (23%)
  Pallas kernels  13.5 us (13%)
    all_to_all x3, blocking collectives, exchange(): return lax.all_to_all(x, axes, split_axis=0, concat_axis=0, tiled=True)  42.5 us
    all_to_all x2, starting transfers between devices, exchange(): return lax.all_to_all(x, axes, split_axis=0, concat_axis=0, tiled=True)  24.9 us
    all_to_all x2, waiting for transfers between devices, exchange(): return lax.all_to_all(x, axes, split_axis=0, concat_axis=0, tiled=True)  24.5 us
    pallas_call x1, Pallas kernels, on_device(): pl.pallas_call(partial_t, out_shape=shape_of((NA, TROWS + CROWS, LANES),...  4.5 us
    pallas_call x1, Pallas kernels, on_device(): pl.pallas_call(all_blocks, out_shape=shape_of((NO, 48, LANES), F32), in_s...  3.88 us
  transfers between devices with their start and end apart: 2, of which 2 were waited for; matrix products, arithmetic and copies ran while one was open for 0% of the time, Pallas kernels for 2%

profile of v5, /device:TPU:1, one launch (start us, length us, event | category | flops | bytes accessed | tf_op | source)
XLA Modules:
  0.0 106.5 jit_solution(9795492390481015299)
XLA Ops:
  0.0 2.1 %shard_map.91 = bf16[16,24,256]{2,1,0:T(8,128)(2,1)} custom-call(bf16[18,32,288]{2,1,0:T(8,128)(2,1)} %bitcast.10, bf16[12,18,288]{2,1,0:T(8,128)(2,1)} %bitcast.11, bf16[18,3072]{1,0:T(8,128)(2,1)} %coef_hbm.1), custom_call_target="tpu_custom_call" | custom-call | tf_op jit(solution)/shard_map/pallas_call | solution.py:314
  2.1 0.0 copy-start.2
  2.1 15.8 %all-to-all-start = ((bf16[16,24,256]{2,1,0:T(8,128)(2,1)}), bf16[16,24,256]{2,1,0:T(8,128)(2,1)S(1)}, u32[]{:S(2)}, u32[]{:S(2)}) async-start(bf16[16,24,256]{2,1,0:T(8,128)(2,1)} %shard_map.91), calls=%async_computation | async-start | bytes 393216 | tf_op jit(solution)/shard_map/all_to_all | solution.py:304
  17.9 1.7 %shard_map.92.cabs = bf16[216,3072]{1,0:T(8,128)(2,1)S(1)} custom-call(bf16[12,18,3072]{2,1,0:T(8,128)(2,1)} %cabs_hbm.1), custom_call_target="tpu_custom_call" | custom-call | bytes 5000000 | tf_op jit(solution)/shard_map/pallas_call | solution.py:333
  19.5 0.0 copy-done.2
  19.6 0.1 tile.10
  19.7 10.8 %all-to-all-done.got = bf16[16,24,256]{2,1,0:T(8,128)(2,1)S(1)} async-done(((bf16[16,24,256]{2,1,0:T(8,128)(2,1)}), bf16[16,24,256]{2,1,0:T(8,128)(2,1)S(1)}, u32[]{:S(2)}, u32[]{:S(2)}) %all-to-all-start) | async-done | bytes 196640 | tf_op jit(solution)/shard_map/all_to_all | solution.py:304
  30.4 4.5 %shard_map.93 = bf16[8,480,128]{2,1,0:T(8,128)(2,1)} custom-call(bf16[16,24,256]{2,1,0:T(8,128)(2,1)S(1)} %all-to-all-done.got, f32[1,256]{1,0:T(1,128)S(1)} %bitcast.7, bf16[216,3072]{1,0:T(8,128)(2,1)S(1)} %shard_map.92.cabs, bf16[576,3072]{1,0:T(8,128)(2,1)} %bitcast.9), custom_call_target="tpu_custom_call" | custom-call | tf_op jit(solution)/shard_map/pallas_call | solution.py:342
  34.9 0.0 copy-start
  35.0 9.1 %all-to-all-start.1 = ((bf16[8,480,128]{2,1,0:T(8,128)(2,1)}), bf16[8,480,128]{2,1,0:T(8,128)(2,1)S(1)}, u32[]{:S(2)}, u32[]{:S(2)}) async-start(bf16[8,480,128]{2,1,0:T(8,128)(2,1)} %shard_map.93), calls=%async_computation.1 | async-start | bytes 1966080 | tf_op jit(solution)/shard_map/all_to_all | solution.py:304
  44.1 0.0 copy-start.1
  44.8 13.7 %all-to-all-done.1.got.coefs = bf16[8,480,128]{2,1,0:T(8,128)(2,1)S(1)} async-done(((bf16[8,480,128]{2,1,0:T(8,128)(2,1)}), bf16[8,480,128]{2,1,0:T(8,128)(2,1)S(1)}, u32[]{:S(2)}, u32[]{:S(2)}) %all-to-all-start.1) | async-done | bytes 983072 | tf_op jit(solution)/shard_map/all_to_all | solution.py:304
  58.5 0.0 copy-done
  58.5 0.2 shard_map.94
  58.8 9.5 %all_to_all.25 = f16[4,256,128]{2,1,0:T(8,128)(2,1)S(1)} all-to-all(f16[4,256,128]{2,1,0:T(8,128)(2,1)S(1)} %broadcast_in_dim.10), channel_id=1, replica_groups=mesh['occ'=16,'aux'=8,'pair'=4] {'pair'}, dimensions={0} | all-to-all | bytes 524288 | tf_op jit(solution)/shard_map/all_to_all | solution.py:304
  68.3 0.0 copy-done.1
  68.3 3.9 %shard_map.95 = f32[16,48,128]{2,1,0:T(8,128)S(1)} custom-call(s32[24]{0:T(128)S(1)} %copy-done.1, f32[4,256,128]{2,1,0:T(8,128)S(1)} %convert_element_type.21.got, bf16[8,480,128]{2,1,0:T(8,128)(2,1)S(1)} %all-to-all-done.1.got.coefs), custom_call_target="tpu_custom_call" | custom-call | tf_op jit(solution)/shard_map/pallas_call | solution.py:368
  72.3 16.8 %all_to_all.26 = f16[16,48,128]{2,1,0:T(8,128)(2,1)S(1)} all-to-all(f16[16,48,128]{2,1,0:T(8,128)(2,1)S(1)} %convert_element_type.22), channel_id=1, replica_groups=mesh['occ'=16,'aux'=8,'pair'=4] {'occ'}, dimensions={0} | all-to-all | bytes 393216 | tf_op jit(solution)/shard_map/all_to_all | solution.py:304
  89.1 0.2 shard_map.96
  89.3 16.2 %all_to_all.27 = f16[32,16,128]{2,1,0:T(8,128)(2,1)S(1)} all-to-all(f16[32,16,128]{2,1,0:T(8,128)(2,1)S(1)} %convert_element_type.24), channel_id=1, replica_groups=mesh['occ'=16,'aux'=8,'pair'=4] {'pair','aux'}, dimensions={0} | all-to-all | bytes 262144 | tf_op jit(solution)/shard_map/all_to_all | solution.py:304
  105.5 1.0 shard_map.97
  (9 shorter events, 0.2 us)
Async XLA Ops:
  2.1 17.4 %copy-start.2 = (f32[18]{0:T(128)S(1)}, f32[18]{0:T(128)}, u32[]{:S(2)}) copy-start(f32[18]{0:T(128)} %param.12) | copy-start | bytes 220
  2.1 28.3 %all-to-all-start = ((bf16[16,24,256]{2,1,0:T(8,128)(2,1)}), bf16[16,24,256]{2,1,0:T(8,128)(2,1)S(1)}, u32[]{:S(2)}, u32[]{:S(2)}) async-start(bf16[16,24,256]{2,1,0:T(8,128)(2,1)} %shard_map.91), calls=%async_computation | async-start | bytes 393216 | tf_op jit(solution)/shard_map/all_to_all | solution.py:304
  34.9 23.5 %copy-start = (s32[40,2]{0,1:T(2,128)S(1)}, s32[40,2]{0,1:T(2,128)}, u32[]{:S(2)}) copy-start(s32[40,2]{0,1:T(2,128)} %param.16) | copy-start | bytes 964
  35.0 23.5 %all-to-all-start.1 = ((bf16[8,480,128]{2,1,0:T(8,128)(2,1)}), bf16[8,480,128]{2,1,0:T(8,128)(2,1)S(1)}, u32[]{:S(2)}, u32[]{:S(2)}) async-start(bf16[8,480,128]{2,1,0:T(8,128)(2,1)} %shard_map.93), calls=%async_computation.1 | async-start | bytes 1966080 | tf_op jit(solution)/shard_map/all_to_all | solution.py:304
  44.1 24.2 %copy-start.1 = (s32[24]{0:T(128)S(1)}, s32[24]{0:T(128)}, u32[]{:S(2)}) copy-start(s32[24]{0:T(128)} %lens.1) | copy-start | bytes 292

commit v6 on v5

--- a/solution.py
+++ b/solution.py
@@ -107,9 +107,12 @@
     out[...] = (dot(place, x[...], NT).reshape(NO, ROWS, 256) + extra[...][None]).astype(BF16)
 
 
-def join_cabs(cabs_hbm, out, cabs, sem):
+def join_cabs(counts, pairs, cabs_hbm, out, slots, cabs, sem):
     copy = pltpu.make_async_copy(cabs_hbm, cabs, sem)
     copy.start()
+    slots[...] = jnp.zeros(slots.shape, F32)
+    slots[1:3, 0:40] = pairs[...].astype(F32)
+    slots[3:4, :] = jnp.broadcast_to(counts[0].astype(F32), (1, LANES))
     copy.wait()
     for q in range(NC):
         out[NI * q : NI * (q + 1), :] = cabs[q]
@@ -196,14 +199,12 @@
     return jnp.exp(power * LN2) * (1.0 / 16384.0)
 
 
-def sum_aux(counts, pairs, got, out):
+def sum_aux(slots, got, out):
     total = jnp.sum(got[:, 0:TROWS, :].astype(F32), axis=0)
     power, factor = scale_of(jnp.abs(total))
     out[0:TROWS, :] = total * factor
-    out[TROWS:, :] = jnp.zeros((16, LANES), F32)
-    out[TROWS : TROWS + 1, :] = jnp.broadcast_to(power, (1, LANES))
-    out[TROWS + 1 : TROWS + 3, 0:40] = pairs[...].astype(F32)
-    out[TROWS + 3 : TROWS + 4, :] = jnp.broadcast_to(counts[0].astype(F32), (1, LANES))
+    out[TROWS : TROWS + 8, :] = jnp.where(iota((8, LANES), 0) == 0, power, slots[...])
+    out[TROWS + 8 :, :] = jnp.zeros((8, LANES), F32)
 
 
 def all_blocks(lens, got, coefs, out, ints, words, tmat, dmat, msg, sem):
@@ -330,15 +331,15 @@
     )(jnp.transpose(amp_fit, (2, 0, 1)), jnp.transpose(amp_cabs, (0, 2, 1)), coef)
     amps = exchange(sent, "occ")
 
-    cabs = pl.pallas_call(
+    cabs, slots = pl.pallas_call(
         join_cabs,
-        out_shape=shape_of((NC * NI, 24 * LANES), BF16),
-        in_specs=[ANY],
-        out_specs=vmem(1)[0],
+        out_shape=[shape_of((NC * NI, 24 * LANES), BF16), shape_of((8, LANES), F32)],
+        in_specs=[SMEM] + vmem(1) + [ANY],
+        out_specs=vmem(2),
         scratch_shapes=[pltpu.VMEM((NC, NI, 24 * LANES), BF16), pltpu.SemaphoreType.DMA],
         compiler_params=room(51),
         cost_estimate=pl.CostEstimate(flops=0, bytes_accessed=5_000_000, transcendentals=0),
-    )(ints_cabs)
+    )(pair_count, pair_blocks.T, ints_cabs)
     sent = pl.pallas_call(
         partial_t,
         out_shape=shape_of((NA, TROWS + CROWS, LANES), BF16),
@@ -358,10 +359,10 @@
     sent = pl.pallas_call(
         sum_aux,
         out_shape=shape_of((TROWS + 16, LANES), F32),
-        in_specs=[SMEM] + vmem(2),
+        in_specs=vmem(2),
         out_specs=vmem(1)[0],
         compiler_params=PARAMS,
-    )(pair_count, pair_blocks.T, shares)
+    )(slots, shares)
     sent = jnp.broadcast_to(sent.astype(F16)[None], (NP, TROWS + 16, LANES))
     got = exchange(sent, "pair").astype(F32)
 

time: 107 us -> 106 us (level)
  blocking collectives: 42.5 us -> 65.9 us
  waiting for transfers between devices: 24.5 us -> 8.81 us
  starting transfers between devices: 24.9 us -> 15.8 us
  local copies, waits for them, and re-layouts: 0.14 us -> 1.46 us
    all_to_all x3 -> x4, blocking collectives: 42.5 us -> 65.9 us  [exchange(): return lax.all_to_all(x, axes, split_axis=0, concat_axis=0, tiled=True)]
    all_to_all x2 -> x1, waiting for transfers between devices: 24.5 us -> 8.81 us  [exchange(): return lax.all_to_all(x, axes, split_axis=0, concat_axis=0, tiled=True)]
    all_to_all x2 -> x1, starting transfers between devices: 24.9 us -> 15.8 us  [exchange(): return lax.all_to_all(x, axes, split_axis=0, concat_axis=0, tiled=True)]
  transfers between devices with their start and end apart: 2 -> 1, of which waited for: 2 -> 1; matrix products, arithmetic and copies ran while one was open for 0% -> 1% of each run, Pallas kernels for 2% -> 2%
where the time goes in v6:
time: 106 us; the launch traced here: 105 us
  blocking collectives  65.9 us (62%)
  starting transfers between devices  15.8 us (15%)
  Pallas kernels  12.5 us (12%)
  waiting for transfers between devices  8.81 us (8%)
  local copies, waits for them, and re-layouts  1.46 us (1%)
    all_to_all x4, blocking collectives, exchange(): return lax.all_to_all(x, axes, split_axis=0, concat_axis=0, tiled=True)  65.9 us
    all_to_all x1, starting transfers between devices, exchange(): return lax.all_to_all(x, axes, split_axis=0, concat_axis=0, tiled=True)  15.8 us
    all_to_all x1, waiting for transfers between devices, exchange(): return lax.all_to_all(x, axes, split_axis=0, concat_axis=0, tiled=True)  8.81 us
    pallas_call x1, Pallas kernels, on_device(): pl.pallas_call(all_blocks, out_shape=shape_of((NO, 48, LANES), F32), in_s...  3.88 us
    pallas_call x1, Pallas kernels, on_device(): pl.pallas_call(partial_t, out_shape=shape_of((NA, TROWS + CROWS, LANES),...  3.53 us
  transfers between devices with their start and end apart: 1, of which 1 were waited for; matrix products, arithmetic and copies ran while one was open for 1% of the time, Pallas kernels for 2%

profile of v6, /device:TPU:1, one launch (start us, length us, event | category | flops | bytes accessed | tf_op | source)
XLA Modules:
  0.0 105.3 jit_solution(13375892767328588641)
XLA Ops:
  0.0 2.1 %shard_map.92 = bf16[16,24,256]{2,1,0:T(8,128)(2,1)} custom-call(bf16[18,32,288]{2,1,0:T(8,128)(2,1)} %bitcast.10, bf16[12,18,288]{2,1,0:T(8,128)(2,1)} %bitcast.11, bf16[18,3072]{1,0:T(8,128)(2,1)} %coef_hbm.1), custom_call_target="tpu_custom_call" | custom-call | tf_op jit(solution)/shard_map/pallas_call | solution.py:315
  2.1 15.8 %all-to-all-start = ((bf16[16,24,256]{2,1,0:T(8,128)(2,1)}), bf16[16,24,256]{2,1,0:T(8,128)(2,1)S(1)}, u32[]{:S(2)}, u32[]{:S(2)}) async-start(bf16[16,24,256]{2,1,0:T(8,128)(2,1)} %shard_map.92), calls=%async_computation | async-start | bytes 393216 | tf_op jit(solution)/shard_map/all_to_all | solution.py:305
  18.5 0.7 tile.4
  19.2 0.1 tile.10
  19.3 0.0 copy-start
  19.3 0.7 copy-done
  20.0 1.7 %shard_map.91 = (bf16[216,3072]{1,0:T(8,128)(2,1)S(1)}, f32[8,128]{1,0:T(8,128)S(1)}) custom-call(s32[1]{0:T(128)S(6)} %copy.10.counts, s32[2,40]{1,0:T(2,128)S(1)} %bitcast.8, bf16[12,18,3072]{2,1,0:T(8,128)(2,1)} %cabs_hbm.1), custom_call_target="tpu_custom_call" | custom-call | bytes 5000000 | tf_op jit(solution)/shard_map/pallas_call | solution.py:334
  21.6 8.8 %all-to-all-done.got = bf16[16,24,256]{2,1,0:T(8,128)(2,1)S(1)} async-done(((bf16[16,24,256]{2,1,0:T(8,128)(2,1)}), bf16[16,24,256]{2,1,0:T(8,128)(2,1)S(1)}, u32[]{:S(2)}, u32[]{:S(2)}) %all-to-all-start) | async-done | bytes 196640 | tf_op jit(solution)/shard_map/all_to_all | solution.py:305
  30.4 3.5 %shard_map.93 = bf16[8,480,128]{2,1,0:T(8,128)(2,1)S(1)} custom-call(bf16[16,24,256]{2,1,0:T(8,128)(2,1)S(1)} %all-to-all-done.got, f32[1,256]{1,0:T(1,128)S(1)} %bitcast.7, bf16[216,3072]{1,0:T(8,128)(2,1)S(1)} %get-tuple-element.8.cabs, bf16[576,3072]{1,0:T(8,128)(2,1)} %bitcast.9), custom_call_target="tpu_custom_call" | custom-call | tf_op jit(solution)/shard_map/pallas_call | solution.py:343
  34.0 23.4 %all_to_all.25.got.coefs = bf16[8,480,128]{2,1,0:T(8,128)(2,1)S(1)} all-to-all(bf16[8,480,128]{2,1,0:T(8,128)(2,1)S(1)} %shard_map.93), channel_id=1, replica_groups=mesh['occ'=16,'aux'=8,'pair'=4] {'aux'}, dimensions={0} | all-to-all | bytes 1966080 | tf_op jit(solution)/shard_map/all_to_all | solution.py:305
  57.4 0.0 copy-start.1
  57.4 0.2 shard_map.94
  57.6 9.5 %all_to_all.26 = f16[4,256,128]{2,1,0:T(8,128)(2,1)S(1)} all-to-all(f16[4,256,128]{2,1,0:T(8,128)(2,1)S(1)} %broadcast_in_dim.10), channel_id=1, replica_groups=mesh['occ'=16,'aux'=8,'pair'=4] {'pair'}, dimensions={0} | all-to-all | bytes 524288 | tf_op jit(solution)/shard_map/all_to_all | solution.py:305
  67.2 0.0 copy-done.1
  67.2 3.9 %shard_map.95 = f32[16,48,128]{2,1,0:T(8,128)S(1)} custom-call(s32[24]{0:T(128)S(1)} %copy-done.1, f32[4,256,128]{2,1,0:T(8,128)S(1)} %convert_element_type.21.got, bf16[8,480,128]{2,1,0:T(8,128)(2,1)S(1)} %all_to_all.25.got.coefs), custom_call_target="tpu_custom_call" | custom-call | tf_op jit(solution)/shard_map/pallas_call | solution.py:369
  71.1 16.8 %all_to_all.27 = f16[16,48,128]{2,1,0:T(8,128)(2,1)S(1)} all-to-all(f16[16,48,128]{2,1,0:T(8,128)(2,1)S(1)} %convert_element_type.22), channel_id=1, replica_groups=mesh['occ'=16,'aux'=8,'pair'=4] {'occ'}, dimensions={0} | all-to-all | bytes 393216 | tf_op jit(solution)/shard_map/all_to_all | solution.py:305
  87.9 0.2 shard_map.96
  88.1 16.2 %all_to_all.28 = f16[32,16,128]{2,1,0:T(8,128)(2,1)S(1)} all-to-all(f16[32,16,128]{2,1,0:T(8,128)(2,1)S(1)} %convert_element_type.24), channel_id=1, replica_groups=mesh['occ'=16,'aux'=8,'pair'=4] {'pair','aux'}, dimensions={0} | all-to-all | bytes 262144 | tf_op jit(solution)/shard_map/all_to_all | solution.py:305
  104.3 1.0 shard_map.97
  (8 shorter events, 0.2 us)
Async XLA Ops:
  2.1 28.3 %all-to-all-start = ((bf16[16,24,256]{2,1,0:T(8,128)(2,1)}), bf16[16,24,256]{2,1,0:T(8,128)(2,1)S(1)}, u32[]{:S(2)}, u32[]{:S(2)}) async-start(bf16[16,24,256]{2,1,0:T(8,128)(2,1)} %shard_map.92), calls=%async_computation | async-start | bytes 393216 | tf_op jit(solution)/shard_map/all_to_all | solution.py:305
  19.3 0.7 copy-start
  57.4 9.8 %copy-start.1 = (s32[24]{0:T(128)S(1)}, s32[24]{0:T(128)}, u32[]{:S(2)}) copy-start(s32[24]{0:T(128)} %lens.1) | copy-start | bytes 292

commit v7 on v6

--- a/solution.py
+++ b/solution.py
@@ -59,21 +59,28 @@
 
 NO, NI, NA, NP, NF, NC, NJ = 16, 18, 8, 4, 32, 12, 5
 CQ = 16
-TJ = NO * NJ
+TJ = 72
 GROUP = 8 * LANES
 TROWS = 3 * TJ
 ROWS = 24
-CROWS = 240
+CROWS = 216
+SROWS = 3 * (TJ + 8) + 192
+
+
+def first_column(occ, pair):
+    return (9 * pair + 1 - (occ & 1)) >> 1
 
 
 def pack_amps(fit_hbm, cabs_hbm, coef_hbm, out, fit, cabs, coef, cab32, x, extra, piece, sems):
     aux, pair = lax.axis_index("aux"), lax.axis_index("pair")
-    first_j = jnp.minimum(NJ * pair, NI - NJ)
+    first_j = first_column(lax.axis_index("occ"), pair)
+    fifth_j = jnp.minimum(first_j + 4, NI - 1)
     columns = pl.ds(pl.multiple_of(3 * LANES * aux, LANES), 3 * LANES)
     copies = [
         pltpu.make_async_copy(cabs_hbm, cabs, sems.at[0]),
-        pltpu.make_async_copy(fit_hbm.at[pl.ds(first_j, NJ)], fit, sems.at[1]),
-        pltpu.make_async_copy(coef_hbm.at[:, columns], coef, sems.at[2]),
+        pltpu.make_async_copy(fit_hbm.at[pl.ds(first_j, 4)], fit.at[pl.ds(0, 4)], sems.at[1]),
+        pltpu.make_async_copy(fit_hbm.at[pl.ds(fifth_j, 1)], fit.at[pl.ds(4, 1)], sems.at[2]),
+        pltpu.make_async_copy(coef_hbm.at[:, columns], coef, sems.at[3]),
     ]
     for c in copies:
         c.start()
@@ -90,7 +97,8 @@
         cab32[24 * q : 24 * q + NI, :] = cabs[q].astype(F32)
     zero = jnp.zeros((CQ - NC, NO * NI), F32)
     for jj in range(NJ):
-        picked = [cab32[pl.ds(24 * q + first_j + jj, 1), :] for q in range(NC)]
+        j = fifth_j if jj == 4 else first_j + jj
+        picked = [cab32[pl.ds(24 * q + j, 1), :] for q in range(NC)]
         rows = jnp.concatenate(picked + [zero], axis=0)
         x[NJ * NF + CQ * jj : NJ * NF + CQ * (jj + 1), :] = rows.astype(BF16)
     x[NJ * (NF + CQ) :, :] = jnp.zeros((256 - NJ * (NF + CQ), NO * NI), BF16)
@@ -124,25 +132,33 @@
     for c in copies:
         c.start()
     messages = got[...].reshape(NO * ROWS, 256)
-    shape = (NI, NO, NO * ROWS)
-    pick = jnp.where(iota(shape, 2) == ROWS * iota(shape, 1) + iota(shape, 0), 1.0, 0.0)
-    pick = pick.reshape(NI * NO, NO * ROWS).astype(BF16)
-    amps = dot(pick, messages)
-    amps = [[amps[NO * t : NO * (t + 1), LANES * h : LANES * (h + 1)] for h in (0, 1)] for t in range(NI)]
-    lane = iota((NO, LANES), 1)
+    first = lax.axis_index("pair") & 1
+
+    def picked(step, start):
+        count = NO // step
+        shape = (NI, count, NO * ROWS)
+        pick = iota(shape, 2) == ROWS * (step * iota(shape, 1) + start) + iota(shape, 0)
+        pick = jnp.where(pick, 1.0, 0.0).reshape(NI * count, NO * ROWS).astype(BF16)
+        rows = dot(pick, messages)
+        return [[rows[count * t : count * (t + 1), LANES * h : LANES * (h + 1)] for h in (0, 1)] for t in range(NI)]
+
+    amps, fifth = picked(1, 0), picked(2, first)
 
     def lay(width, start, store):
         per = LANES // width
         for jj in range(NJ):
+            tiles = amps if jj < 4 else fifth
+            count = tiles[0][0].shape[0]
+            lane = iota((count, LANES), 1)
             half, off = divmod(start + width * jj, LANES)
             for m in range(-(-NI // per)):
-                tile = jnp.zeros((NO, LANES), F32)
+                tile = jnp.zeros((count, LANES), F32)
                 for k in range(min(per, NI - m * per)):
-                    moved = amps[m * per + k][half]
+                    moved = tiles[m * per + k][half]
                     if (width * k - off) % LANES:
                         moved = pltpu.roll(moved, (width * k - off) % LANES, 1)
                     tile = jnp.where((lane >= width * k) & (lane < width * (k + 1)), moved, tile)
-                store[NO * jj : NO * (jj + 1), LANES * m : LANES * (m + 1)] = tile.astype(BF16)
+                store[NO * jj : NO * jj + count, LANES * m : LANES * (m + 1)] = tile.astype(BF16)
 
     lay(NF, 0, a_fit)
     lay(CQ, NJ * NF, a_cab)
@@ -169,24 +185,23 @@
         third = jnp.where(lane < 64, third, pltpu.roll(spare0, 80, 1))
         third = jnp.where(lane < 80, third, pltpu.roll(spare1, 96, 1))
         coef = jnp.where(rest < 6, main[:, :LANES], jnp.where(rest < 12, main[:, LANES:], third))
-        last = coef[TROWS:]
-        lane = iota((48, LANES), 1)
+        last = coef[3 * TJ :]
+        lane = iota((TJ, LANES), 1)
         for b in range(3):
-            own[TJ * b : TJ * (b + 1), :] = coef[TJ * b : TJ * (b + 1)]
             moved = pltpu.roll(last, 96 - 32 * b, 1)
-            own[TJ * b : TJ * b + 48, :] = jnp.where(lane < 96, coef[TJ * b : TJ * b + 48], moved)
-        packed = own[...].astype(BF16)
+            own[TJ * b : TJ * (b + 1), :] = jnp.where(lane < 96, coef[TJ * b : TJ * (b + 1)], moved)
+        packed = own[0:192, :].astype(BF16)
         for p in range(NA):
-            out[p, TROWS:, :] = packed
-
+            out[p, SROWS - 192 :, :] = packed
+
+    pack_coefficients()
     for g in range(3):
         copies[g].wait()
         total = dot(a_fit[:, : NI * NF], fit[:, spans[g]]) + dot(a_cab[:, : NI * NC], cabs[:, spans[g]])
         pieces = swap_pieces([total[:, LANES * k : LANES * (k + 1)] for k in range(8)], 16)
         for k in range(8):
-            out[k, TJ * g : TJ * (g + 1), :] = pieces[k].astype(BF16)
-        if g == 0:
-            pack_coefficients()
+            rows = jnp.concatenate([pieces[k], own[192 + 8 * g : 200 + 8 * g, :]], axis=0)
+            out[k, (TJ + 8) * g : (TJ + 8) * (g + 1), :] = rows.astype(BF16)
 
 
 def scale_of(top):
@@ -200,11 +215,11 @@
 
 
 def sum_aux(slots, got, out):
-    total = jnp.sum(got[:, 0:TROWS, :].astype(F32), axis=0)
+    total = jnp.sum(got[:, 0 : 3 * (TJ + 8), :].astype(F32), axis=0)
+    total = jnp.concatenate([total[(TJ + 8) * g : (TJ + 8) * g + TJ] for g in range(3)], axis=0)
     power, factor = scale_of(jnp.abs(total))
     out[0:TROWS, :] = total * factor
-    out[TROWS : TROWS + 8, :] = jnp.where(iota((8, LANES), 0) == 0, power, slots[...])
-    out[TROWS + 8 :, :] = jnp.zeros((8, LANES), F32)
+    out[TROWS:, :] = jnp.where(iota((8, LANES), 0) == 0, power, slots[...])
 
 
 def all_blocks(lens, got, coefs, out, ints, words, tmat, dmat, msg, sem):
@@ -223,26 +238,30 @@
         for y in range(NP):
             part = got[y, TJ * g : TJ * (g + 1), :] * unscale(got[y, TROWS : TROWS + 1, :])
             part = jnp.where(kept, part, 0.0)
-            high = part.astype(BF16)
+            high = part.astype(BF16).astype(F32)
             tmat[TJ * y : TJ * (y + 1), LANES * g : LANES * (g + 1)] = high
-            low = (part - high.astype(F32)).astype(BF16)
-            tmat[TJ * y : TJ * (y + 1), LANES * (g + 3) : LANES * (g + 4)] = low
-    shape = (NP, NJ, NO, NO * NI)
-    y, jj = iota(shape, 0), iota(shape, 1)
-    j = jnp.minimum(NJ * y, NI - NJ) + jj
-    pick = (iota(shape, 3) == NI * iota(shape, 2) + j) & (j >= NJ * y)
-    pick = jnp.where(pick, 1.0, 0.0).reshape(NP * TJ, NO * NI).astype(BF16)
-    ordered = dot(pick, tmat[...], TN).astype(BF16)
+            tmat[TJ * y : TJ * (y + 1), LANES * (g + 3) : LANES * (g + 4)] = part - high
+    shape = (NP, TJ, NO * NI)
+    y, row = iota(shape, 0), iota(shape, 1)
+    fifth = row >= 4 * NO
+    occ = jnp.where(fifth, 2 * (row - 4 * NO) + (y & 1), row & (NO - 1))
+    j = first_column(occ, y) + jnp.where(fifth, 4, row >> 4)
+    pick = jnp.where(iota(shape, 2) == NI * occ + j, 1.0, 0.0)
+    pick = pick.reshape(NP * TJ, NO * NI).astype(BF16)
+    ordered = dot(pick, tmat[...].astype(BF16), TN).astype(BF16)
 
     for p in range(NA):
         limit = jnp.zeros((1, LANES), jnp.int32)
         for k in range(3):
             limit = jnp.where((lane >> 5) == k, lens[3 * p + k], limit)
         kept = 8 * (lane & 15) + 2 * pair + ((lane >> 4) & 1) < limit
-        rows = [coefs[p, TROWS + TJ * b : TROWS + TJ * (b + 1), :].astype(F32) for b in range(3)]
-        last = pltpu.roll(rows[0][:48], 32, 1)
-        last = jnp.where(lane >= 32, pltpu.roll(rows[1][:48], 64, 1), last)
-        last = jnp.where(lane >= 64, pltpu.roll(rows[2][:48], 96, 1), last)
+        packed = coefs[p].astype(F32)
+        spare = [packed[(TJ + 8) * g + TJ : (TJ + 8) * (g + 1)] for g in range(3)]
+        packed = jnp.concatenate([packed[SROWS - 192 :]] + spare, axis=0)
+        rows = [packed[TJ * b : TJ * (b + 1)] for b in range(3)]
+        last = pltpu.roll(rows[0], 32, 1)
+        last = jnp.where(lane >= 32, pltpu.roll(rows[1], 64, 1), last)
+        last = jnp.where(lane >= 64, pltpu.roll(rows[2], 96, 1), last)
         coef = jnp.concatenate(rows + [last], axis=0)
         coef = jnp.where(kept, coef, 0.0).astype(BF16)
         blocks = dot(coef, ordered, TN)
@@ -325,7 +344,7 @@
             pltpu.VMEM((256, NO * NI), BF16),
             pltpu.VMEM((ROWS, 256), F32),
             pltpu.VMEM((NI, LANES), F32),
-            pltpu.SemaphoreType.DMA((3,)),
+            pltpu.SemaphoreType.DMA((4,)),
         ],
         compiler_params=room(60),
     )(jnp.transpose(amp_fit, (2, 0, 1)), jnp.transpose(amp_cabs, (0, 2, 1)), coef)
@@ -342,7 +361,7 @@
     )(pair_count, pair_blocks.T, ints_cabs)
     sent = pl.pallas_call(
         partial_t,
-        out_shape=shape_of((NA, TROWS + CROWS, LANES), BF16),
+        out_shape=shape_of((NA, SROWS, LANES), BF16),
         in_specs=vmem(3) + [ANY],
         out_specs=vmem(1)[0],
         scratch_shapes=[
@@ -358,12 +377,12 @@
 
     sent = pl.pallas_call(
         sum_aux,
-        out_shape=shape_of((TROWS + 16, LANES), F32),
+        out_shape=shape_of((TROWS + 8, LANES), F32),
         in_specs=vmem(2),
         out_specs=vmem(1)[0],
         compiler_params=PARAMS,
     )(slots, shares)
-    sent = jnp.broadcast_to(sent.astype(F16)[None], (NP, TROWS + 16, LANES))
+    sent = jnp.broadcast_to(sent.astype(F16)[None], (NP, TROWS + 8, LANES))
     got = exchange(sent, "pair").astype(F32)
 
     sent = pl.pallas_call(
@@ -374,7 +393,7 @@
         scratch_shapes=[
             pltpu.VMEM((8 * NP, LANES), jnp.int32),
             pltpu.SMEM((8 * NP, LANES), jnp.int32),
-            pltpu.VMEM((NP * TJ, 6 * LANES), BF16),
+            pltpu.VMEM((NP * TJ, 6 * LANES), F32),
             pltpu.VMEM((3, 8 * LANES, LANES), F32),
             pltpu.VMEM((NO * 48, LANES), F32),
             pltpu.SemaphoreType.DMA,

time: 106 us -> 105 us (level)
  blocking collectives: 65.9 us -> 64.8 us
where the time goes in v7:
time: 105 us
  blocking collectives  64.8 us (62%)
  starting transfers between devices  15.8 us (15%)
  Pallas kernels  13 us (12%)
  waiting for transfers between devices  8.81 us (8%)
  local copies, waits for them, and re-layouts  1.46 us (1%)
    all_to_all x4, blocking collectives, exchange(): return lax.all_to_all(x, axes, split_axis=0, concat_axis=0, tiled=True)  64.8 us
    all_to_all x1, starting transfers between devices, exchange(): return lax.all_to_all(x, axes, split_axis=0, concat_axis=0, tiled=True)  15.8 us
    all_to_all x1, waiting for transfers between devices, exchange(): return lax.all_to_all(x, axes, split_axis=0, concat_axis=0, tiled=True)  8.81 us
    pallas_call x1, Pallas kernels, on_device(): pl.pallas_call(partial_t, out_shape=shape_of((NA, SROWS, LANES), BF16), i...  4.09 us
    pallas_call x1, Pallas kernels, on_device(): pl.pallas_call(all_blocks, out_shape=shape_of((NO, 48, LANES), F32), in_s...  3.84 us
  transfers between devices with their start and end apart: 1, of which 1 were waited for; matrix products, arithmetic and copies ran while one was open for 1% of the time, Pallas kernels for 2%

profile of v7, /device:TPU:1, one launch (start us, length us, event | category | flops | bytes accessed | tf_op | source)
XLA Modules:
  0.0 104.8 jit_solution(12669801253834998870)
XLA Ops:
  0.0 2.1 %shard_map.92 = bf16[16,24,256]{2,1,0:T(8,128)(2,1)} custom-call(bf16[18,32,288]{2,1,0:T(8,128)(2,1)} %bitcast.10, bf16[12,18,288]{2,1,0:T(8,128)(2,1)} %bitcast.11, bf16[18,3072]{1,0:T(8,128)(2,1)} %coef_hbm.1), custom_call_target="tpu_custom_call" | custom-call | tf_op jit(solution)/shard_map/pallas_call | solution.py:334
  2.1 15.8 %all-to-all-start = ((bf16[16,24,256]{2,1,0:T(8,128)(2,1)}), bf16[16,24,256]{2,1,0:T(8,128)(2,1)S(1)}, u32[]{:S(2)}, u32[]{:S(2)}) async-start(bf16[16,24,256]{2,1,0:T(8,128)(2,1)} %shard_map.92), calls=%async_computation | async-start | bytes 393216 | tf_op jit(solution)/shard_map/all_to_all | solution.py:324
  18.5 0.7 tile.4
  19.2 0.1 tile.10
  19.3 0.0 copy-start
  19.3 0.7 copy-done
  20.0 1.7 %shard_map.91 = (bf16[216,3072]{1,0:T(8,128)(2,1)S(1)}, f32[8,128]{1,0:T(8,128)S(1)}) custom-call(s32[1]{0:T(128)S(6)} %copy.10.counts, s32[2,40]{1,0:T(2,128)S(1)} %bitcast.8, bf16[12,18,3072]{2,1,0:T(8,128)(2,1)} %cabs_hbm.1), custom_call_target="tpu_custom_call" | custom-call | bytes 5000000 | tf_op jit(solution)/shard_map/pallas_call | solution.py:353
  21.6 8.8 %all-to-all-done.got = bf16[16,24,256]{2,1,0:T(8,128)(2,1)S(1)} async-done(((bf16[16,24,256]{2,1,0:T(8,128)(2,1)}), bf16[16,24,256]{2,1,0:T(8,128)(2,1)S(1)}, u32[]{:S(2)}, u32[]{:S(2)}) %all-to-all-start) | async-done | bytes 196640 | tf_op jit(solution)/shard_map/all_to_all | solution.py:324
  30.4 4.1 %shard_map.93 = bf16[8,432,128]{2,1,0:T(8,128)(2,1)S(1)} custom-call(bf16[16,24,256]{2,1,0:T(8,128)(2,1)S(1)} %all-to-all-done.got, f32[1,256]{1,0:T(1,128)S(1)} %bitcast.7, bf16[216,3072]{1,0:T(8,128)(2,1)S(1)} %get-tuple-element.8.cabs, bf16[576,3072]{1,0:T(8,128)(2,1)} %bitcast.9), custom_call_target="tpu_custom_call" | custom-call | tf_op jit(solution)/shard_map/pallas_call | solution.py:362
  34.5 0.0 copy-start.1
  34.5 22.4 %all_to_all.25.got.coefs = bf16[8,432,128]{2,1,0:T(8,128)(2,1)S(1)} all-to-all(bf16[8,432,128]{2,1,0:T(8,128)(2,1)S(1)} %shard_map.93), channel_id=1, replica_groups=mesh['occ'=16,'aux'=8,'pair'=4] {'aux'}, dimensions={0} | all-to-all | bytes 1769472 | tf_op jit(solution)/shard_map/all_to_all | solution.py:324
  57.0 0.2 shard_map.94
  57.2 9.3 %all_to_all.26 = f16[4,224,128]{2,1,0:T(8,128)(2,1)S(1)} all-to-all(f16[4,224,128]{2,1,0:T(8,128)(2,1)S(1)} %broadcast_in_dim.10), channel_id=1, replica_groups=mesh['occ'=16,'aux'=8,'pair'=4] {'pair'}, dimensions={0} | all-to-all | bytes 458752 | tf_op jit(solution)/shard_map/all_to_all | solution.py:324
  66.6 0.0 copy-done.1
  66.6 3.8 %shard_map.95 = f32[16,48,128]{2,1,0:T(8,128)S(1)} custom-call(s32[24]{0:T(128)S(1)} %copy-done.1, f32[4,224,128]{2,1,0:T(8,128)S(1)} %convert_element_type.21.got, bf16[8,432,128]{2,1,0:T(8,128)(2,1)S(1)} %all_to_all.25.got.coefs), custom_call_target="tpu_custom_call" | custom-call | tf_op jit(solution)/shard_map/pallas_call | solution.py:388
  70.5 16.8 %all_to_all.27 = f16[16,48,128]{2,1,0:T(8,128)(2,1)S(1)} all-to-all(f16[16,48,128]{2,1,0:T(8,128)(2,1)S(1)} %convert_element_type.22), channel_id=1, replica_groups=mesh['occ'=16,'aux'=8,'pair'=4] {'occ'}, dimensions={0} | all-to-all | bytes 393216 | tf_op jit(solution)/shard_map/all_to_all | solution.py:324
  87.3 0.2 shard_map.96
  87.5 16.3 %all_to_all.28 = f16[32,16,128]{2,1,0:T(8,128)(2,1)S(1)} all-to-all(f16[32,16,128]{2,1,0:T(8,128)(2,1)S(1)} %convert_element_type.24), channel_id=1, replica_groups=mesh['occ'=16,'aux'=8,'pair'=4] {'pair','aux'}, dimensions={0} | all-to-all | bytes 262144 | tf_op jit(solution)/shard_map/all_to_all | solution.py:324
  103.8 1.0 shard_map.97
  (8 shorter events, 0.2 us)
Async XLA Ops:
  2.1 28.3 %all-to-all-start = ((bf16[16,24,256]{2,1,0:T(8,128)(2,1)}), bf16[16,24,256]{2,1,0:T(8,128)(2,1)S(1)}, u32[]{:S(2)}, u32[]{:S(2)}) async-start(bf16[16,24,256]{2,1,0:T(8,128)(2,1)} %shard_map.92), calls=%async_computation | async-start | bytes 393216 | tf_op jit(solution)/shard_map/all_to_all | solution.py:324
  19.3 0.7 copy-start
  34.5 32.0 %copy-start.1 = (s32[24]{0:T(128)S(1)}, s32[24]{0:T(128)}, u32[]{:S(2)}) copy-start(s32[24]{0:T(128)} %lens.1) | copy-start | bytes 292

commit v8 on v7

--- a/solution.py
+++ b/solution.py
@@ -194,10 +194,11 @@
         for p in range(NA):
             out[p, SROWS - 192 :, :] = packed
 
-    pack_coefficients()
     for g in range(3):
         copies[g].wait()
         total = dot(a_fit[:, : NI * NF], fit[:, spans[g]]) + dot(a_cab[:, : NI * NC], cabs[:, spans[g]])
+        if g == 0:
+            pack_coefficients()
         pieces = swap_pieces([total[:, LANES * k : LANES * (k + 1)] for k in range(8)], 16)
         for k in range(8):
             rows = jnp.concatenate([pieces[k], own[192 + 8 * g : 200 + 8 * g, :]], axis=0)

time: 105 us -> 105 us (level)
  no operation moved by 1% of the time
where the time goes in v8:
time: 105 us; the launch traced here: 104 us
  blocking collectives  64.8 us (62%)
  starting transfers between devices  15.8 us (15%)
  Pallas kernels  12.5 us (12%)
  waiting for transfers between devices  8.81 us (8%)
  local copies, waits for them, and re-layouts  1.46 us (1%)
    all_to_all x4, blocking collectives, exchange(): return lax.all_to_all(x, axes, split_axis=0, concat_axis=0, tiled=True)  64.8 us
    all_to_all x1, starting transfers between devices, exchange(): return lax.all_to_all(x, axes, split_axis=0, concat_axis=0, tiled=True)  15.8 us
    all_to_all x1, waiting for transfers between devices, exchange(): return lax.all_to_all(x, axes, split_axis=0, concat_axis=0, tiled=True)  8.81 us
    pallas_call x1, Pallas kernels, on_device(): pl.pallas_call(all_blocks, out_shape=shape_of((NO, 48, LANES), F32), in_s...  3.84 us
    pallas_call x1, Pallas kernels, on_device(): pl.pallas_call(partial_t, out_shape=shape_of((NA, SROWS, LANES), BF16), i...  3.59 us
  transfers between devices with their start and end apart: 1, of which 1 were waited for; matrix products, arithmetic and copies ran while one was open for 1% of the time, Pallas kernels for 2%

profile of v8, /device:TPU:1, one launch (start us, length us, event | category | flops | bytes accessed | tf_op | source)
XLA Modules:
  0.0 104.3 jit_solution(2291988539900280339)
XLA Ops:
  0.0 2.1 %shard_map.92 = bf16[16,24,256]{2,1,0:T(8,128)(2,1)} custom-call(bf16[18,32,288]{2,1,0:T(8,128)(2,1)} %bitcast.10, bf16[12,18,288]{2,1,0:T(8,128)(2,1)} %bitcast.11, bf16[18,3072]{1,0:T(8,128)(2,1)} %coef_hbm.1), custom_call_target="tpu_custom_call" | custom-call | tf_op jit(solution)/shard_map/pallas_call | solution.py:335
  2.1 15.8 %all-to-all-start = ((bf16[16,24,256]{2,1,0:T(8,128)(2,1)}), bf16[16,24,256]{2,1,0:T(8,128)(2,1)S(1)}, u32[]{:S(2)}, u32[]{:S(2)}) async-start(bf16[16,24,256]{2,1,0:T(8,128)(2,1)} %shard_map.92), calls=%async_computation | async-start | bytes 393216 | tf_op jit(solution)/shard_map/all_to_all | solution.py:325
  18.5 0.7 tile.4
  19.2 0.1 tile.10
  19.3 0.0 copy-start
  19.3 0.7 copy-done
  20.0 1.7 %shard_map.91 = (bf16[216,3072]{1,0:T(8,128)(2,1)S(1)}, f32[8,128]{1,0:T(8,128)S(1)}) custom-call(s32[1]{0:T(128)S(6)} %copy.10.counts, s32[2,40]{1,0:T(2,128)S(1)} %bitcast.8, bf16[12,18,3072]{2,1,0:T(8,128)(2,1)} %cabs_hbm.1), custom_call_target="tpu_custom_call" | custom-call | bytes 5000000 | tf_op jit(solution)/shard_map/pallas_call | solution.py:354
  21.6 8.8 %all-to-all-done.got = bf16[16,24,256]{2,1,0:T(8,128)(2,1)S(1)} async-done(((bf16[16,24,256]{2,1,0:T(8,128)(2,1)}), bf16[16,24,256]{2,1,0:T(8,128)(2,1)S(1)}, u32[]{:S(2)}, u32[]{:S(2)}) %all-to-all-start) | async-done | bytes 196640 | tf_op jit(solution)/shard_map/all_to_all | solution.py:325
  30.4 3.6 %shard_map.93 = bf16[8,432,128]{2,1,0:T(8,128)(2,1)S(1)} custom-call(bf16[16,24,256]{2,1,0:T(8,128)(2,1)S(1)} %all-to-all-done.got, f32[1,256]{1,0:T(1,128)S(1)} %bitcast.7, bf16[216,3072]{1,0:T(8,128)(2,1)S(1)} %get-tuple-element.8.cabs, bf16[576,3072]{1,0:T(8,128)(2,1)} %bitcast.9), custom_call_target="tpu_custom_call" | custom-call | tf_op jit(solution)/shard_map/pallas_call | solution.py:363
  34.0 0.0 copy-start.1
  34.0 22.4 %all_to_all.25.got.coefs = bf16[8,432,128]{2,1,0:T(8,128)(2,1)S(1)} all-to-all(bf16[8,432,128]{2,1,0:T(8,128)(2,1)S(1)} %shard_map.93), channel_id=1, replica_groups=mesh['occ'=16,'aux'=8,'pair'=4] {'aux'}, dimensions={0} | all-to-all | bytes 1769472 | tf_op jit(solution)/shard_map/all_to_all | solution.py:325
  56.5 0.2 shard_map.94
  56.7 9.3 %all_to_all.26 = f16[4,224,128]{2,1,0:T(8,128)(2,1)S(1)} all-to-all(f16[4,224,128]{2,1,0:T(8,128)(2,1)S(1)} %broadcast_in_dim.10), channel_id=1, replica_groups=mesh['occ'=16,'aux'=8,'pair'=4] {'pair'}, dimensions={0} | all-to-all | bytes 458752 | tf_op jit(solution)/shard_map/all_to_all | solution.py:325
  66.1 0.0 copy-done.1
  66.1 3.8 %shard_map.95 = f32[16,48,128]{2,1,0:T(8,128)S(1)} custom-call(s32[24]{0:T(128)S(1)} %copy-done.1, f32[4,224,128]{2,1,0:T(8,128)S(1)} %convert_element_type.21.got, bf16[8,432,128]{2,1,0:T(8,128)(2,1)S(1)} %all_to_all.25.got.coefs), custom_call_target="tpu_custom_call" | custom-call | tf_op jit(solution)/shard_map/pallas_call | solution.py:389
  70.0 16.8 %all_to_all.27 = f16[16,48,128]{2,1,0:T(8,128)(2,1)S(1)} all-to-all(f16[16,48,128]{2,1,0:T(8,128)(2,1)S(1)} %convert_element_type.22), channel_id=1, replica_groups=mesh['occ'=16,'aux'=8,'pair'=4] {'occ'}, dimensions={0} | all-to-all | bytes 393216 | tf_op jit(solution)/shard_map/all_to_all | solution.py:325
  86.8 0.2 shard_map.96
  87.0 16.3 %all_to_all.28 = f16[32,16,128]{2,1,0:T(8,128)(2,1)S(1)} all-to-all(f16[32,16,128]{2,1,0:T(8,128)(2,1)S(1)} %convert_element_type.24), channel_id=1, replica_groups=mesh['occ'=16,'aux'=8,'pair'=4] {'pair','aux'}, dimensions={0} | all-to-all | bytes 262144 | tf_op jit(solution)/shard_map/all_to_all | solution.py:325
  103.3 1.0 shard_map.97
  (8 shorter events, 0.2 us)
Async XLA Ops:
  2.1 28.3 %all-to-all-start = ((bf16[16,24,256]{2,1,0:T(8,128)(2,1)}), bf16[16,24,256]{2,1,0:T(8,128)(2,1)S(1)}, u32[]{:S(2)}, u32[]{:S(2)}) async-start(bf16[16,24,256]{2,1,0:T(8,128)(2,1)} %shard_map.92), calls=%async_computation | async-start | bytes 393216 | tf_op jit(solution)/shard_map/all_to_all | solution.py:325
  19.3 0.7 copy-start
  34.0 32.0 %copy-start.1 = (s32[24]{0:T(128)S(1)}, s32[24]{0:T(128)}, u32[]{:S(2)}) copy-start(s32[24]{0:T(128)} %lens.1) | copy-start | bytes 292

commit v9 on v8

--- a/solution.py
+++ b/solution.py
@@ -62,9 +62,15 @@
 TJ = 72
 GROUP = 8 * LANES
 TROWS = 3 * TJ
+ROOT, STEP, BACK = 11, 7, 7
+FROM_ROOT = [[(STEP * k + ROOT) % NO for k in range(NO)]]
 ROWS = 24
 CROWS = 216
 SROWS = 3 * (TJ + 8) + 192
+
+
+def slot_of(occ):
+    return (BACK * (occ + NO - ROOT)) & (NO - 1)
 
 
 def first_column(occ, pair):
@@ -86,7 +92,7 @@
         c.start()
     shape = (NO, ROWS, NO * NI)
     t = iota(shape, 1)
-    place = jnp.where((iota(shape, 2) == NI * iota(shape, 0) + t) & (t < NI), 1.0, 0.0)
+    place = jnp.where((iota(shape, 2) == NI * ((STEP * iota(shape, 0) + ROOT) & (NO - 1)) + t) & (t < NI), 1.0, 0.0)
     place = place.reshape(NO * ROWS, NO * NI).astype(BF16)
     source, target = iota((LANES, LANES), 0), iota((LANES, LANES), 1)
     mine = source == 8 * (target & 15) + 2 * pair + ((target >> 4) & 1)
@@ -137,7 +143,7 @@
     def picked(step, start):
         count = NO // step
         shape = (NI, count, NO * ROWS)
-        pick = iota(shape, 2) == ROWS * (step * iota(shape, 1) + start) + iota(shape, 0)
+        pick = iota(shape, 2) == ROWS * slot_of(step * iota(shape, 1) + start) + iota(shape, 0)
         pick = jnp.where(pick, 1.0, 0.0).reshape(NI * count, NO * ROWS).astype(BF16)
         rows = dot(pick, messages)
         return [[rows[count * t : count * (t + 1), LANES * h : LANES * (h + 1)] for h in (0, 1)] for t in range(NI)]
@@ -174,7 +180,7 @@
         occ = (row * 3641) >> 16
         rest = row - NI * occ
         sixth = rest - jnp.where(rest >= 12, 12, jnp.where(rest >= 6, 6, 0))
-        base = source - ROWS * occ - sixth
+        base = source - ROWS * slot_of(occ) - sixth
         main = dot(one_hot(base == 18), messages)
         spare0 = dot(one_hot(base == 0), messages[:, LANES:])
         spare1 = dot(one_hot(base == 6), messages[:, LANES:])
@@ -293,7 +299,7 @@
     row = iota((48, LANES), 0)
     for o in range(NO):
         scaled = jnp.where(row < 40, msg[48 * o : 48 * (o + 1), :] * factor, 0.0)
-        out[o] = jnp.where(row == 40, power, scaled)
+        out[slot_of(o)] = jnp.where(row == 40, power, scaled)
 
 
 def sum_occ(got, out, total):
@@ -321,8 +327,8 @@
             out[8 * q + k] = blocks[k]
 
 
-def exchange(x, axes):
-    return lax.all_to_all(x, axes, split_axis=0, concat_axis=0, tiled=True)
+def exchange(x, axes, groups=None):
+    return lax.all_to_all(x, axes, split_axis=0, concat_axis=0, tiled=True, axis_index_groups=groups)
 
 
 def shape_of(shape, dtype):
@@ -349,7 +355,7 @@
         ],
         compiler_params=room(60),
     )(jnp.transpose(amp_fit, (2, 0, 1)), jnp.transpose(amp_cabs, (0, 2, 1)), coef)
-    amps = exchange(sent, "occ")
+    amps = exchange(sent, "occ", FROM_ROOT)
 
     cabs, slots = pl.pallas_call(
         join_cabs,
@@ -401,7 +407,7 @@
         ],
         compiler_params=PARAMS,
     )(shell_len, got, shares)
-    got = exchange(sent.astype(F16), "occ").astype(F32)
+    got = exchange(sent.astype(F16), "occ", FROM_ROOT).astype(F32)
 
     sent = pl.pallas_call(
         sum_occ,

time: 105 us -> 100 us (0.952)
  blocking collectives: 64.8 us -> 60.8 us
    all_to_all x4, blocking collectives: 64.8 us -> 60.8 us  [exchange(): lax.all_to_all(x, axes, split_axis=0, concat_axis=0, tiled=True, axis_ind...]
where the time goes in v9:
time: 100 us; the launch traced here: 99.9 us
  blocking collectives  60.8 us (61%)
  starting transfers between devices  16.4 us (16%)
  Pallas kernels  12.5 us (12%)
  waiting for transfers between devices  7.8 us (8%)
  local copies, waits for them, and re-layouts  1.46 us (1%)
    all_to_all x4, blocking collectives, exchange(): lax.all_to_all(x, axes, split_axis=0, concat_axis=0, tiled=True, axis_ind...  60.8 us
    all_to_all x1, starting transfers between devices, exchange(): lax.all_to_all(x, axes, split_axis=0, concat_axis=0, tiled=True, axis_ind...  16.4 us
    all_to_all x1, waiting for transfers between devices, exchange(): lax.all_to_all(x, axes, split_axis=0, concat_axis=0, tiled=True, axis_ind...  7.8 us
    pallas_call x1, Pallas kernels, on_device(): pl.pallas_call(all_blocks, out_shape=shape_of((NO, 48, LANES), F32), in_s...  3.84 us
    pallas_call x1, Pallas kernels, on_device(): pl.pallas_call(partial_t, out_shape=shape_of((NA, SROWS, LANES), BF16), i...  3.59 us
    pallas_call x1, Pallas kernels, on_device(): pl.pallas_call(pack_amps, out_shape=shape_of((NO, ROWS, 256), BF16), in_s...  2.1 us
  transfers between devices with their start and end apart: 1, of which 1 were waited for; matrix products, arithmetic and copies ran while one was open for 1% of the time, Pallas kernels for 2%

profile of v9, /device:TPU:1, one launch (start us, length us, event | category | flops | bytes accessed | tf_op | source)
XLA Modules:
  0.0 99.9 jit_solution(12567928865392321562)
XLA Ops:
  0.0 2.1 %shard_map.92 = bf16[16,24,256]{2,1,0:T(8,128)(2,1)} custom-call(bf16[18,32,288]{2,1,0:T(8,128)(2,1)} %bitcast.10, bf16[12,18,288]{2,1,0:T(8,128)(2,1)} %bitcast.11, bf16[18,3072]{1,0:T(8,128)(2,1)} %coef_hbm.1), custom_call_target="tpu_custom_call" | custom-call | tf_op jit(solution)/shard_map/pallas_call | solution.py:341
  2.1 16.4 %all-to-all-start = ((bf16[16,24,256]{2,1,0:T(8,128)(2,1)}), bf16[16,24,256]{2,1,0:T(8,128)(2,1)S(1)}, u32[]{:S(2)}, u32[]{:S(2)}) async-start(bf16[16,24,256]{2,1,0:T(8,128)(2,1)} %shard_map.92), calls=%async_computation | async-start | bytes 393216 | tf_op jit(solution)/shard_map/all_to_all | solution.py:331
  19.2 0.7 tile.4
  19.9 0.1 tile.10
  19.9 0.0 copy-start
  20.0 0.7 copy-done
  20.6 1.7 %shard_map.91 = (bf16[216,3072]{1,0:T(8,128)(2,1)S(1)}, f32[8,128]{1,0:T(8,128)S(1)}) custom-call(s32[1]{0:T(128)S(6)} %copy.10.counts, s32[2,40]{1,0:T(2,128)S(1)} %bitcast.8, bf16[12,18,3072]{2,1,0:T(8,128)(2,1)} %cabs_hbm.1), custom_call_target="tpu_custom_call" | custom-call | bytes 5000000 | tf_op jit(solution)/shard_map/pallas_call | solution.py:360
  22.3 7.8 %all-to-all-done.got = bf16[16,24,256]{2,1,0:T(8,128)(2,1)S(1)} async-done(((bf16[16,24,256]{2,1,0:T(8,128)(2,1)}), bf16[16,24,256]{2,1,0:T(8,128)(2,1)S(1)}, u32[]{:S(2)}, u32[]{:S(2)}) %all-to-all-start) | async-done | bytes 196640 | tf_op jit(solution)/shard_map/all_to_all | solution.py:331
  30.1 3.6 %shard_map.93 = bf16[8,432,128]{2,1,0:T(8,128)(2,1)S(1)} custom-call(bf16[16,24,256]{2,1,0:T(8,128)(2,1)S(1)} %all-to-all-done.got, f32[1,256]{1,0:T(1,128)S(1)} %bitcast.7, bf16[216,3072]{1,0:T(8,128)(2,1)S(1)} %get-tuple-element.8.cabs, bf16[576,3072]{1,0:T(8,128)(2,1)} %bitcast.9), custom_call_target="tpu_custom_call" | custom-call | tf_op jit(solution)/shard_map/pallas_call | solution.py:369
  33.7 0.0 copy-start.1
  33.7 18.9 %all_to_all.25.got.coefs = bf16[8,432,128]{2,1,0:T(8,128)(2,1)S(1)} all-to-all(bf16[8,432,128]{2,1,0:T(8,128)(2,1)S(1)} %shard_map.93), channel_id=1, replica_groups=mesh['occ'=16,'aux'=8,'pair'=4] {'aux'}, dimensions={0} | all-to-all | bytes 1769472 | tf_op jit(solution)/shard_map/all_to_all | solution.py:331
  52.6 0.2 shard_map.94
  52.8 9.3 %all_to_all.26 = f16[4,224,128]{2,1,0:T(8,128)(2,1)S(1)} all-to-all(f16[4,224,128]{2,1,0:T(8,128)(2,1)S(1)} %broadcast_in_dim.10), channel_id=1, replica_groups=mesh['occ'=16,'aux'=8,'pair'=4] {'pair'}, dimensions={0} | all-to-all | bytes 458752 | tf_op jit(solution)/shard_map/all_to_all | solution.py:331
  62.2 0.0 copy-done.1
  62.2 3.8 %shard_map.95 = f32[16,48,128]{2,1,0:T(8,128)S(1)} custom-call(s32[24]{0:T(128)S(1)} %copy-done.1, f32[4,224,128]{2,1,0:T(8,128)S(1)} %convert_element_type.21.got, bf16[8,432,128]{2,1,0:T(8,128)(2,1)S(1)} %all_to_all.25.got.coefs), custom_call_target="tpu_custom_call" | custom-call | tf_op jit(solution)/shard_map/pallas_call | solution.py:395
  66.1 18.6 %all_to_all.27 = f16[16,48,128]{2,1,0:T(8,128)(2,1)S(1)} all-to-all(f16[16,48,128]{2,1,0:T(8,128)(2,1)S(1)} %convert_element_type.22), channel_id=1, replica_groups={{352,64,288,0,224,448,160,384,96,320,32,256,480,192,416,128},{353,65,28..., dimensions={0} | all-to-all | bytes 393216 | tf_op jit(solution)/shard_map/all_to_all | solution.py:331
  84.7 0.2 shard_map.96
  84.9 14.0 %all_to_all.28 = f16[32,16,128]{2,1,0:T(8,128)(2,1)S(1)} all-to-all(f16[32,16,128]{2,1,0:T(8,128)(2,1)S(1)} %convert_element_type.24), channel_id=1, replica_groups=mesh['occ'=16,'aux'=8,'pair'=4] {'pair','aux'}, dimensions={0} | all-to-all | bytes 262144 | tf_op jit(solution)/shard_map/all_to_all | solution.py:331
  98.9 1.0 shard_map.97
  (8 shorter events, 0.2 us)
Async XLA Ops:
  2.1 28.0 %all-to-all-start = ((bf16[16,24,256]{2,1,0:T(8,128)(2,1)}), bf16[16,24,256]{2,1,0:T(8,128)(2,1)S(1)}, u32[]{:S(2)}, u32[]{:S(2)}) async-start(bf16[16,24,256]{2,1,0:T(8,128)(2,1)} %shard_map.92), calls=%async_computation | async-start | bytes 393216 | tf_op jit(solution)/shard_map/all_to_all | solution.py:331
  19.9 0.7 copy-start
  33.7 28.5 %copy-start.1 = (s32[24]{0:T(128)S(1)}, s32[24]{0:T(128)}, u32[]{:S(2)}) copy-start(s32[24]{0:T(128)} %lens.1) | copy-start | bytes 292

commit v10 on v9

--- a/solution.py
+++ b/solution.py
@@ -64,6 +64,9 @@
 TROWS = 3 * TJ
 ROOT, STEP, BACK = 11, 7, 7
 FROM_ROOT = [[(STEP * k + ROOT) % NO for k in range(NO)]]
+FROM_AUX = [[(k + 6) % NA for k in range(NA)]]
+FROM_PAIR = [[(k + 3) % NP for k in range(NP)]]
+FROM_BOTH = [[NA * y + p for y in FROM_PAIR[0] for p in FROM_AUX[0]]]
 ROWS = 24
 CROWS = 216
 SROWS = 3 * (TJ + 8) + 192
@@ -71,6 +74,18 @@
 
 def slot_of(occ):
     return (BACK * (occ + NO - ROOT)) & (NO - 1)
+
+
+def aux_slot(aux):
+    return (aux + NA - 6) % NA
+
+
+def pair_slot(pair):
+    return (pair + NP - 3) % NP
+
+
+def both_slot(pair, aux):
+    return NA * pair_slot(pair) + aux_slot(aux)
 
 
 def first_column(occ, pair):
@@ -208,7 +223,7 @@
         pieces = swap_pieces([total[:, LANES * k : LANES * (k + 1)] for k in range(8)], 16)
         for k in range(8):
             rows = jnp.concatenate([pieces[k], own[192 + 8 * g : 200 + 8 * g, :]], axis=0)
-            out[k, (TJ + 8) * g : (TJ + 8) * (g + 1), :] = rows.astype(BF16)
+            out[aux_slot(k), (TJ + 8) * g : (TJ + 8) * (g + 1), :] = rows.astype(BF16)
 
 
 def scale_of(top):
@@ -232,7 +247,7 @@
 def all_blocks(lens, got, coefs, out, ints, words, tmat, dmat, msg, sem):
     aux, pair = lax.axis_index("aux"), lax.axis_index("pair")
     for y in range(NP):
-        ints[8 * y : 8 * (y + 1), :] = got[y, TROWS : TROWS + 8, :].astype(jnp.int32)
+        ints[8 * y : 8 * (y + 1), :] = got[pair_slot(y), TROWS : TROWS + 8, :].astype(jnp.int32)
     copy = pltpu.make_async_copy(ints, words, sem)
     copy.start()
 
@@ -243,7 +258,8 @@
             limit = jnp.where((lane >> 4) == k, lens[8 * g + k], limit)
         kept = (lane & 15) + 16 * aux < limit
         for y in range(NP):
-            part = got[y, TJ * g : TJ * (g + 1), :] * unscale(got[y, TROWS : TROWS + 1, :])
+            slot = pair_slot(y)
+            part = got[slot, TJ * g : TJ * (g + 1), :] * unscale(got[slot, TROWS : TROWS + 1, :])
             part = jnp.where(kept, part, 0.0)
             high = part.astype(BF16).astype(F32)
             tmat[TJ * y : TJ * (y + 1), LANES * g : LANES * (g + 1)] = high
@@ -262,7 +278,7 @@
         for k in range(3):
             limit = jnp.where((lane >> 5) == k, lens[3 * p + k], limit)
         kept = 8 * (lane & 15) + 2 * pair + ((lane >> 4) & 1) < limit
-        packed = coefs[p].astype(F32)
+        packed = coefs[aux_slot(p)].astype(F32)
         spare = [packed[(TJ + 8) * g + TJ : (TJ + 8) * (g + 1)] for g in range(3)]
         packed = jnp.concatenate([packed[SROWS - 192 :]] + spare, axis=0)
         rows = [packed[TJ * b : TJ * (b + 1)] for b in range(3)]
@@ -310,14 +326,14 @@
     for y in range(NP):
         rows = total[10 * y : 10 * (y + 1), :]
         for p in range(NA):
-            out[NA * y + p, 0:10, :] = rows
-            out[NA * y + p, 10:16, :] = rest
+            out[both_slot(y, p), 0:10, :] = rows
+            out[both_slot(y, p), 10:16, :] = rest
 
 
 def unpack(got, out, rows):
     for y in range(NP):
         for p in range(NA):
-            part = got[NA * y + p]
+            part = got[both_slot(y, p)]
             part = part * unscale(part[10:11, :])
             for q in range(5):
                 rows[q, p, 2 * y : 2 * y + 2, :] = part[2 * q : 2 * q + 2, :]
@@ -380,7 +396,7 @@
         ],
         compiler_params=room(49),
     )(amps, weight, cabs, jnp.transpose(ints_fit, (1, 0, 2)).reshape(NI * NF, 24 * LANES))
-    shares = exchange(sent, "aux")
+    shares = exchange(sent, "aux", FROM_AUX)
 
     sent = pl.pallas_call(
         sum_aux,
@@ -390,7 +406,7 @@
         compiler_params=PARAMS,
     )(slots, shares)
     sent = jnp.broadcast_to(sent.astype(F16)[None], (NP, TROWS + 8, LANES))
-    got = exchange(sent, "pair").astype(F32)
+    got = exchange(sent, "pair", FROM_PAIR).astype(F32)
 
     sent = pl.pallas_call(
         all_blocks,
@@ -417,7 +433,7 @@
         scratch_shapes=[pltpu.VMEM((40, LANES), F32)],
         compiler_params=PARAMS,
     )(got)
-    got = exchange(sent.astype(F16), ("pair", "aux")).astype(F32)
+    got = exchange(sent.astype(F16), ("pair", "aux"), FROM_BOTH).astype(F32)
 
     return pl.pallas_call(
         unpack,

time: 100 us -> 98.8 us (0.988)
  blocking collectives: 60.8 us -> 59.3 us
    all_to_all x4, blocking collectives: 60.8 us -> 59.3 us  [exchange(): lax.all_to_all(x, axes, split_axis=0, concat_axis=0, tiled=True, axis_ind...]
where the time goes in v10:
time: 98.8 us; the launch traced here: 98.4 us
  blocking collectives  59.3 us (60%)
  starting transfers between devices  16.4 us (17%)
  Pallas kernels  12.5 us (13%)
  waiting for transfers between devices  7.8 us (8%)
  local copies, waits for them, and re-layouts  1.46 us (1%)
    all_to_all x4, blocking collectives, exchange(): lax.all_to_all(x, axes, split_axis=0, concat_axis=0, tiled=True, axis_ind...  59.3 us
    all_to_all x1, starting transfers between devices, exchange(): lax.all_to_all(x, axes, split_axis=0, concat_axis=0, tiled=True, axis_ind...  16.4 us
    all_to_all x1, waiting for transfers between devices, exchange(): lax.all_to_all(x, axes, split_axis=0, concat_axis=0, tiled=True, axis_ind...  7.8 us
    pallas_call x1, Pallas kernels, on_device(): pl.pallas_call(all_blocks, out_shape=shape_of((NO, 48, LANES), F32), in_s...  3.84 us
    pallas_call x1, Pallas kernels, on_device(): pl.pallas_call(partial_t, out_shape=shape_of((NA, SROWS, LANES), BF16), i...  3.59 us
    pallas_call x1, Pallas kernels, on_device(): pl.pallas_call(pack_amps, out_shape=shape_of((NO, ROWS, 256), BF16), in_s...  2.1 us
  transfers between devices with their start and end apart: 1, of which 1 were waited for; matrix products, arithmetic and copies ran while one was open for 1% of the time, Pallas kernels for 2%

profile of v10, /device:TPU:1, one launch (start us, length us, event | category | flops | bytes accessed | tf_op | source)
XLA Modules:
  0.0 98.4 jit_solution(6070332867779003124)
XLA Ops:
  0.0 2.1 %shard_map.92 = bf16[16,24,256]{2,1,0:T(8,128)(2,1)} custom-call(bf16[18,32,288]{2,1,0:T(8,128)(2,1)} %bitcast.10, bf16[12,18,288]{2,1,0:T(8,128)(2,1)} %bitcast.11, bf16[18,3072]{1,0:T(8,128)(2,1)} %coef_hbm.1), custom_call_target="tpu_custom_call" | custom-call | tf_op jit(solution)/shard_map/pallas_call | solution.py:357
  2.1 16.4 %all-to-all-start = ((bf16[16,24,256]{2,1,0:T(8,128)(2,1)}), bf16[16,24,256]{2,1,0:T(8,128)(2,1)S(1)}, u32[]{:S(2)}, u32[]{:S(2)}) async-start(bf16[16,24,256]{2,1,0:T(8,128)(2,1)} %shard_map.92), calls=%async_computation | async-start | bytes 393216 | tf_op jit(solution)/shard_map/all_to_all | solution.py:347
  19.2 0.7 tile.4
  19.9 0.1 tile.10
  19.9 0.0 copy-start
  20.0 0.7 copy-done
  20.6 1.7 %shard_map.91 = (bf16[216,3072]{1,0:T(8,128)(2,1)S(1)}, f32[8,128]{1,0:T(8,128)S(1)}) custom-call(s32[1]{0:T(128)S(6)} %copy.10.counts, s32[2,40]{1,0:T(2,128)S(1)} %bitcast.8, bf16[12,18,3072]{2,1,0:T(8,128)(2,1)} %cabs_hbm.1), custom_call_target="tpu_custom_call" | custom-call | bytes 5000000 | tf_op jit(solution)/shard_map/pallas_call | solution.py:376
  22.3 7.8 %all-to-all-done.got = bf16[16,24,256]{2,1,0:T(8,128)(2,1)S(1)} async-done(((bf16[16,24,256]{2,1,0:T(8,128)(2,1)}), bf16[16,24,256]{2,1,0:T(8,128)(2,1)S(1)}, u32[]{:S(2)}, u32[]{:S(2)}) %all-to-all-start) | async-done | bytes 196640 | tf_op jit(solution)/shard_map/all_to_all | solution.py:347
  30.1 3.6 %shard_map.93 = bf16[8,432,128]{2,1,0:T(8,128)(2,1)S(1)} custom-call(bf16[16,24,256]{2,1,0:T(8,128)(2,1)S(1)} %all-to-all-done.got, f32[1,256]{1,0:T(1,128)S(1)} %bitcast.7, bf16[216,3072]{1,0:T(8,128)(2,1)S(1)} %get-tuple-element.8.cabs, bf16[576,3072]{1,0:T(8,128)(2,1)} %bitcast.9), custom_call_target="tpu_custom_call" | custom-call | tf_op jit(solution)/shard_map/pallas_call | solution.py:385
  33.7 0.0 copy-start.1
  33.7 18.0 %all_to_all.25.got.coefs = bf16[8,432,128]{2,1,0:T(8,128)(2,1)S(1)} all-to-all(bf16[8,432,128]{2,1,0:T(8,128)(2,1)S(1)} %shard_map.93), channel_id=1, replica_groups={{24,28,0,4,8,12,16,20},{25,29,1,5,9,13,17,21},{26,30,2,6,10,14,18,22},{..., dimensions={0} | all-to-all | bytes 1769472 | tf_op jit(solution)/shard_map/all_to_all | solution.py:347
  51.7 0.2 shard_map.94
  51.9 8.7 %all_to_all.26 = f16[4,224,128]{2,1,0:T(8,128)(2,1)S(1)} all-to-all(f16[4,224,128]{2,1,0:T(8,128)(2,1)S(1)} %broadcast_in_dim.10), channel_id=1, replica_groups={{3,0,1,2},{7,4,5,6},{11,8,9,10},{15,12,13,14},{19,16,17,18},{23,20,21,2..., dimensions={0} | all-to-all | bytes 458752 | tf_op jit(solution)/shard_map/all_to_all | solution.py:347
  60.6 0.0 copy-done.1
  60.6 3.8 %shard_map.95 = f32[16,48,128]{2,1,0:T(8,128)S(1)} custom-call(s32[24]{0:T(128)S(1)} %copy-done.1, f32[4,224,128]{2,1,0:T(8,128)S(1)} %convert_element_type.21.got, bf16[8,432,128]{2,1,0:T(8,128)(2,1)S(1)} %all_to_all.25.got.coefs), custom_call_target="tpu_custom_call" | custom-call | tf_op jit(solution)/shard_map/pallas_call | solution.py:411
  64.5 19.0 %all_to_all.27 = f16[16,48,128]{2,1,0:T(8,128)(2,1)S(1)} all-to-all(f16[16,48,128]{2,1,0:T(8,128)(2,1)S(1)} %convert_element_type.22), channel_id=1, replica_groups={{352,64,288,0,224,448,160,384,96,320,32,256,480,192,416,128},{353,65,28..., dimensions={0} | all-to-all | bytes 393216 | tf_op jit(solution)/shard_map/all_to_all | solution.py:347
  83.5 0.2 shard_map.96
  83.7 13.7 %all_to_all.28 = f16[32,16,128]{2,1,0:T(8,128)(2,1)S(1)} all-to-all(f16[32,16,128]{2,1,0:T(8,128)(2,1)S(1)} %convert_element_type.24), channel_id=1, replica_groups={{27,31,3,7,11,15,19,23,24,28,0,4,8,12,16,20,25,29,1,5,9,13,17,21,26,30,..., dimensions={0} | all-to-all | bytes 262144 | tf_op jit(solution)/shard_map/all_to_all | solution.py:347
  97.4 1.0 shard_map.97
  (8 shorter events, 0.2 us)
Async XLA Ops:
  2.1 28.0 %all-to-all-start = ((bf16[16,24,256]{2,1,0:T(8,128)(2,1)}), bf16[16,24,256]{2,1,0:T(8,128)(2,1)S(1)}, u32[]{:S(2)}, u32[]{:S(2)}) async-start(bf16[16,24,256]{2,1,0:T(8,128)(2,1)} %shard_map.92), calls=%async_computation | async-start | bytes 393216 | tf_op jit(solution)/shard_map/all_to_all | solution.py:347
  19.9 0.7 copy-start
  33.7 26.9 %copy-start.1 = (s32[24]{0:T(128)S(1)}, s32[24]{0:T(128)}, u32[]{:S(2)}) copy-start(s32[24]{0:T(128)} %lens.1) | copy-start | bytes 292

commit v11 on v10

--- a/solution.py
+++ b/solution.py
@@ -69,7 +69,7 @@
 FROM_BOTH = [[NA * y + p for y in FROM_PAIR[0] for p in FROM_AUX[0]]]
 ROWS = 24
 CROWS = 216
-SROWS = 3 * (TJ + 8) + 192
+SROWS = TROWS + 8 + CROWS
 
 
 def slot_of(occ):
@@ -147,7 +147,7 @@
         out[NI * q : NI * (q + 1), :] = cabs[q]
 
 
-def partial_t(got, weight, cabs, fit_hbm, out, a_fit, a_cab, own, fit, sems):
+def partial_t(got, weight, cabs, fit_hbm, out, factors, a_fit, a_cab, own, fit, sems):
     spans = [pl.ds(GROUP * g, GROUP) for g in range(3)]
     copies = [pltpu.make_async_copy(fit_hbm.at[:, s], fit.at[:, s], sems.at[g]) for g, s in enumerate(spans)]
     for c in copies:
@@ -211,9 +211,10 @@
         for b in range(3):
             moved = pltpu.roll(last, 96 - 32 * b, 1)
             own[TJ * b : TJ * (b + 1), :] = jnp.where(lane < 96, coef[TJ * b : TJ * (b + 1)], moved)
-        packed = own[0:192, :].astype(BF16)
         for p in range(NA):
-            out[p, SROWS - 192 :, :] = packed
+            out[p, TROWS + 8 :, :] = own[...]
+
+    top = jnp.zeros((TJ, LANES), F32)
 
     for g in range(3):
         copies[g].wait()
@@ -221,9 +222,17 @@
         if g == 0:
             pack_coefficients()
         pieces = swap_pieces([total[:, LANES * k : LANES * (k + 1)] for k in range(8)], 16)
+        top = functools.reduce(jnp.maximum, [jnp.abs(piece) for piece in pieces], top)
         for k in range(8):
-            rows = jnp.concatenate([pieces[k], own[192 + 8 * g : 200 + 8 * g, :]], axis=0)
-            out[aux_slot(k), (TJ + 8) * g : (TJ + 8) * (g + 1), :] = rows.astype(BF16)
+            out[aux_slot(k), TJ * g : TJ * (g + 1), :] = pieces[k]
+    power_t, factor_t = scale_of(top)
+    power_c, factor_c = scale_of(jnp.abs(own[...]))
+    factors[0:TROWS, :] = jnp.broadcast_to(factor_t, (TROWS, LANES))
+    factors[TROWS : TROWS + 8, :] = jnp.ones((8, LANES), F32)
+    factors[TROWS + 8 :, :] = jnp.broadcast_to(factor_c, (CROWS, LANES))
+    powers = jnp.where(iota((8, LANES), 0) == 0, power_t, power_c)
+    for p in range(NA):
+        out[p, TROWS : TROWS + 8, :] = powers
 
 
 def scale_of(top):
@@ -237,8 +246,7 @@
 
 
 def sum_aux(slots, got, out):
-    total = jnp.sum(got[:, 0 : 3 * (TJ + 8), :].astype(F32), axis=0)
-    total = jnp.concatenate([total[(TJ + 8) * g : (TJ + 8) * g + TJ] for g in range(3)], axis=0)
+    total = sum(got[p, 0:TROWS, :] * unscale(got[p, TROWS : TROWS + 1, :]) for p in range(NA))
     power, factor = scale_of(jnp.abs(total))
     out[0:TROWS, :] = total * factor
     out[TROWS:, :] = jnp.where(iota((8, LANES), 0) == 0, power, slots[...])
@@ -278,9 +286,8 @@
         for k in range(3):
             limit = jnp.where((lane >> 5) == k, lens[3 * p + k], limit)
         kept = 8 * (lane & 15) + 2 * pair + ((lane >> 4) & 1) < limit
-        packed = coefs[aux_slot(p)].astype(F32)
-        spare = [packed[(TJ + 8) * g + TJ : (TJ + 8) * (g + 1)] for g in range(3)]
-        packed = jnp.concatenate([packed[SROWS - 192 :]] + spare, axis=0)
+        packed = coefs[aux_slot(p)]
+        packed = packed[8:] * unscale(packed[1:2])
         rows = [packed[TJ * b : TJ * (b + 1)] for b in range(3)]
         last = pltpu.roll(rows[0], 32, 1)
         last = jnp.where(lane >= 32, pltpu.roll(rows[1], 64, 1), last)
@@ -294,7 +301,6 @@
 
     copy.wait()
     lane = iota((32, LANES), 1)
-    top = jnp.zeros((32, LANES), F32)
     for q in range(20):
         y = q // 5
         count = words[8 * y + 3, 0]
@@ -308,18 +314,14 @@
             block = pltpu.roll(block, (16 * (k + 8 - (b & 7))) & 127, 1)
             end = jnp.where(slot < count, 16 * (k + 1), 0)
             tile = jnp.where((lane >= 16 * k) & (lane < end), block, tile)
-        top = jnp.maximum(top, jnp.abs(tile))
         for e in range(2):
-            msg[pl.ds(2 * q + e, NO, stride=48), :] = tile[NO * e : NO * (e + 1)]
-    power, factor = scale_of(top)
-    row = iota((48, LANES), 0)
+            msg[pl.ds(2 * q + e, NO, stride=40), :] = tile[NO * e : NO * (e + 1)]
     for o in range(NO):
-        scaled = jnp.where(row < 40, msg[48 * o : 48 * (o + 1), :] * factor, 0.0)
-        out[slot_of(o)] = jnp.where(row == 40, power, scaled)
+        out[slot_of(o)] = msg[40 * o : 40 * (o + 1), :].astype(BF16)
 
 
 def sum_occ(got, out, total):
-    blocks = sum(got[o, 0:40, :] * unscale(got[o, 40:41, :]) for o in range(NO))
+    blocks = jnp.sum(got[...].astype(F32), axis=0)
     power, factor = scale_of(jnp.abs(blocks))
     total[...] = blocks * factor
     rest = jnp.where(iota((6, LANES), 0) == 0, power, 0.0)
@@ -382,11 +384,11 @@
         compiler_params=room(51),
         cost_estimate=pl.CostEstimate(flops=0, bytes_accessed=5_000_000, transcendentals=0),
     )(pair_count, pair_blocks.T, ints_cabs)
-    sent = pl.pallas_call(
+    sent, factors = pl.pallas_call(
         partial_t,
-        out_shape=shape_of((NA, SROWS, LANES), BF16),
+        out_shape=[shape_of((NA, SROWS, LANES), F32), shape_of((SROWS, LANES), F32)],
         in_specs=vmem(3) + [ANY],
-        out_specs=vmem(1)[0],
+        out_specs=vmem(2),
         scratch_shapes=[
             pltpu.VMEM((TJ, 5 * LANES), BF16),
             pltpu.VMEM((TJ, 3 * LANES), BF16),
@@ -396,7 +398,7 @@
         ],
         compiler_params=room(49),
     )(amps, weight, cabs, jnp.transpose(ints_fit, (1, 0, 2)).reshape(NI * NF, 24 * LANES))
-    shares = exchange(sent, "aux", FROM_AUX)
+    shares = exchange((sent * factors[None]).astype(F16), "aux", FROM_AUX)
 
     sent = pl.pallas_call(
         sum_aux,
@@ -404,13 +406,13 @@
         in_specs=vmem(2),
         out_specs=vmem(1)[0],
         compiler_params=PARAMS,
-    )(slots, shares)
+    )(slots, shares[:, : TROWS + 8].astype(F32))
     sent = jnp.broadcast_to(sent.astype(F16)[None], (NP, TROWS + 8, LANES))
     got = exchange(sent, "pair", FROM_PAIR).astype(F32)
 
     sent = pl.pallas_call(
         all_blocks,
-        out_shape=shape_of((NO, 48, LANES), F32),
+        out_shape=shape_of((NO, 40, LANES), BF16),
         in_specs=[SMEM] + vmem(2),
         out_specs=vmem(1)[0],
         scratch_shapes=[
@@ -418,12 +420,12 @@
             pltpu.SMEM((8 * NP, LANES), jnp.int32),
             pltpu.VMEM((NP * TJ, 6 * LANES), F32),
             pltpu.VMEM((3, 8 * LANES, LANES), F32),
-            pltpu.VMEM((NO * 48, LANES), F32),
+            pltpu.VMEM((NO * 40, LANES), F32),
             pltpu.SemaphoreType.DMA,
         ],
         compiler_params=PARAMS,
-    )(shell_len, got, shares)
-    got = exchange(sent.astype(F16), "occ", FROM_ROOT).astype(F32)
+    )(shell_len, got, shares[:, TROWS:].astype(F32))
+    got = exchange(sent, "occ", FROM_ROOT)
 
     sent = pl.pallas_call(
         sum_occ,

time: 98.8 us -> 97.9 us (level)
  blocking collectives: 59.3 us -> 58 us
    all_to_all x4, blocking collectives: 59.3 us -> 58 us  [exchange(): lax.all_to_all(x, axes, split_axis=0, concat_axis=0, tiled=True, axis_ind...]
where the time goes in v11:
time: 97.9 us; the launch traced here: 97.5 us
  blocking collectives  58 us (59%)
  starting transfers between devices  16.4 us (17%)
  Pallas kernels  12.6 us (13%)
  waiting for transfers between devices  7.8 us (8%)
  local copies, waits for them, and re-layouts  1.46 us (1%)
    all_to_all x4, blocking collectives, exchange(): lax.all_to_all(x, axes, split_axis=0, concat_axis=0, tiled=True, axis_ind...  58 us
    all_to_all x1, starting transfers between devices, exchange(): lax.all_to_all(x, axes, split_axis=0, concat_axis=0, tiled=True, axis_ind...  16.4 us
    all_to_all x1, waiting for transfers between devices, exchange(): lax.all_to_all(x, axes, split_axis=0, concat_axis=0, tiled=True, axis_ind...  7.8 us
    pallas_call x1, Pallas kernels, on_device(): pl.pallas_call(partial_t, out_shape=[shape_of((NA, SROWS, LANES), F32), s...  3.83 us
    pallas_call x1, Pallas kernels, on_device(): pl.pallas_call(all_blocks, out_shape=shape_of((NO, 40, LANES), BF16), in_...  3.7 us
    pallas_call x1, Pallas kernels, on_device(): pl.pallas_call(pack_amps, out_shape=shape_of((NO, ROWS, 256), BF16), in_s...  2.09 us
  transfers between devices with their start and end apart: 1, of which 1 were waited for; matrix products, arithmetic and copies ran while one was open for 1% of the time, Pallas kernels for 2%

profile of v11, /device:TPU:1, one launch (start us, length us, event | category | flops | bytes accessed | tf_op | source)
XLA Modules:
  0.0 97.5 jit_solution(833243861462978058)
XLA Ops:
  0.0 2.1 %shard_map.92 = bf16[16,24,256]{2,1,0:T(8,128)(2,1)} custom-call(bf16[18,32,288]{2,1,0:T(8,128)(2,1)} %bitcast.10, bf16[12,18,288]{2,1,0:T(8,128)(2,1)} %bitcast.11, bf16[18,3072]{1,0:T(8,128)(2,1)} %coef_hbm.1), custom_call_target="tpu_custom_call" | custom-call | tf_op jit(solution)/shard_map/pallas_call | solution.py:359
  2.1 16.4 %all-to-all-start = ((bf16[16,24,256]{2,1,0:T(8,128)(2,1)}), bf16[16,24,256]{2,1,0:T(8,128)(2,1)S(1)}, u32[]{:S(2)}, u32[]{:S(2)}) async-start(bf16[16,24,256]{2,1,0:T(8,128)(2,1)} %shard_map.92), calls=%async_computation | async-start | bytes 393216 | tf_op jit(solution)/shard_map/all_to_all | solution.py:349
  19.2 0.7 tile.4
  19.8 0.1 tile.10
  19.9 0.0 copy-start
  20.0 0.7 copy-done
  20.6 1.7 %shard_map.91 = (bf16[216,3072]{1,0:T(8,128)(2,1)S(1)}, f32[8,128]{1,0:T(8,128)S(1)}) custom-call(s32[1]{0:T(128)S(6)} %copy.10.counts, s32[2,40]{1,0:T(2,128)S(1)} %bitcast.8, bf16[12,18,3072]{2,1,0:T(8,128)(2,1)} %cabs_hbm.1), custom_call_target="tpu_custom_call" | custom-call | bytes 5000000 | tf_op jit(solution)/shard_map/pallas_call | solution.py:378
  22.3 7.8 %all-to-all-done.got = bf16[16,24,256]{2,1,0:T(8,128)(2,1)S(1)} async-done(((bf16[16,24,256]{2,1,0:T(8,128)(2,1)}), bf16[16,24,256]{2,1,0:T(8,128)(2,1)S(1)}, u32[]{:S(2)}, u32[]{:S(2)}) %all-to-all-start) | async-done | bytes 196640 | tf_op jit(solution)/shard_map/all_to_all | solution.py:349
  30.1 3.8 %shard_map.93 = (f32[8,440,128]{2,1,0:T(8,128)S(1)}, f32[440,128]{1,0:T(8,128)S(1)}) custom-call(bf16[16,24,256]{2,1,0:T(8,128)(2,1)S(1)} %all-to-all-done.got, f32[1,256]{1,0:T(1,128)S(1)} %bitcast.7, bf16[216,3072]{1,0:T(8,128)(2,1)S(1)} %get-tuple-element.10.cabs, bf16[576,3072]{1,0:T(8,128)(2,1)} %bitcast.9), custom_call_target="tpu_custom_call" | custom-call | tf_op jit(solution)/shard_map/pallas_call | solution.py:387
  33.9 0.2 multiply_convert_fusion
  34.1 18.1 %all_to_all.25 = f16[8,440,128]{2,1,0:T(8,128)(2,1)S(1)} all-to-all(f16[8,440,128]{2,1,0:T(8,128)(2,1)S(1)} %multiply_convert_fusion), channel_id=1, replica_groups={{24,28,0,4,8,12,16,20},{25,29,1,5,9,13,17,21},{26,30,2,6,10,14,18,22},{..., dimensions={0} | all-to-all | bytes 1802240 | tf_op jit(solution)/shard_map/all_to_all | solution.py:349
  52.2 0.1 slice_convert_fusion
  52.3 0.0 copy-start.1
  52.4 0.2 shard_map.94
  52.6 8.7 %all_to_all.26 = f16[4,224,128]{2,1,0:T(8,128)(2,1)S(1)} all-to-all(f16[4,224,128]{2,1,0:T(8,128)(2,1)S(1)} %broadcast_in_dim.5), channel_id=1, replica_groups={{3,0,1,2},{7,4,5,6},{11,8,9,10},{15,12,13,14},{19,16,17,18},{23,20,21,2..., dimensions={0} | all-to-all | bytes 458752 | tf_op jit(solution)/shard_map/all_to_all | solution.py:349
  61.3 0.0 copy-done.1
  61.3 3.7 %shard_map.95 = bf16[16,40,128]{2,1,0:T(8,128)(2,1)S(1)} custom-call(s32[24]{0:T(128)S(1)} %copy-done.1, f32[4,224,128]{2,1,0:T(8,128)S(1)} %convert_element_type.26.got, f32[8,224,128]{2,1,0:T(8,128)S(1)} %get-tuple-element.13.coefs), custom_call_target="tpu_custom_call" | custom-call | tf_op jit(solution)/shard_map/pallas_call | solution.py:413
  65.0 17.7 %all_to_all.27.got = bf16[16,40,128]{2,1,0:T(8,128)(2,1)S(1)} all-to-all(bf16[16,40,128]{2,1,0:T(8,128)(2,1)S(1)} %shard_map.95), channel_id=1, replica_groups={{352,64,288,0,224,448,160,384,96,320,32,256,480,192,416,128},{353,65,28..., dimensions={0} | all-to-all | bytes 327680 | tf_op jit(solution)/shard_map/all_to_all | solution.py:349
  82.7 0.1 shard_map.96
  82.9 13.6 %all_to_all.28 = f16[32,16,128]{2,1,0:T(8,128)(2,1)S(1)} all-to-all(f16[32,16,128]{2,1,0:T(8,128)(2,1)S(1)} %convert_element_type.28), channel_id=1, replica_groups={{27,31,3,7,11,15,19,23,24,28,0,4,8,12,16,20,25,29,1,5,9,13,17,21,26,30,..., dimensions={0} | all-to-all | bytes 262144 | tf_op jit(solution)/shard_map/all_to_all | solution.py:349
  96.5 1.0 %shard_map.97 = f32[40,8,128]{2,1,0:T(8,128)} custom-call(f32[32,16,128]{2,1,0:T(8,128)S(1)} %convert_element_type.29.got), custom_call_target="tpu_custom_call" | custom-call | tf_op jit(solution)/shard_map/pallas_call | solution.py:440
  (6 shorter events, 0.1 us)
Async XLA Ops:
  2.1 28.0 %all-to-all-start = ((bf16[16,24,256]{2,1,0:T(8,128)(2,1)}), bf16[16,24,256]{2,1,0:T(8,128)(2,1)S(1)}, u32[]{:S(2)}, u32[]{:S(2)}) async-start(bf16[16,24,256]{2,1,0:T(8,128)(2,1)} %shard_map.92), calls=%async_computation | async-start | bytes 393216 | tf_op jit(solution)/shard_map/all_to_all | solution.py:349
  19.9 0.7 copy-start
  52.3 9.0 %copy-start.1 = (s32[24]{0:T(128)S(1)}, s32[24]{0:T(128)}, u32[]{:S(2)}) copy-start(s32[24]{0:T(128)} %lens.1) | copy-start | bytes 292

commit v12 on v11

--- a/solution.py
+++ b/solution.py
@@ -187,7 +187,11 @@
     source, target = iota(shape, 0), iota(shape, 1)
     q = (target * 3641) >> 16
     order = one_hot((q == (source & 15)) & (target - NI * q == (source >> 4)))
-    a_cab[:, : 2 * LANES] = (dot(a_cab[...], order) * weight[...]).astype(BF16)
+    weighted = dot(a_cab[0:TJ, :], order) * weight[...]
+    high = weighted.astype(BF16).astype(F32)
+    gap = jnp.zeros((8, 2 * LANES), F32)
+    both = jnp.concatenate([high, gap, weighted - high, gap], axis=0)
+    a_cab[:, : 2 * LANES] = both.astype(BF16)
 
     def pack_coefficients():
         shape = (NO * NI, NO * ROWS)
@@ -218,7 +222,8 @@
 
     for g in range(3):
         copies[g].wait()
-        total = dot(a_fit[:, : NI * NF], fit[:, spans[g]]) + dot(a_cab[:, : NI * NC], cabs[:, spans[g]])
+        two = dot(a_cab[:, : NI * NC], cabs[:, spans[g]])
+        total = dot(a_fit[:, : NI * NF], fit[:, spans[g]]) + two[0:TJ] + two[TJ + 8 : 2 * TJ + 8]
         if g == 0:
             pack_coefficients()
         pieces = swap_pieces([total[:, LANES * k : LANES * (k + 1)] for k in range(8)], 16)
@@ -255,7 +260,14 @@
 def all_blocks(lens, got, coefs, out, ints, words, tmat, dmat, msg, sem):
     aux, pair = lax.axis_index("aux"), lax.axis_index("pair")
     for y in range(NP):
-        ints[8 * y : 8 * (y + 1), :] = got[pair_slot(y), TROWS : TROWS + 8, :].astype(jnp.int32)
+        slots = got[pair_slot(y), TROWS : TROWS + 8, :].astype(jnp.int32)
+        a, b, count = slots[1:2], slots[2:3], slots[3:4]
+        third = (a * 171) >> 9
+        ints[8 * y : 8 * y + 1, :] = LANES * third + 32 * (a - 3 * third)
+        ints[8 * y + 1 : 8 * y + 2, :] = b >> 3
+        ints[8 * y + 2 : 8 * y + 3, :] = LANES - 16 * (b & 7)
+        ints[8 * y + 3 : 8 * y + 4, :] = jnp.where(iota((1, LANES), 1) < count, LANES, 0)
+        ints[8 * y + 4 : 8 * y + 8, :] = slots[4:8]
     copy = pltpu.make_async_copy(ints, words, sem)
     copy.start()
 
@@ -303,16 +315,13 @@
     lane = iota((32, LANES), 1)
     for q in range(20):
         y = q // 5
-        count = words[8 * y + 3, 0]
         tile = jnp.zeros((32, LANES), F32)
         for k in range(8):
             slot = 8 * (q % 5) + k
-            a, b = words[8 * y + 1, slot], words[8 * y + 2, slot]
-            third = (a * 171) >> 9
-            start = pl.multiple_of(LANES * third + 32 * (a - 3 * third), 32)
-            block = dmat[b >> 3, pl.ds(start, 32), :]
-            block = pltpu.roll(block, (16 * (k + 8 - (b & 7))) & 127, 1)
-            end = jnp.where(slot < count, 16 * (k + 1), 0)
+            start = pl.multiple_of(words[8 * y, slot], 32)
+            block = dmat[words[8 * y + 1, slot], pl.ds(start, 32), :]
+            block = pltpu.roll(block, (words[8 * y + 2, slot] + 16 * k) & 127, 1)
+            end = jnp.minimum(words[8 * y + 3, slot], 16 * (k + 1))
             tile = jnp.where((lane >= 16 * k) & (lane < end), block, tile)
         for e in range(2):
             msg[pl.ds(2 * q + e, NO, stride=40), :] = tile[NO * e : NO * (e + 1)]
@@ -391,7 +400,7 @@
         out_specs=vmem(2),
         scratch_shapes=[
             pltpu.VMEM((TJ, 5 * LANES), BF16),
-            pltpu.VMEM((TJ, 3 * LANES), BF16),
+            pltpu.VMEM((2 * TJ + 16, 3 * LANES), BF16),
             pltpu.VMEM((CROWS, LANES), F32),
             pltpu.VMEM((NI * NF, 24 * LANES), BF16),
             pltpu.SemaphoreType.DMA((3,)),

time: 97.9 us -> 97.7 us (level)
  no operation moved by 1% of the time
where the time goes in v12:
time: 97.7 us; the launch traced here: 97.3 us
  blocking collectives  58.1 us (59%)
  starting transfers between devices  16.4 us (17%)
  Pallas kernels  12.4 us (13%)
  waiting for transfers between devices  7.8 us (8%)
  local copies, waits for them, and re-layouts  1.46 us (1%)
    all_to_all x4, blocking collectives, exchange(): lax.all_to_all(x, axes, split_axis=0, concat_axis=0, tiled=True, axis_ind...  58.1 us
    all_to_all x1, starting transfers between devices, exchange(): lax.all_to_all(x, axes, split_axis=0, concat_axis=0, tiled=True, axis_ind...  16.4 us
    all_to_all x1, waiting for transfers between devices, exchange(): lax.all_to_all(x, axes, split_axis=0, concat_axis=0, tiled=True, axis_ind...  7.8 us
    pallas_call x1, Pallas kernels, on_device(): pl.pallas_call(partial_t, out_shape=[shape_of((NA, SROWS, LANES), F32), s...  3.83 us
    pallas_call x1, Pallas kernels, on_device(): pl.pallas_call(all_blocks, out_shape=shape_of((NO, 40, LANES), BF16), in_...  3.52 us
    pallas_call x1, Pallas kernels, on_device(): pl.pallas_call(pack_amps, out_shape=shape_of((NO, ROWS, 256), BF16), in_s...  2.09 us
  transfers between devices with their start and end apart: 1, of which 1 were waited for; matrix products, arithmetic and copies ran while one was open for 1% of the time, Pallas kernels for 2%

profile of v12, /device:TPU:1, one launch (start us, length us, event | category | flops | bytes accessed | tf_op | source)
XLA Modules:
  0.0 97.3 jit_solution(13315111158485510061)
XLA Ops:
  0.0 2.1 %shard_map.92 = bf16[16,24,256]{2,1,0:T(8,128)(2,1)} custom-call(bf16[18,32,288]{2,1,0:T(8,128)(2,1)} %bitcast.10, bf16[12,18,288]{2,1,0:T(8,128)(2,1)} %bitcast.11, bf16[18,3072]{1,0:T(8,128)(2,1)} %coef_hbm.1), custom_call_target="tpu_custom_call" | custom-call | tf_op jit(solution)/shard_map/pallas_call | solution.py:368
  2.1 16.4 %all-to-all-start = ((bf16[16,24,256]{2,1,0:T(8,128)(2,1)}), bf16[16,24,256]{2,1,0:T(8,128)(2,1)S(1)}, u32[]{:S(2)}, u32[]{:S(2)}) async-start(bf16[16,24,256]{2,1,0:T(8,128)(2,1)} %shard_map.92), calls=%async_computation | async-start | bytes 393216 | tf_op jit(solution)/shard_map/all_to_all | solution.py:358
  19.2 0.7 tile.4
  19.8 0.1 tile.10
  19.9 0.0 copy-start
  20.0 0.7 copy-done
  20.6 1.7 %shard_map.91 = (bf16[216,3072]{1,0:T(8,128)(2,1)S(1)}, f32[8,128]{1,0:T(8,128)S(1)}) custom-call(s32[1]{0:T(128)S(6)} %copy.10.counts, s32[2,40]{1,0:T(2,128)S(1)} %bitcast.8, bf16[12,18,3072]{2,1,0:T(8,128)(2,1)} %cabs_hbm.1), custom_call_target="tpu_custom_call" | custom-call | bytes 5000000 | tf_op jit(solution)/shard_map/pallas_call | solution.py:387
  22.3 7.8 %all-to-all-done.got = bf16[16,24,256]{2,1,0:T(8,128)(2,1)S(1)} async-done(((bf16[16,24,256]{2,1,0:T(8,128)(2,1)}), bf16[16,24,256]{2,1,0:T(8,128)(2,1)S(1)}, u32[]{:S(2)}, u32[]{:S(2)}) %all-to-all-start) | async-done | bytes 196640 | tf_op jit(solution)/shard_map/all_to_all | solution.py:358
  30.1 3.8 %shard_map.93 = (f32[8,440,128]{2,1,0:T(8,128)S(1)}, f32[440,128]{1,0:T(8,128)S(1)}) custom-call(bf16[16,24,256]{2,1,0:T(8,128)(2,1)S(1)} %all-to-all-done.got, f32[1,256]{1,0:T(1,128)S(1)} %bitcast.7, bf16[216,3072]{1,0:T(8,128)(2,1)S(1)} %get-tuple-element.10.cabs, bf16[576,3072]{1,0:T(8,128)(2,1)} %bitcast.9), custom_call_target="tpu_custom_call" | custom-call | tf_op jit(solution)/shard_map/pallas_call | solution.py:396
  33.9 0.2 multiply_convert_fusion
  34.1 18.1 %all_to_all.25 = f16[8,440,128]{2,1,0:T(8,128)(2,1)S(1)} all-to-all(f16[8,440,128]{2,1,0:T(8,128)(2,1)S(1)} %multiply_convert_fusion), channel_id=1, replica_groups={{24,28,0,4,8,12,16,20},{25,29,1,5,9,13,17,21},{26,30,2,6,10,14,18,22},{..., dimensions={0} | all-to-all | bytes 1802240 | tf_op jit(solution)/shard_map/all_to_all | solution.py:358
  52.2 0.1 slice_convert_fusion
  52.4 0.0 copy-start.1
  52.4 0.2 shard_map.94
  52.6 8.7 %all_to_all.26 = f16[4,224,128]{2,1,0:T(8,128)(2,1)S(1)} all-to-all(f16[4,224,128]{2,1,0:T(8,128)(2,1)S(1)} %broadcast_in_dim.5), channel_id=1, replica_groups={{3,0,1,2},{7,4,5,6},{11,8,9,10},{15,12,13,14},{19,16,17,18},{23,20,21,2..., dimensions={0} | all-to-all | bytes 458752 | tf_op jit(solution)/shard_map/all_to_all | solution.py:358
  61.4 0.0 copy-done.1
  61.4 3.5 %shard_map.95 = bf16[16,40,128]{2,1,0:T(8,128)(2,1)S(1)} custom-call(s32[24]{0:T(128)S(1)} %copy-done.1, f32[4,224,128]{2,1,0:T(8,128)S(1)} %convert_element_type.26.got, f32[8,224,128]{2,1,0:T(8,128)S(1)} %get-tuple-element.13.coefs), custom_call_target="tpu_custom_call" | custom-call | tf_op jit(solution)/shard_map/pallas_call | solution.py:422
  64.9 17.7 %all_to_all.27.got = bf16[16,40,128]{2,1,0:T(8,128)(2,1)S(1)} all-to-all(bf16[16,40,128]{2,1,0:T(8,128)(2,1)S(1)} %shard_map.95), channel_id=1, replica_groups={{352,64,288,0,224,448,160,384,96,320,32,256,480,192,416,128},{353,65,28..., dimensions={0} | all-to-all | bytes 327680 | tf_op jit(solution)/shard_map/all_to_all | solution.py:358
  82.6 0.1 shard_map.96
  82.8 13.6 %all_to_all.28 = f16[32,16,128]{2,1,0:T(8,128)(2,1)S(1)} all-to-all(f16[32,16,128]{2,1,0:T(8,128)(2,1)S(1)} %convert_element_type.28), channel_id=1, replica_groups={{27,31,3,7,11,15,19,23,24,28,0,4,8,12,16,20,25,29,1,5,9,13,17,21,26,30,..., dimensions={0} | all-to-all | bytes 262144 | tf_op jit(solution)/shard_map/all_to_all | solution.py:358
  96.4 1.0 %shard_map.97 = f32[40,8,128]{2,1,0:T(8,128)} custom-call(f32[32,16,128]{2,1,0:T(8,128)S(1)} %convert_element_type.29.got), custom_call_target="tpu_custom_call" | custom-call | tf_op jit(solution)/shard_map/pallas_call | solution.py:449
  (6 shorter events, 0.1 us)
Async XLA Ops:
  2.1 28.0 %all-to-all-start = ((bf16[16,24,256]{2,1,0:T(8,128)(2,1)}), bf16[16,24,256]{2,1,0:T(8,128)(2,1)S(1)}, u32[]{:S(2)}, u32[]{:S(2)}) async-start(bf16[16,24,256]{2,1,0:T(8,128)(2,1)} %shard_map.92), calls=%async_computation | async-start | bytes 393216 | tf_op jit(solution)/shard_map/all_to_all | solution.py:358
  19.9 0.7 copy-start
  52.4 9.0 %copy-start.1 = (s32[24]{0:T(128)S(1)}, s32[24]{0:T(128)}, u32[]{:S(2)}) copy-start(s32[24]{0:T(128)} %lens.1) | copy-start | bytes 292

commit v13 on v12

--- a/solution.py
+++ b/solution.py
@@ -64,8 +64,8 @@
 TROWS = 3 * TJ
 ROOT, STEP, BACK = 11, 7, 7
 FROM_ROOT = [[(STEP * k + ROOT) % NO for k in range(NO)]]
-FROM_AUX = [[(k + 6) % NA for k in range(NA)]]
-FROM_PAIR = [[(k + 3) % NP for k in range(NP)]]
+FROM_AUX = [[(k + 4) % NA for k in range(NA)]]
+FROM_PAIR = [[(k + 2) % NP for k in range(NP)]]
 FROM_BOTH = [[NA * y + p for y in FROM_PAIR[0] for p in FROM_AUX[0]]]
 ROWS = 24
 CROWS = 216
@@ -77,11 +77,11 @@
 
 
 def aux_slot(aux):
-    return (aux + NA - 6) % NA
+    return (aux + NA - 4) % NA
 
 
 def pair_slot(pair):
-    return (pair + NP - 3) % NP
+    return (pair + NP - 2) % NP
 
 
 def both_slot(pair, aux):

time: 97.7 us -> 96 us (0.983)
  blocking collectives: 58.1 us -> 56.4 us
    all_to_all x4, blocking collectives: 58.1 us -> 56.4 us  [exchange(): lax.all_to_all(x, axes, split_axis=0, concat_axis=0, tiled=True, axis_ind...]
where the time goes in v13:
time: 96 us; the launch traced here: 95.6 us
  blocking collectives  56.4 us (59%)
  starting transfers between devices  16.4 us (17%)
  Pallas kernels  12.4 us (13%)
  waiting for transfers between devices  7.8 us (8%)
  local copies, waits for them, and re-layouts  1.46 us (2%)
    all_to_all x4, blocking collectives, exchange(): lax.all_to_all(x, axes, split_axis=0, concat_axis=0, tiled=True, axis_ind...  56.4 us
    all_to_all x1, starting transfers between devices, exchange(): lax.all_to_all(x, axes, split_axis=0, concat_axis=0, tiled=True, axis_ind...  16.4 us
    all_to_all x1, waiting for transfers between devices, exchange(): lax.all_to_all(x, axes, split_axis=0, concat_axis=0, tiled=True, axis_ind...  7.8 us
    pallas_call x1, Pallas kernels, on_device(): pl.pallas_call(partial_t, out_shape=[shape_of((NA, SROWS, LANES), F32), s...  3.83 us
    pallas_call x1, Pallas kernels, on_device(): pl.pallas_call(all_blocks, out_shape=shape_of((NO, 40, LANES), BF16), in_...  3.51 us
    pallas_call x1, Pallas kernels, on_device(): pl.pallas_call(pack_amps, out_shape=shape_of((NO, ROWS, 256), BF16), in_s...  2.09 us
  transfers between devices with their start and end apart: 1, of which 1 were waited for; matrix products, arithmetic and copies ran while one was open for 1% of the time, Pallas kernels for 2%

profile of v13, /device:TPU:1, one launch (start us, length us, event | category | flops | bytes accessed | tf_op | source)
XLA Modules:
  0.0 95.6 jit_solution(3711137652459210589)
XLA Ops:
  0.0 2.1 %shard_map.92 = bf16[16,24,256]{2,1,0:T(8,128)(2,1)} custom-call(bf16[18,32,288]{2,1,0:T(8,128)(2,1)} %bitcast.10, bf16[12,18,288]{2,1,0:T(8,128)(2,1)} %bitcast.11, bf16[18,3072]{1,0:T(8,128)(2,1)} %coef_hbm.1), custom_call_target="tpu_custom_call" | custom-call | tf_op jit(solution)/shard_map/pallas_call | solution.py:368
  2.1 16.4 %all-to-all-start = ((bf16[16,24,256]{2,1,0:T(8,128)(2,1)}), bf16[16,24,256]{2,1,0:T(8,128)(2,1)S(1)}, u32[]{:S(2)}, u32[]{:S(2)}) async-start(bf16[16,24,256]{2,1,0:T(8,128)(2,1)} %shard_map.92), calls=%async_computation | async-start | bytes 393216 | tf_op jit(solution)/shard_map/all_to_all | solution.py:358
  19.2 0.7 tile.4
  19.8 0.1 tile.10
  19.9 0.0 copy-start
  20.0 0.7 copy-done
  20.6 1.7 %shard_map.91 = (bf16[216,3072]{1,0:T(8,128)(2,1)S(1)}, f32[8,128]{1,0:T(8,128)S(1)}) custom-call(s32[1]{0:T(128)S(6)} %copy.10.counts, s32[2,40]{1,0:T(2,128)S(1)} %bitcast.8, bf16[12,18,3072]{2,1,0:T(8,128)(2,1)} %cabs_hbm.1), custom_call_target="tpu_custom_call" | custom-call | bytes 5000000 | tf_op jit(solution)/shard_map/pallas_call | solution.py:387
  22.3 7.8 %all-to-all-done.got = bf16[16,24,256]{2,1,0:T(8,128)(2,1)S(1)} async-done(((bf16[16,24,256]{2,1,0:T(8,128)(2,1)}), bf16[16,24,256]{2,1,0:T(8,128)(2,1)S(1)}, u32[]{:S(2)}, u32[]{:S(2)}) %all-to-all-start) | async-done | bytes 196640 | tf_op jit(solution)/shard_map/all_to_all | solution.py:358
  30.1 3.8 %shard_map.93 = (f32[8,440,128]{2,1,0:T(8,128)S(1)}, f32[440,128]{1,0:T(8,128)S(1)}) custom-call(bf16[16,24,256]{2,1,0:T(8,128)(2,1)S(1)} %all-to-all-done.got, f32[1,256]{1,0:T(1,128)S(1)} %bitcast.7, bf16[216,3072]{1,0:T(8,128)(2,1)S(1)} %get-tuple-element.10.cabs, bf16[576,3072]{1,0:T(8,128)(2,1)} %bitcast.9), custom_call_target="tpu_custom_call" | custom-call | tf_op jit(solution)/shard_map/pallas_call | solution.py:396
  33.9 0.2 multiply_convert_fusion
  34.1 17.2 %all_to_all.25 = f16[8,440,128]{2,1,0:T(8,128)(2,1)S(1)} all-to-all(f16[8,440,128]{2,1,0:T(8,128)(2,1)S(1)} %multiply_convert_fusion), channel_id=1, replica_groups={{16,20,24,28,0,4,8,12},{17,21,25,29,1,5,9,13},{18,22,26,30,2,6,10,14},{..., dimensions={0} | all-to-all | bytes 1802240 | tf_op jit(solution)/shard_map/all_to_all | solution.py:358
  51.4 0.1 slice_convert_fusion
  51.5 0.0 copy-start.1
  51.5 0.2 shard_map.94
  51.8 8.2 %all_to_all.26 = f16[4,224,128]{2,1,0:T(8,128)(2,1)S(1)} all-to-all(f16[4,224,128]{2,1,0:T(8,128)(2,1)S(1)} %broadcast_in_dim.5), channel_id=1, replica_groups={{2,3,0,1},{6,7,4,5},{10,11,8,9},{14,15,12,13},{18,19,16,17},{22,23,20,2..., dimensions={0} | all-to-all | bytes 458752 | tf_op jit(solution)/shard_map/all_to_all | solution.py:358
  60.0 0.0 copy-done.1
  60.0 3.5 %shard_map.95 = bf16[16,40,128]{2,1,0:T(8,128)(2,1)S(1)} custom-call(s32[24]{0:T(128)S(1)} %copy-done.1, f32[4,224,128]{2,1,0:T(8,128)S(1)} %convert_element_type.26.got, f32[8,224,128]{2,1,0:T(8,128)S(1)} %get-tuple-element.13.coefs), custom_call_target="tpu_custom_call" | custom-call | tf_op jit(solution)/shard_map/pallas_call | solution.py:422
  63.5 18.4 %all_to_all.27.got = bf16[16,40,128]{2,1,0:T(8,128)(2,1)S(1)} all-to-all(bf16[16,40,128]{2,1,0:T(8,128)(2,1)S(1)} %shard_map.95), channel_id=1, replica_groups={{352,64,288,0,224,448,160,384,96,320,32,256,480,192,416,128},{353,65,28..., dimensions={0} | all-to-all | bytes 327680 | tf_op jit(solution)/shard_map/all_to_all | solution.py:358
  81.9 0.1 shard_map.96
  82.1 12.6 %all_to_all.28 = f16[32,16,128]{2,1,0:T(8,128)(2,1)S(1)} all-to-all(f16[32,16,128]{2,1,0:T(8,128)(2,1)S(1)} %convert_element_type.28), channel_id=1, replica_groups={{18,22,26,30,2,6,10,14,19,23,27,31,3,7,11,15,16,20,24,28,0,4,8,12,17,21..., dimensions={0} | all-to-all | bytes 262144 | tf_op jit(solution)/shard_map/all_to_all | solution.py:358
  94.7 1.0 %shard_map.97 = f32[40,8,128]{2,1,0:T(8,128)} custom-call(f32[32,16,128]{2,1,0:T(8,128)S(1)} %convert_element_type.29.got), custom_call_target="tpu_custom_call" | custom-call | tf_op jit(solution)/shard_map/pallas_call | solution.py:449
  (6 shorter events, 0.1 us)
Async XLA Ops:
  2.1 28.0 %all-to-all-start = ((bf16[16,24,256]{2,1,0:T(8,128)(2,1)}), bf16[16,24,256]{2,1,0:T(8,128)(2,1)S(1)}, u32[]{:S(2)}, u32[]{:S(2)}) async-start(bf16[16,24,256]{2,1,0:T(8,128)(2,1)} %shard_map.92), calls=%async_computation | async-start | bytes 393216 | tf_op jit(solution)/shard_map/all_to_all | solution.py:358
  19.9 0.7 copy-start
  51.5 8.5 %copy-start.1 = (s32[24]{0:T(128)S(1)}, s32[24]{0:T(128)}, u32[]{:S(2)}) copy-start(s32[24]{0:T(128)} %lens.1) | copy-start | bytes 292

commit v14 on v13

--- a/solution.py
+++ b/solution.py
@@ -64,7 +64,7 @@
 TROWS = 3 * TJ
 ROOT, STEP, BACK = 11, 7, 7
 FROM_ROOT = [[(STEP * k + ROOT) % NO for k in range(NO)]]
-FROM_AUX = [[(k + 4) % NA for k in range(NA)]]
+FROM_AUX = [[(k + 5) % NA for k in range(NA)]]
 FROM_PAIR = [[(k + 2) % NP for k in range(NP)]]
 FROM_BOTH = [[NA * y + p for y in FROM_PAIR[0] for p in FROM_AUX[0]]]
 ROWS = 24
@@ -77,7 +77,7 @@
 
 
 def aux_slot(aux):
-    return (aux + NA - 4) % NA
+    return (aux + NA - 5) % NA
 
 
 def pair_slot(pair):

time: 96 us -> 95.4 us (level)
  no operation moved by 1% of the time
where the time goes in v14:
time: 95.4 us; the launch traced here: 95 us
  blocking collectives  55.7 us (58%)
  starting transfers between devices  16.4 us (17%)
  Pallas kernels  12.4 us (13%)
  waiting for transfers between devices  7.8 us (8%)
  local copies, waits for them, and re-layouts  1.46 us (2%)
    all_to_all x4, blocking collectives, exchange(): lax.all_to_all(x, axes, split_axis=0, concat_axis=0, tiled=True, axis_ind...  55.7 us
    all_to_all x1, starting transfers between devices, exchange(): lax.all_to_all(x, axes, split_axis=0, concat_axis=0, tiled=True, axis_ind...  16.4 us
    all_to_all x1, waiting for transfers between devices, exchange(): lax.all_to_all(x, axes, split_axis=0, concat_axis=0, tiled=True, axis_ind...  7.8 us
    pallas_call x1, Pallas kernels, on_device(): pl.pallas_call(partial_t, out_shape=[shape_of((NA, SROWS, LANES), F32), s...  3.83 us
    pallas_call x1, Pallas kernels, on_device(): pl.pallas_call(all_blocks, out_shape=shape_of((NO, 40, LANES), BF16), in_...  3.52 us
    pallas_call x1, Pallas kernels, on_device(): pl.pallas_call(pack_amps, out_shape=shape_of((NO, ROWS, 256), BF16), in_s...  2.09 us
  transfers between devices with their start and end apart: 1, of which 1 were waited for; matrix products, arithmetic and copies ran while one was open for 1% of the time, Pallas kernels for 2%

profile of v14, /device:TPU:1, one launch (start us, length us, event | category | flops | bytes accessed | tf_op | source)
XLA Modules:
  0.0 95.0 jit_solution(14523541097847223032)
XLA Ops:
  0.0 2.1 %shard_map.92 = bf16[16,24,256]{2,1,0:T(8,128)(2,1)} custom-call(bf16[18,32,288]{2,1,0:T(8,128)(2,1)} %bitcast.10, bf16[12,18,288]{2,1,0:T(8,128)(2,1)} %bitcast.11, bf16[18,3072]{1,0:T(8,128)(2,1)} %coef_hbm.1), custom_call_target="tpu_custom_call" | custom-call | tf_op jit(solution)/shard_map/pallas_call | solution.py:368
  2.1 16.4 %all-to-all-start = ((bf16[16,24,256]{2,1,0:T(8,128)(2,1)}), bf16[16,24,256]{2,1,0:T(8,128)(2,1)S(1)}, u32[]{:S(2)}, u32[]{:S(2)}) async-start(bf16[16,24,256]{2,1,0:T(8,128)(2,1)} %shard_map.92), calls=%async_computation | async-start | bytes 393216 | tf_op jit(solution)/shard_map/all_to_all | solution.py:358
  19.2 0.7 tile.4
  19.8 0.1 tile.10
  19.9 0.0 copy-start
  20.0 0.7 copy-done
  20.6 1.7 %shard_map.91 = (bf16[216,3072]{1,0:T(8,128)(2,1)S(1)}, f32[8,128]{1,0:T(8,128)S(1)}) custom-call(s32[1]{0:T(128)S(6)} %copy.10.counts, s32[2,40]{1,0:T(2,128)S(1)} %bitcast.8, bf16[12,18,3072]{2,1,0:T(8,128)(2,1)} %cabs_hbm.1), custom_call_target="tpu_custom_call" | custom-call | bytes 5000000 | tf_op jit(solution)/shard_map/pallas_call | solution.py:387
  22.3 7.8 %all-to-all-done.got = bf16[16,24,256]{2,1,0:T(8,128)(2,1)S(1)} async-done(((bf16[16,24,256]{2,1,0:T(8,128)(2,1)}), bf16[16,24,256]{2,1,0:T(8,128)(2,1)S(1)}, u32[]{:S(2)}, u32[]{:S(2)}) %all-to-all-start) | async-done | bytes 196640 | tf_op jit(solution)/shard_map/all_to_all | solution.py:358
  30.1 3.8 %shard_map.93 = (f32[8,440,128]{2,1,0:T(8,128)S(1)}, f32[440,128]{1,0:T(8,128)S(1)}) custom-call(bf16[16,24,256]{2,1,0:T(8,128)(2,1)S(1)} %all-to-all-done.got, f32[1,256]{1,0:T(1,128)S(1)} %bitcast.7, bf16[216,3072]{1,0:T(8,128)(2,1)S(1)} %get-tuple-element.10.cabs, bf16[576,3072]{1,0:T(8,128)(2,1)} %bitcast.9), custom_call_target="tpu_custom_call" | custom-call | tf_op jit(solution)/shard_map/pallas_call | solution.py:396
  33.9 0.2 multiply_convert_fusion
  34.1 16.6 %all_to_all.25 = f16[8,440,128]{2,1,0:T(8,128)(2,1)S(1)} all-to-all(f16[8,440,128]{2,1,0:T(8,128)(2,1)S(1)} %multiply_convert_fusion), channel_id=1, replica_groups={{20,24,28,0,4,8,12,16},{21,25,29,1,5,9,13,17},{22,26,30,2,6,10,14,18},{..., dimensions={0} | all-to-all | bytes 1802240 | tf_op jit(solution)/shard_map/all_to_all | solution.py:358
  50.7 0.1 slice_convert_fusion
  50.8 0.0 copy-start.1
  50.8 0.2 shard_map.94
  51.1 8.3 %all_to_all.26 = f16[4,224,128]{2,1,0:T(8,128)(2,1)S(1)} all-to-all(f16[4,224,128]{2,1,0:T(8,128)(2,1)S(1)} %broadcast_in_dim.5), channel_id=1, replica_groups={{2,3,0,1},{6,7,4,5},{10,11,8,9},{14,15,12,13},{18,19,16,17},{22,23,20,2..., dimensions={0} | all-to-all | bytes 458752 | tf_op jit(solution)/shard_map/all_to_all | solution.py:358
  59.4 0.0 copy-done.1
  59.4 3.5 %shard_map.95 = bf16[16,40,128]{2,1,0:T(8,128)(2,1)S(1)} custom-call(s32[24]{0:T(128)S(1)} %copy-done.1, f32[4,224,128]{2,1,0:T(8,128)S(1)} %convert_element_type.26.got, f32[8,224,128]{2,1,0:T(8,128)S(1)} %get-tuple-element.13.coefs), custom_call_target="tpu_custom_call" | custom-call | tf_op jit(solution)/shard_map/pallas_call | solution.py:422
  62.9 18.3 %all_to_all.27.got = bf16[16,40,128]{2,1,0:T(8,128)(2,1)S(1)} all-to-all(bf16[16,40,128]{2,1,0:T(8,128)(2,1)S(1)} %shard_map.95), channel_id=1, replica_groups={{352,64,288,0,224,448,160,384,96,320,32,256,480,192,416,128},{353,65,28..., dimensions={0} | all-to-all | bytes 327680 | tf_op jit(solution)/shard_map/all_to_all | solution.py:358
  81.2 0.1 shard_map.96
  81.4 12.6 %all_to_all.28 = f16[32,16,128]{2,1,0:T(8,128)(2,1)S(1)} all-to-all(f16[32,16,128]{2,1,0:T(8,128)(2,1)S(1)} %convert_element_type.28), channel_id=1, replica_groups={{22,26,30,2,6,10,14,18,23,27,31,3,7,11,15,19,20,24,28,0,4,8,12,16,21,25..., dimensions={0} | all-to-all | bytes 262144 | tf_op jit(solution)/shard_map/all_to_all | solution.py:358
  94.0 1.0 %shard_map.97 = f32[40,8,128]{2,1,0:T(8,128)} custom-call(f32[32,16,128]{2,1,0:T(8,128)S(1)} %convert_element_type.29.got), custom_call_target="tpu_custom_call" | custom-call | tf_op jit(solution)/shard_map/pallas_call | solution.py:449
  (6 shorter events, 0.1 us)
Async XLA Ops:
  2.1 28.0 %all-to-all-start = ((bf16[16,24,256]{2,1,0:T(8,128)(2,1)}), bf16[16,24,256]{2,1,0:T(8,128)(2,1)S(1)}, u32[]{:S(2)}, u32[]{:S(2)}) async-start(bf16[16,24,256]{2,1,0:T(8,128)(2,1)} %shard_map.92), calls=%async_computation | async-start | bytes 393216 | tf_op jit(solution)/shard_map/all_to_all | solution.py:358
  19.9 0.7 copy-start
  50.8 8.6 %copy-start.1 = (s32[24]{0:T(128)S(1)}, s32[24]{0:T(128)}, u32[]{:S(2)}) copy-start(s32[24]{0:T(128)} %lens.1) | copy-start | bytes 292
